TPU v7x, 32 devices: a whole 2x2x4 slice. The times are simulated.
32 devices in a mesh: dp: 8 (over z, x), tensor: 4 (over y, core).
Axes of the slice: x: 2, y: 2, z: 4, core: 2. Of those that a mesh axis runs over, the one named last changes fastest.
Arguments:
- tokens: bfloat16 [8192, 2048], P(('dp', 'tensor')), may hold values from -6 to 6
- cotangent: bfloat16 [8192, 2048], P(('dp', 'tensor')), may hold values from -7 to 7
- doc_lengths: int32 [8, 2], P('dp'), may hold values from 1 to 768, 1024 in all within a row
- attend_in: float32 [2048, 3072], P('dp', 'tensor'), may hold values from -0.125 to 0.125
- attend_out: float32 [2048, 2048], P('tensor', 'dp'), may hold values from -3 to 3
- feed_in: float32 [2, 2048, 8192], P(None, 'dp', 'tensor'), may hold values from -1 to 1
- feed_out: float32 [8192, 2048], P('tensor', 'dp'), may hold values from -1 to 1
- norm_gains: float32 [2, 2048], P(None, 'dp'), may hold values from 0 to 3, as said below
- moment_attend_in: float32 [2048, 3072], P('dp', 'tensor'), may hold values from -1 to 1
- square_attend_in: float32 [2048, 3072], P('dp', 'tensor'), may hold values from 0 to 1, as said below
- moment_attend_out: float32 [2048, 2048], P('tensor', 'dp'), may hold values from -1 to 1
- square_attend_out: float32 [2048, 2048], P('tensor', 'dp'), may hold values from 0 to 1, as said below
- moment_feed_in: float32 [2, 2048, 8192], P(None, 'dp', 'tensor'), may hold values from -1 to 1
- square_feed_in: float32 [2, 2048, 8192], P(None, 'dp', 'tensor'), may hold values from 0 to 1, as said below
- moment_feed_out: float32 [8192, 2048], P('tensor', 'dp'), may hold values from -1 to 1
- square_feed_out: float32 [8192, 2048], P('tensor', 'dp'), may hold values from 0 to 1, as said below
- moment_gains: float32 [2, 2048], P(None, 'dp'), may hold values from -1 to 1
- square_gains: float32 [2, 2048], P(None, 'dp'), may hold values from 0 to 1, as said below
Outputs:
- block_out: bfloat16 [8192, 2048], P(('dp', 'tensor'))
- tokens_grad: bfloat16 [8192, 2048], P(('dp', 'tensor'))
- grad_norm: float32 [], replicated
- updated_attend_in: float32 [2048, 3072], P('dp', 'tensor')
- moment_attend_in_next: float32 [2048, 3072], P('dp', 'tensor')
- square_attend_in_next: float32 [2048, 3072], P('dp', 'tensor')
- updated_attend_out: float32 [2048, 2048], P('tensor', 'dp')
- moment_attend_out_next: float32 [2048, 2048], P('tensor', 'dp')
- square_attend_out_next: float32 [2048, 2048], P('tensor', 'dp')
- updated_feed_in: float32 [2, 2048, 8192], P(None, 'dp', 'tensor')
- moment_feed_in_next: float32 [2, 2048, 8192], P(None, 'dp', 'tensor')
- square_feed_in_next: float32 [2, 2048, 8192], P(None, 'dp', 'tensor')
- updated_feed_out: float32 [8192, 2048], P('tensor', 'dp')
- moment_feed_out_next: float32 [8192, 2048], P('tensor', 'dp')
- square_feed_out_next: float32 [8192, 2048], P('tensor', 'dp')
- updated_gains: float32 [2, 2048], P(None, 'dp')
- moment_gains_next: float32 [2, 2048], P(None, 'dp')
- square_gains_next: float32 [2, 2048], P(None, 'dp')
Inputs may be any that keep to these rules, and one draw needn't show every extreme that they name: `norm_gains`: gains are positive. `square_attend_in`: second moments are positive. `square_attend_out`: second moments are positive. `square_feed_in`: second moments are positive. `square_feed_out`: second moments are positive. `square_gains`: second moments are positive.
All inputs are finite; a program needn't handle non-finite values.
Results may differ from a plain program's by a relative error of at most 0.025.
Values may be sent and summed in bfloat16 or wider, within the bound.
No kernel may reach another device: no remote copies, remote signals or barrier semaphores. Data moves between devices by JAX's collectives and lax.ppermute only.
A program may use at most 256 MiB of HBM per device.

v0:
```python
import math

import jax
import jax.numpy as jnp
from jax import lax
from jax.sharding import PartitionSpec as P

H = 32
KV = 8
HD = 64
STEP = 10


EPSILON = 1e-05
NEGATIVE = -1e30
CLIP_LIMIT = 0.25
BETA_ONE = 0.9
BETA_TWO = 0.95
ADAM_EPSILON = 1e-08
MATRIX_RATE = 0.04
OUTPUT_RATE = 0.3
MATRIX_DECAY = 0.1
GAIN_RATE = 0.6


def frequencies(head_size):
    half_index = jnp.arange(head_size // 2, dtype=jnp.float32)
    inverse = jnp.power(500000.0, -2.0 * half_index / head_size)
    wavelength = 2.0 * math.pi / inverse
    smooth = (8192.0 / wavelength - 1.0) / 3.0
    blended = (1.0 - smooth) * inverse / 32.0 + smooth * inverse
    return jnp.where(
        wavelength < 2048.0, inverse, jnp.where(wavelength > 8192.0, inverse / 32.0, blended)
    )


def documents(lengths_row, rows):
    token_ids = jnp.arange(rows, dtype=jnp.int32)
    ends = jnp.cumsum(lengths_row)
    past = (token_ids[:, None] >= ends[None, :]).astype(jnp.int32)
    segments = jnp.sum(past, axis=1)
    positions = token_ids - jnp.sum(past * lengths_row[None, :], axis=1)
    return (token_ids, segments, positions)


def rotate(block, cosine, sine):
    half = block.shape[-1] // 2
    first = block[..., :half]
    second = block[..., half:]
    return jnp.concatenate(
        [first * cosine - second * sine, second * cosine + first * sine], axis=-1
    )


def rms_scale(vector, gain):
    return vector * lax.rsqrt(jnp.mean(vector * vector, axis=-1, keepdims=True) + EPSILON) * gain


def contract(left, right, left_dim, right_dim):
    return lax.dot_general(
        left, right, (((left_dim,), (right_dim,)), ((), ())), preferred_element_type=jnp.float32
    )


def adam(weight, grad, moment, square, clip, rate, decay):
    clipped = clip * grad
    moment_new = BETA_ONE * moment + (1.0 - BETA_ONE) * clipped
    square_new = BETA_TWO * square + (1.0 - BETA_TWO) * clipped * clipped
    direction = (
        moment_new
        / (1.0 - BETA_ONE**STEP)
        / (jnp.sqrt(square_new / (1.0 - BETA_TWO**STEP)) + ADAM_EPSILON)
    )
    return (weight - rate * (direction + decay * weight), moment_new, square_new)


def shards(
    tokens,
    cotangent,
    doc_lengths,
    attend_in,
    attend_out,
    feed_in,
    feed_out,
    norm_gains,
    moment_attend_in,
    square_attend_in,
    moment_attend_out,
    square_attend_out,
    moment_feed_in,
    square_feed_in,
    moment_feed_out,
    square_feed_out,
    moment_gains,
    square_gains,
):
    full_in, full_out, full_feed_in, full_feed_out, gains_low = (
        lax.all_gather(attend_in.astype(jnp.bfloat16), "dp", axis=0, tiled=True),
        lax.all_gather(attend_out.astype(jnp.bfloat16), "dp", axis=1, tiled=True),
        lax.all_gather(feed_in.astype(jnp.bfloat16), "dp", axis=1, tiled=True),
        lax.all_gather(feed_out.astype(jnp.bfloat16), "dp", axis=1, tiled=True),
        lax.all_gather(norm_gains.astype(jnp.bfloat16), "dp", axis=1, tiled=True),
    )
    gains = gains_low.astype(jnp.float32)
    local_rows = tokens.shape[0]
    rows = local_rows * lax.axis_size("tensor")
    token_total = rows * lax.axis_size("dp")
    inverse_total = 1.0 / token_total
    group = H // KV
    kv_local = full_in.shape[1] // ((group + 2) * HD)
    heads_local = kv_local * group
    token_ids, segments, positions = documents(doc_lengths[0], rows)
    angles = positions.astype(jnp.float32)[:, None] * frequencies(HD)[None, :]
    cosine = jnp.cos(angles)
    sine = jnp.sin(angles)
    scale = HD ** (-0.5)
    block_rows = min(512, rows)
    blocks = rows // block_rows
    inputs = tokens.astype(jnp.float32)
    normed_exact, pull_one = jax.vjp(rms_scale, inputs, gains[0])
    normed_one = normed_exact.astype(jnp.bfloat16)
    gathered_one = lax.all_gather(normed_one, "tensor", axis=0, tiled=True)
    joined = jnp.dot(gathered_one, full_in, preferred_element_type=jnp.float32).reshape(
        rows, kv_local, group + 2, HD
    )
    query_exact, pull_queries = jax.vjp(
        lambda block: rotate(block, cosine[:, None, None, :], sine[:, None, None, :]),
        joined[:, :, :group],
    )
    key_exact, pull_keys = jax.vjp(
        lambda block: rotate(block, cosine[:, None, :], sine[:, None, :]), joined[:, :, group]
    )
    queries = query_exact.astype(jnp.bfloat16)
    keys = key_exact.astype(jnp.bfloat16)
    values = joined[:, :, group + 1].astype(jnp.bfloat16)

    def block_scores(index):
        start = index * block_rows
        query_block = lax.dynamic_slice_in_dim(queries, start, block_rows, 0)
        query_ids = lax.dynamic_slice_in_dim(token_ids, start, block_rows, 0)
        query_segments = lax.dynamic_slice_in_dim(segments, start, block_rows, 0)
        allowed = (query_segments[:, None] == segments[None, :]) & (
            query_ids[:, None] >= token_ids[None, :]
        )
        scores = (
            jnp.einsum("qkgd,tkd->kgqt", query_block, keys, preferred_element_type=jnp.float32)
            * scale
        )
        return (query_block, jnp.where(allowed[None, None], scores, NEGATIVE))

    def forward_block(index):
        query_block, scores = block_scores(index)
        peak = jnp.max(scores, axis=-1, keepdims=True)
        raised = jnp.exp(scores - peak)
        total = jnp.sum(raised, axis=-1, keepdims=True)
        probs = (raised / total).astype(jnp.bfloat16)
        attended_block = jnp.einsum(
            "kgqt,tkd->qkgd", probs, values, preferred_element_type=jnp.float32
        )
        return (attended_block.astype(jnp.bfloat16), peak[..., 0] + jnp.log(total[..., 0]))

    attended_blocks, log_totals = lax.map(forward_block, jnp.arange(blocks, dtype=jnp.int32))
    attended = attended_blocks.reshape(rows, heads_local * HD)
    branch_one = lax.psum_scatter(
        jnp.dot(attended, full_out, preferred_element_type=jnp.float32).astype(jnp.bfloat16),
        "tensor",
        scatter_dimension=0,
        tiled=True,
    ).astype(jnp.float32)
    hidden_state = inputs + branch_one
    normed_two_exact, pull_two = jax.vjp(rms_scale, hidden_state, gains[1])
    normed_two = normed_two_exact.astype(jnp.bfloat16)
    gathered_two = lax.all_gather(normed_two, "tensor", axis=0, tiled=True)
    gate_up = jnp.einsum(
        "sd,kdf->ksf", gathered_two, full_feed_in, preferred_element_type=jnp.float32
    )
    activated_exact, pull_gate = jax.vjp(
        lambda gate, upward: jax.nn.silu(gate) * upward, gate_up[0], gate_up[1]
    )
    activated = activated_exact.astype(jnp.bfloat16)
    branch_two = lax.psum_scatter(
        jnp.dot(activated, full_feed_out, preferred_element_type=jnp.float32).astype(jnp.bfloat16),
        "tensor",
        scatter_dimension=0,
        tiled=True,
    ).astype(jnp.float32)
    block_out = (hidden_state + branch_two).astype(jnp.bfloat16)
    back_out = cotangent.astype(jnp.float32)
    gathered_back = lax.all_gather(cotangent, "tensor", axis=0, tiled=True)
    grad_feed_out = contract(activated, gathered_back, 0, 0)
    grad_activated = contract(gathered_back, full_feed_out, 1, 1)
    grad_gate, grad_upward = pull_gate(grad_activated)
    grad_gate_up = jnp.stack([grad_gate, grad_upward]).astype(jnp.bfloat16)
    grad_feed_in = jnp.einsum(
        "sd,ksf->kdf", gathered_two, grad_gate_up, preferred_element_type=jnp.float32
    )
    grad_normed_two = lax.psum_scatter(
        jnp.einsum(
            "ksf,kdf->sd", grad_gate_up, full_feed_in, preferred_element_type=jnp.float32
        ).astype(jnp.bfloat16),
        "tensor",
        scatter_dimension=0,
        tiled=True,
    ).astype(jnp.float32)
    grad_from_two, gain_two_grad = pull_two(grad_normed_two)
    grad_hidden = back_out + grad_from_two
    grad_branch = grad_hidden.astype(jnp.bfloat16)
    gathered_grad = lax.all_gather(grad_branch, "tensor", axis=0, tiled=True)
    grad_attend_out = contract(attended, gathered_grad, 0, 0)
    grad_attended = contract(gathered_grad, full_out, 1, 1).astype(jnp.bfloat16)
    grad_attended_blocks = grad_attended.reshape(blocks, block_rows, kv_local, group, HD)

    def backward_block(carry, pieces):
        key_total, value_total = carry
        index, log_total, grad_block = pieces
        query_block, scores = block_scores(index)
        probs = jnp.exp(scores - log_total[..., None])
        probs_low = probs.astype(jnp.bfloat16)
        value_total = value_total + jnp.einsum(
            "kgqt,qkgd->tkd", probs_low, grad_block, preferred_element_type=jnp.float32
        )
        grad_probs = jnp.einsum(
            "qkgd,tkd->kgqt", grad_block, values, preferred_element_type=jnp.float32
        )
        inner = jnp.sum(probs * grad_probs, axis=-1, keepdims=True)
        grad_scores = (probs * (grad_probs - inner)).astype(jnp.bfloat16)
        grad_query = (
            jnp.einsum("kgqt,tkd->qkgd", grad_scores, keys, preferred_element_type=jnp.float32)
            * scale
        )
        key_total = (
            key_total
            + jnp.einsum(
                "kgqt,qkgd->tkd", grad_scores, query_block, preferred_element_type=jnp.float32
            )
            * scale
        )
        return ((key_total, value_total), grad_query)

    zero_heads = jnp.zeros((rows, kv_local, HD), jnp.float32)
    (grad_keys, grad_values), grad_query_blocks = lax.scan(
        backward_block,
        (zero_heads, zero_heads),
        (jnp.arange(blocks, dtype=jnp.int32), log_totals, grad_attended_blocks),
    )
    grad_queries = grad_query_blocks.reshape(rows, kv_local, group, HD)
    (query_plain,) = pull_queries(grad_queries)
    (key_plain,) = pull_keys(grad_keys)
    grad_joined = jnp.concatenate(
        [query_plain, key_plain[:, :, None], grad_values[:, :, None]], axis=2
    )
    grad_joined = grad_joined.astype(jnp.bfloat16).reshape(rows, kv_local * (group + 2) * HD)
    grad_attend_in = contract(gathered_one, grad_joined, 0, 0)
    grad_normed_one = lax.psum_scatter(
        contract(grad_joined, full_in, 1, 1).astype(jnp.bfloat16),
        "tensor",
        scatter_dimension=0,
        tiled=True,
    ).astype(jnp.float32)
    grad_from_one, gain_one_grad = pull_one(grad_normed_one)
    tokens_grad = (grad_hidden + grad_from_one).astype(jnp.bfloat16)
    attend_in_shard, attend_out_shard, feed_in_shard, feed_out_shard = (
        lax.psum_scatter(
            (grad_attend_in * inverse_total).astype(jnp.bfloat16),
            "dp",
            scatter_dimension=0,
            tiled=True,
        ).astype(jnp.float32),
        lax.psum_scatter(
            (grad_attend_out * inverse_total).astype(jnp.bfloat16),
            "dp",
            scatter_dimension=1,
            tiled=True,
        ).astype(jnp.float32),
        lax.psum_scatter(
            (grad_feed_in * inverse_total).astype(jnp.bfloat16),
            "dp",
            scatter_dimension=1,
            tiled=True,
        ).astype(jnp.float32),
        lax.psum_scatter(
            (grad_feed_out * inverse_total).astype(jnp.bfloat16),
            "dp",
            scatter_dimension=1,
            tiled=True,
        ).astype(jnp.float32),
    )
    matrix_squares = (
        jnp.sum(attend_in_shard * attend_in_shard)
        + jnp.sum(attend_out_shard * attend_out_shard)
        + jnp.sum(feed_in_shard * feed_in_shard)
        + jnp.sum(feed_out_shard * feed_out_shard)
    )
    gain_partial = jnp.stack([gain_one_grad, gain_two_grad]) * inverse_total
    total_squares, gain_grads = lax.psum((matrix_squares, gain_partial), ("dp", "tensor"))
    grad_norm = jnp.sqrt(total_squares + jnp.sum(gain_grads * gain_grads))
    clip = jnp.minimum(1.0, CLIP_LIMIT / (grad_norm + 1e-06))
    gain_width = norm_gains.shape[1]
    gain_shard = lax.dynamic_slice_in_dim(
        gain_grads, lax.axis_index("dp") * gain_width, gain_width, 1
    )
    first = adam(
        attend_in,
        attend_in_shard,
        moment_attend_in,
        square_attend_in,
        clip,
        MATRIX_RATE,
        MATRIX_DECAY,
    )
    second = adam(
        attend_out,
        attend_out_shard,
        moment_attend_out,
        square_attend_out,
        clip,
        OUTPUT_RATE,
        MATRIX_DECAY,
    )
    third = adam(
        feed_in, feed_in_shard, moment_feed_in, square_feed_in, clip, MATRIX_RATE, MATRIX_DECAY
    )
    fourth = adam(
        feed_out, feed_out_shard, moment_feed_out, square_feed_out, clip, MATRIX_RATE, MATRIX_DECAY
    )
    fifth = adam(norm_gains, gain_shard, moment_gains, square_gains, clip, GAIN_RATE, 0.0)
    return (
        block_out,
        tokens_grad,
        grad_norm,
        first[0],
        first[1],
        first[2],
        second[0],
        second[1],
        second[2],
        third[0],
        third[1],
        third[2],
        fourth[0],
        fourth[1],
        fourth[2],
        fifth[0],
        fifth[1],
        fifth[2],
    )


def solution(mesh):
    placed = (
        P(("dp", "tensor"), None),
        P(("dp", "tensor"), None),
        P("dp", None),
        P("dp", "tensor"),
        P("tensor", "dp"),
        P(None, "dp", "tensor"),
        P("tensor", "dp"),
        P(None, "dp"),
        P("dp", "tensor"),
        P("dp", "tensor"),
        P("tensor", "dp"),
        P("tensor", "dp"),
        P(None, "dp", "tensor"),
        P(None, "dp", "tensor"),
        P("tensor", "dp"),
        P("tensor", "dp"),
        P(None, "dp"),
        P(None, "dp"),
    )
    return jax.shard_map(
        shards,
        mesh=mesh,
        in_specs=placed,
        out_specs=(
            P(("dp", "tensor"), None),
            P(("dp", "tensor"), None),
            P(),
            P("dp", "tensor"),
            P("dp", "tensor"),
            P("dp", "tensor"),
            P("tensor", "dp"),
            P("tensor", "dp"),
            P("tensor", "dp"),
            P(None, "dp", "tensor"),
            P(None, "dp", "tensor"),
            P(None, "dp", "tensor"),
            P("tensor", "dp"),
            P("tensor", "dp"),
            P("tensor", "dp"),
            P(None, "dp"),
            P(None, "dp"),
            P(None, "dp"),
        ),
        check_vma=False,
    )
```

profile of v0, /device:TPU:0, one launch (start us, length us, event | category | flops | bytes accessed | tf_op | source)
XLA Modules:
  0.0 1545.8 jit_solution(13903508098464077351)
XLA Ops:
  10.0 22.2 %all_gather.27 = bf16[2,2048]{1,0:T(2,128)(2,1)S(1)} all-gather(bf16[2,256]{1,0:T(2,128)(2,1)S(1)} %convert_element_type.135), channel_id=1, replica_groups=mesh['dp'=8,'tensor'=4] {'dp'}, dimensions={1}, use_global_device_ids=true | all-gather | bytes 9216 | tf_op jit(solution)/shard_map/all_gather | solution.py:102
  39.3 34.8 %all-gather.11.cloned.1.call-done = bf16[2048,768]{1,0:T(8,128)(2,1)} async-done(((bf16[256,768]{1,0:T(8,128)(2,1)}), bf16[2048,768]{1,0:T(8,128)(2,1)}) %all-gather.11.cloned.1.call-update) | async-done | bytes 3145744 | tf_op jit(solution)/shard_map/all_gather | solution.py:98
  74.1 35.3 %all-gather.9.cloned.1.call-done = bf16[1024,2048]{1,0:T(8,128)(2,1)} async-done(((bf16[256,2048]{1,0:T(8,128)(2,1)}), bf16[1024,2048]{1,0:T(8,128)(2,1)}) %all-gather.9.cloned.1.call-update) | async-done | bytes 4194320 | tf_op jit(solution)/shard_map/all_gather | solution.py:122
  117.2 31.7 %while.29 = (s32[]{:T(128)}, bf16[2,512,2,4,64]{1,4,3,2,0:T(8,128)(2,1)S(1)}, f32[2,2,4,512]{3,2,1,0:T(4,128)}, s32[2]{0:T(128)S(1)}, s32[1024]{0:T(1024)S(1)}, ...) while((s32[]{:T(128)}, ...), condition=%wide.region_7.8_spmd.clone, body=%wide.region_4.7_spmd.clone.sunk | while | flops 1125904384 | bytes 54153924 | solution.py:162
  169.5 42.5 %reduce-scatter.9.cloned.1.call-done = bf16[256,2048]{1,0:T(8,128)(2,1)} async-done(((bf16[1024,2048]{1,0:T(8,128)(2,1)}), bf16[256,2048]{1,0:T(8,128)(2,1)}) %reduce-scatter.9.cloned.1.call-update) | async-done | bytes 1048592 | tf_op jit(solution)/shard_map/reduce_scatter | solution.py:164
  223.8 27.1 %all-gather.15.cloned.1.call-done = bf16[1024,2048]{1,0:T(8,128)(2,1)} async-done(((bf16[256,2048]{1,0:T(8,128)(2,1)}), bf16[1024,2048]{1,0:T(8,128)(2,1)}) %all-gather.15.cloned.1.call-update) | async-done | bytes 4194320 | tf_op jit(solution)/shard_map/all_gather | solution.py:173
  250.9 230.5 %all-gather.17.cloned.1.call-done = bf16[2,2048,2048]{2,1,0:T(8,128)(2,1)} async-done(((bf16[2,256,2048]{2,1,0:T(8,128)(2,1)}), bf16[2,2048,2048]{2,1,0:T(8,128)(2,1)}) %all-gather.17.cloned.1.call-update) | async-done | bytes 16777232 | tf_op jit(solution)/shard_map/all_gather | solution.py:100
  481.4 23.5 %convolution_bitcast_fusion.1 = f32[2,1024,2048]{2,1,0:T(8,128)} fusion(bf16[2,2048,2048]{2,1,0:T(8,128)(2,1)} %all-gather.17.cloned.1.call-done, bf16[1024,2048]{1,0:T(8,128)(2,1)} %all-gather.15.cloned.1.call-done), kind=kOutput, calls=%fused_computation.71 | convolution fusion | flops 17179869184 | bytes 37748736 | tf_op jit(solution)/shard_map/sd,kdf->ksf/dot_general | solution.py:174
  515.7 128.3 %all-gather.19.cloned.1.call-done = bf16[2048,2048]{1,0:T(8,128)(2,1)} async-done(((bf16[2048,256]{1,0:T(8,128)(2,1)}), bf16[2048,2048]{1,0:T(8,128)(2,1)}) %all-gather.19.cloned.1.call-update) | async-done | bytes 8388624 | tf_op jit(solution)/shard_map/all_gather | solution.py:101
  644.0 21.8 %fusion.61 = (bf16[1,1024,2048]{2,1,0:T(8,128)(2,1)}, bf16[1,1024,2048]{2,1,0:T(8,128)(2,1)}, bf16[1024,2048]{1,0:T(8,128)(2,1)}) fusion(f32[2,1024,2048]{2,1,0:T(8,128)} %convolution_bitcast_fusion.1, bf16[1024,2048]{1,0:T(8,128)(2,1)} %all-gather.21.cloned.1.call-done, bf16[2048,2048]{1,0:T(8,128)(2,1)} %all-gather.19.cloned.1.call-done), kind=kOutput, calls=%fused_computation.91 | convolution fusion | flops 8623489024 | bytes 41943040 | tf_op jit(solution)/shard_map/dot_general | solution.py:60
  665.7 23.8 %bitcast_convert_fusion = bf16[1024,2048]{1,0:T(8,128)(2,1)} fusion(bf16[2,2048,2048]{2,1,0:T(8,128)(2,1)} %all-gather.17.cloned.1.call-done, bf16[1,1024,2048]{2,1,0:T(8,128)(2,1)} %get-tuple-element.390, bf16[1,1024,2048]{2,1,0:T(8,128)(2,1)} %get-tuple-element.389), kind=kOutput, calls=%fused_computation.66 | convolution fusion | flops 17186160640 | bytes 29360128 | tf_op jit(solution)/shard_map/ksf,kdf->sd/dot_general | solution.py:198
  689.8 42.6 %reduce-scatter.13.cloned.1.call-done = bf16[256,2048]{1,0:T(8,128)(2,1)} async-done(((bf16[1024,2048]{1,0:T(8,128)(2,1)}), bf16[256,2048]{1,0:T(8,128)(2,1)}) %reduce-scatter.13.cloned.1.call-update) | async-done | bytes 1048592 | tf_op jit(solution)/shard_map/reduce_scatter | solution.py:197
  738.8 14.0 multiply_convert_fusion.1
  752.9 20.5 %all-gather.23.cloned.1.call-done = bf16[1024,2048]{1,0:T(8,128)(2,1)} async-done(((bf16[256,2048]{1,0:T(8,128)(2,1)}), bf16[1024,2048]{1,0:T(8,128)(2,1)}) %all-gather.23.cloned.1.call-update) | async-done | bytes 4194320 | tf_op jit(solution)/shard_map/all_gather | solution.py:208
  791.5 142.5 %while.30 = (s32[]{:T(128)}, f32[1024,2,64]{0,2,1:T(8,128)}, f32[1024,2,64]{0,2,1:T(8,128)}, f32[2,512,2,4,64]{1,0,4,3,2:T(2,128)}, s32[2]{0:T(128)S(1)}, /*inde...) while((s32[]{:T(128)}, f32[1024,2,64]{0,2,1:T(8,128)}, ...), condition=%wide.region_15.16_spmd.clone.clone, body=%wide.region_13.15_spmd.clone.clone.sunk | while | flops 2749755392 | bytes 218043344 | solution.py:241
  828.6 19.6 %dynamic_update_slice.23 = f32[2,512,2,4,64]{1,0,4,3,2:T(2,128)} dynamic-update-slice(f32[2,512,2,4,64]{1,0,4,3,2:T(2,128)} %get-tuple-element.602, f32[1,512,2,4,64]{1,0,4,3,2:T(1,128)S(1)} %copy.104, s32[]{:T(128)} %get-tuple-element.599, s32[]{:T(128)} %constant.66.clone.1..sunk.1, s32[]{:T(128)} %constant.66.clone.1..sunk.1, s32[]{:T(128)} %constant.66.clone.1..sunk.1, s32[]{:T(128)} %constant.66.clone.1..sunk.1) | dynamic-update-slice | bytes 2097156 | tf_op jit(solution)/shard_map/while/body/jit(dynamic_update_index_in_dim)/dynamic_update_slice | solution.py:241
  899.8 19.6 %dynamic_update_slice.23 = f32[2,512,2,4,64]{1,0,4,3,2:T(2,128)} dynamic-update-slice(f32[2,512,2,4,64]{1,0,4,3,2:T(2,128)} %get-tuple-element.602, f32[1,512,2,4,64]{1,0,4,3,2:T(1,128)S(1)} %copy.104, s32[]{:T(128)} %get-tuple-element.599, s32[]{:T(128)} %constant.66.clone.1..sunk.1, s32[]{:T(128)} %constant.66.clone.1..sunk.1, s32[]{:T(128)} %constant.66.clone.1..sunk.1, s32[]{:T(128)} %constant.66.clone.1..sunk.1) | dynamic-update-slice | bytes 2097156 | tf_op jit(solution)/shard_map/while/body/jit(dynamic_update_index_in_dim)/dynamic_update_slice | solution.py:241
  951.8 24.7 %fusion.48 = bf16[2,2048,2048]{1,2,0:T(8,128)(2,1)} fusion(bf16[1,1024,2048]{2,1,0:T(8,128)(2,1)} %get-tuple-element.390, bf16[1,1024,2048]{2,1,0:T(8,128)(2,1)} %get-tuple-element.389, bf16[1024,2048]{1,0:T(8,128)(2,1)} %all-gather.15.cloned.1.call-done), kind=kOutput, calls=%fused_computation.57 | convolution fusion | flops 17200840704 | bytes 29360128 | tf_op jit(solution)/shard_map/sd,ksf->kdf/dot_general | solution.py:194
  976.6 14.0 convolution_convert_fusion
  1011.1 64.3 %reduce-scatter.17.cloned.1.call-done = bf16[256,768]{1,0:T(8,128)(2,1)} async-done(((bf16[2048,768]{1,0:T(8,128)(2,1)}), bf16[256,768]{1,0:T(8,128)(2,1)}) %reduce-scatter.17.cloned.1.call-update) | async-done | bytes 393232 | tf_op jit(solution)/shard_map/reduce_scatter | solution.py:263
  1078.5 43.1 %reduce-scatter.15.cloned.1.call-done = bf16[256,2048]{1,0:T(8,128)(2,1)} async-done(((bf16[1024,2048]{1,0:T(8,128)(2,1)}), bf16[256,2048]{1,0:T(8,128)(2,1)}) %reduce-scatter.15.cloned.1.call-update) | async-done | bytes 1048592 | tf_op jit(solution)/shard_map/reduce_scatter | solution.py:254
  1124.0 284.0 %reduce-scatter.21.cloned.1.call-done = bf16[2,256,2048]{1,2,0:T(8,128)(2,1)} async-done(((bf16[2,2048,2048]{1,2,0:T(8,128)(2,1)}), bf16[2,256,2048]{1,2,0:T(8,128)(2,1)}) %reduce-scatter.21.cloned.1.call-update) | async-done | bytes 2097168 | tf_op jit(solution)/shard_map/reduce_scatter | solution.py:275
  1412.5 42.1 %reduce-scatter.11.cloned.1.call-done = bf16[256,2048]{1,0:T(8,128)(2,1)} async-done(((bf16[1024,2048]{1,0:T(8,128)(2,1)}), bf16[256,2048]{1,0:T(8,128)(2,1)}) %reduce-scatter.11.cloned.1.call-update) | async-done | bytes 1048592 | tf_op jit(solution)/shard_map/reduce_scatter | solution.py:181
  1459.5 39.9 %all-reduce.4 = (f32[]{:T(128)}, f32[2,2048]{1,0:T(2,128)S(1)}) all-reduce(f32[]{:T(128)S(6)} %add.222, f32[2,2048]{1,0:T(2,128)S(1)} %maximum_multiply_fusion), channel_id=1, replica_groups=mesh['dp'=8,'tensor'=4] {'dp','tensor'}, use_global_device_ids=true, to_apply=%region_26.27 | all-reduce | flops 4097 | bytes 32776 | tf_op jit(solution)/shard_map/psum | solution.py:295
  (263 shorter events, 304.1 us)
Async XLA Ops:
  7.2 66.9 %all-gather.11.cloned.1.call-start = ((), (), s32[]{:S(2)}) async-start(), calls=%async_computation.9 | async-start | bytes 3538944 | tf_op jit(solution)/shard_map/all_gather | solution.py:98
  9.2 100.1 %all-gather.9.cloned.1.call-start = ((), (), s32[]{:S(2)}) async-start(), calls=%async_computation.8 | async-start | bytes 5242880 | tf_op jit(solution)/shard_map/all_gather | solution.py:122
  37.5 125.6 %all-gather.13.cloned.1.call-start = ((), (), s32[]{:S(2)}) async-start(), calls=%async_computation.10 | async-start | bytes 2359296 | tf_op jit(solution)/shard_map/all_gather | solution.py:99
  38.3 173.6 %reduce-scatter.9.cloned.1.call-start = ((), (), s32[]{:S(2)}) async-start(), calls=%async_computation.11 | async-start | bytes 5242880 | tf_op jit(solution)/shard_map/reduce_scatter | solution.py:164
  169.1 81.8 %all-gather.15.cloned.1.call-start = ((), (), s32[]{:S(2)}) async-start(), calls=%async_computation.12 | async-start | bytes 5242880 | tf_op jit(solution)/shard_map/all_gather | solution.py:173
  213.6 521.6 %copy-start.37 = (f32[256]{0:T(256)}, f32[256]{0:T(256)S(1)}, u32[]{:S(2)}) copy-start(f32[256]{0:T(256)S(1)} %fusion.91) | copy-start | bytes 3076
  216.3 265.1 %all-gather.17.cloned.1.call-start = ((), (), s32[]{:S(2)}) async-start(), calls=%async_computation.13 | async-start | bytes 18874368 | tf_op jit(solution)/shard_map/all_gather | solution.py:100
  220.2 295.5 %all-gather.21.cloned.1.call-start = ((), (), s32[]{:S(2)}) async-start(), calls=%async_computation.16 | async-start | bytes 5242880 | tf_op jit(solution)/shard_map/all_gather | solution.py:189
  220.9 423.0 %all-gather.19.cloned.1.call-start = ((), (), s32[]{:S(2)}) async-start(), calls=%async_computation.14 | async-start | bytes 9437184 | tf_op jit(solution)/shard_map/all_gather | solution.py:101
  223.8 508.7 %reduce-scatter.13.cloned.1.call-start = ((), (), s32[]{:S(2)}) async-start(), calls=%async_computation.17 | async-start | bytes 5242880 | tf_op jit(solution)/shard_map/reduce_scatter | solution.py:197
  689.6 83.8 %all-gather.23.cloned.1.call-start = ((), (), s32[]{:S(2)}) async-start(), calls=%async_computation.18 | async-start | bytes 5242880 | tf_op jit(solution)/shard_map/all_gather | solution.py:208
  738.7 268.2 %reduce-scatter.23.cloned.1.call-start = ((), (), s32[]{:S(2)}) async-start(), calls=%async_computation.23 | async-start | bytes 9437184 | tf_op jit(solution)/shard_map/reduce_scatter | solution.py:281
  752.8 256.6 %reduce-scatter.19.cloned.1.call-start = ((), (), s32[]{:S(2)}) async-start(), calls=%async_computation.21 | async-start | bytes 2359296 | tf_op jit(solution)/shard_map/reduce_scatter | solution.py:269
  791.5 284.0 %reduce-scatter.17.cloned.1.call-start = ((), (), s32[]{:S(2)}) async-start(), calls=%async_computation.20 | async-start | bytes 3538944 | tf_op jit(solution)/shard_map/reduce_scatter | solution.py:263
  944.7 176.9 %reduce-scatter.15.cloned.1.call-start = ((), (), s32[]{:S(2)}) async-start(), calls=%async_computation.19 | async-start | bytes 5242880 | tf_op jit(solution)/shard_map/reduce_scatter | solution.py:254
  951.8 456.2 %reduce-scatter.21.cloned.1.call-start = ((), (), s32[]{:S(2)}) async-start(), calls=%async_computation.22 | async-start | bytes 18874368 | tf_op jit(solution)/shard_map/reduce_scatter | solution.py:275
  976.5 478.1 %reduce-scatter.11.cloned.1.call-start = ((), (), s32[]{:S(2)}) async-start(), calls=%async_computation.15 | async-start | bytes 5242880 | tf_op jit(solution)/shard_map/reduce_scatter | solution.py:181
  1001.4 122.5 %copy-start.42 = (f32[256]{0:T(256)S(1)}, f32[256]{0:T(256)}, u32[]{:S(2)}) copy-start(f32[256]{0:T(256)} %copy-done.41) | copy-start | bytes 3076
  1001.4 122.5 %copy-start.36 = (f32[2048]{0:T(1024)S(1)}, f32[2048]{0:T(1024)}, u32[]{:S(2)}) copy-start(f32[2048]{0:T(1024)} %get-tuple-element.320) | copy-start | bytes 24580
  1006.9 447.8 %copy-start.7 = (bf16[256,2048]{1,0:T(8,128)(2,1)S(1)}, bf16[256,2048]{1,0:T(8,128)(2,1)}, u32[]{:S(2)}) copy-start(bf16[256,2048]{1,0:T(8,128)(2,1)} %reduce-scatter.9.cloned.1.call-done) | copy-start | bytes 3145732
  1006.9 447.8 %copy-start.11 = (bf16[256,2048]{1,0:T(8,128)(2,1)S(1)}, bf16[256,2048]{1,0:T(8,128)(2,1)}, u32[]{:S(2)}) copy-start(bf16[256,2048]{1,0:T(8,128)(2,1)} %param.23) | copy-start | bytes 3145732
  1006.9 447.8 %copy-start.33 = (f32[1,2048]{1,0:T(1,128)S(1)}, f32[1,2048]{1,0:T(1,128)}, u32[]{:S(2)}) copy-start(f32[1,2048]{1,0:T(1,128)} %get-tuple-element.402) | copy-start | bytes 24580
  1006.9 447.8 %copy-start.38 = (f32[256]{0:T(256)S(1)}, f32[256]{0:T(256)}, u32[]{:S(2)}) copy-start(f32[256]{0:T(256)} %copy-done.37) | copy-start | bytes 3076
  1006.9 447.8 %copy-start.44 = (f32[256]{0:T(256)S(1)}, f32[256]{0:T(256)}, u32[]{:S(2)}) copy-start(f32[256]{0:T(256)} %copy-done.43) | copy-start | bytes 3076
  (50 other events, 998.7 us)
Sparse Core Ops, SparseCore 0:
  10.8 63.2 all-gather.10
  76.2 33.0 all-gather.8
  112.0 51.0 all-gather.12
  169.2 42.7 reduce-scatter.8
  216.4 34.4 all-gather.14
  253.7 227.5 all-gather.16
  483.0 32.6 all-gather.20
  518.5 125.4 all-gather.18
  689.7 42.6 reduce-scatter.12
  738.9 34.4 all-gather.22
  777.0 149.4 reduce-scatter.22
  930.8 67.2 reduce-scatter.18
  1002.2 73.1 reduce-scatter.16
  1078.0 43.6 reduce-scatter.14
  1125.3 282.6 reduce-scatter.20
  1411.1 43.4 reduce-scatter.10
where the time goes:
time: 1560 us; the launch traced here: 1550 us
  waiting for transfers between devices  1020 us (65%)
  matrix products  244 us (16%)
  other arithmetic  99 us (6%)
  local copies, waits for them, and re-layouts  96 us (6%)
  blocking collectives  62.1 us (4%)
  between operations  20.1 us (1%)
    reduce_scatter x1, waiting for transfers between devices, shards(): lax.psum_scatter((grad_feed_in * inverse_total).astype(jnp.bfloat16), 'dp...  284 us
    all_gather x1, waiting for transfers between devices, shards(): lax.all_gather(feed_in.astype(jnp.bfloat16), 'dp', axis=1, tiled=True)  230 us
    all_gather x1, waiting for transfers between devices, shards(): lax.all_gather(feed_out.astype(jnp.bfloat16), 'dp', axis=1, tiled=True)  128 us
    reduce_scatter x1, waiting for transfers between devices, shards(): lax.psum_scatter((grad_attend_in * inverse_total).astype(jnp.bfloat16), '...  64.3 us
    dot_general x6, matrix products, contract(): lax.dot_general(left, right, (((left_dim,), (right_dim,)), ((), ())), pre...  59.4 us
    reduce_scatter x1, waiting for transfers between devices, shards(): lax.psum_scatter(contract(grad_joined, full_in, 1, 1).astype(jnp.bfloat16...  43.1 us
    reduce_scatter x1, waiting for transfers between devices, shards(): lax.psum_scatter(jnp.einsum('ksf,kdf->sd', grad_gate_up, full_feed_in, pr...  42.6 us
    reduce_scatter x1, waiting for transfers between devices, shards(): lax.psum_scatter(jnp.dot(attended, full_out, preferred_element_type=jnp.f...  42.5 us
  transfers between devices with their start and end apart: 16, of which 14 were waited for; matrix products, arithmetic and copies ran while one was open for 21% of the time, Pallas kernels for 0%

commit v1 on v0

v1 whole, which is shorter than its diff:
```python
import functools
import math

import jax
import jax.numpy as jnp
from jax import lax
from jax.experimental import pallas as pl
from jax.experimental.pallas import tpu as pltpu
from jax.sharding import Mesh
from jax.sharding import PartitionSpec as P

H = 32
KV = 8
HD = 64
GROUP = H // KV
STEP = 10
LANES = 128
QUERY_ROWS = 256
CHUNKS = 2

EPSILON = 1e-05
NEGATIVE = -1e30
CLIP_LIMIT = 0.25
BETA_ONE = 0.9
BETA_TWO = 0.95
ADAM_EPSILON = 1e-08
MATRIX_RATE = 0.04
OUTPUT_RATE = 0.3
MATRIX_DECAY = 0.1
GAIN_RATE = 0.6

BF16 = jnp.bfloat16
F32 = jnp.float32


def flip(value, axes, sizes):
    count = math.prod(sizes[a] for a in axes)
    pairs = [(i, i ^ (count - 1)) for i in range(count)]
    return lax.ppermute(value, tuple(axes), pairs)


def combos(axes):
    return [
        tuple(a for i, a in enumerate(axes) if place >> (len(axes) - 1 - i) & 1)
        for place in range(2 ** len(axes))
    ]


def spread(block, links, core, sizes):
    parts = [block] + [flip(block, c, sizes) for c in combos(links)[1:]]
    mine = jnp.concatenate(parts, axis=0) if len(parts) > 1 else block
    return jnp.concatenate([mine, flip(mine, (core,), sizes)], axis=0)


def collect(partial, links, core, sizes):
    half = partial.shape[0] // 2
    near = flip(partial[half:], (core,), sizes)
    mine = (partial[:half].astype(F32) + near.astype(F32)).astype(BF16)
    places = combos(links)
    rows = half // len(places)
    total = mine[:rows].astype(F32)
    for place, c in enumerate(places):
        if place:
            total = total + flip(mine[place * rows : (place + 1) * rows], c, sizes).astype(F32)
    return total


def frequencies(head_size):
    half_index = jnp.arange(head_size // 2, dtype=F32)
    inverse = jnp.power(500000.0, -2.0 * half_index / head_size)
    wavelength = 2.0 * math.pi / inverse
    smooth = (8192.0 / wavelength - 1.0) / 3.0
    blended = (1.0 - smooth) * inverse / 32.0 + smooth * inverse
    return jnp.where(
        wavelength < 2048.0, inverse, jnp.where(wavelength > 8192.0, inverse / 32.0, blended)
    )


def rotation_tables(lengths_row, rows):
    token_ids = jnp.arange(rows, dtype=jnp.int32)
    ends = jnp.cumsum(lengths_row)
    past = (token_ids[:, None] >= ends[None, :]).astype(jnp.int32)
    positions = token_ids - jnp.sum(past * lengths_row[None, :], axis=1)
    angles = positions.astype(F32)[:, None] * frequencies(HD)[None, :]
    cosine, sine = jnp.cos(angles), jnp.sin(angles)
    return (
        jnp.concatenate([cosine] * 4, axis=1),
        jnp.concatenate([-sine, sine, -sine, sine], axis=1),
    )


def exchange_halves(tile):
    lane = lax.broadcasted_iota(jnp.int32, tile.shape, 1)
    return jnp.where(
        lane % HD < HD // 2,
        pltpu.roll(tile, LANES - HD // 2, 1),
        pltpu.roll(tile, HD // 2, 1),
    )


def block_place(meta_ref, j, devices):
    relative = meta_ref[0] ^ j
    return (relative & 1) * (devices // 2) + (relative >> 1)


def allowed_bias(meta_ref, docs, first, keys, queries):
    token = lax.broadcasted_iota(jnp.int32, (1, queries), 1) + first
    start = jnp.zeros((1, queries), jnp.int32)
    for j in range(docs - 1):
        start = jnp.where(token >= meta_ref[1 + j], meta_ref[1 + j], start)
    other = lax.broadcasted_iota(jnp.int32, (keys, queries), 0)
    return jnp.where((other <= token) & (other >= start), 0.0, NEGATIVE)


def last_dims(left, right):
    return lax.dot_general(left, right, (((1,), (1,)), ((), ())), preferred_element_type=F32)


def key_halves(qkv_ref, keep_keys, keep_values, keep_turned):
    tile = qkv_ref[:, 2 * LANES : 3 * LANES].astype(F32)
    lane = lax.broadcasted_iota(jnp.int32, tile.shape, 1)
    low = jnp.where(lane < HD, tile, 0.0)
    high = jnp.where(lane < HD, 0.0, tile)
    pairs = ((low, pltpu.roll(low, HD, 1)), (pltpu.roll(high, HD, 1), high))
    for half in range(2):
        if keep_keys is not None:
            keep_keys[half] = pairs[0][half].astype(BF16)
        if keep_values is not None:
            keep_values[half] = pairs[1][half].astype(BF16)
        if keep_turned is not None:
            source, ref = keep_turned
            ref[half] = pairs[source][half].T.astype(BF16)


def forward_kernel(docs, devices, meta_ref, joined_ref, cos_ref, sin_ref, attended_ref, qkv_ref, log_ref, keys_ref, turned_ref):
    rows = joined_ref.shape[0]
    block = rows // devices
    for j in range(devices):
        source = pl.multiple_of(block_place(meta_ref, j, devices) * block, block)
        here = slice(j * block, (j + 1) * block)
        cosine, sine = cos_ref[here, :], sin_ref[here, :]
        lane = lax.broadcasted_iota(jnp.int32, cosine.shape, 1)
        for t in range(3):
            tile = joined_ref[pl.ds(source, block), t * LANES : (t + 1) * LANES]
            turned = tile * cosine + exchange_halves(tile) * sine
            if t == 2:
                turned = jnp.where(lane < HD, turned, tile)
            qkv_ref[here, t * LANES : (t + 1) * LANES] = turned.astype(BF16)
    key_halves(qkv_ref, keys_ref, None, (1, turned_ref))
    for i in range(rows // QUERY_ROWS):
        keys = (i + 1) * QUERY_ROWS
        here = slice(i * QUERY_ROWS, keys)
        bias = allowed_bias(meta_ref, docs, i * QUERY_ROWS, keys, QUERY_ROWS)
        for t in range(2):
            query = qkv_ref[here, t * LANES : (t + 1) * LANES] * BF16(HD**-0.5)
            total = jnp.zeros((LANES, QUERY_ROWS), F32)
            for half in range(2):
                scores = last_dims(keys_ref[half, :keys, :], query) + bias
                peak = jnp.max(scores, axis=0, keepdims=True)
                raised = jnp.exp(scores - peak)
                mass = jnp.sum(raised, axis=0, keepdims=True)
                probs = (raised * (1.0 / mass)).astype(BF16)
                total = total + jnp.dot(
                    turned_ref[half, :, :keys], probs, preferred_element_type=F32
                )
                head = 2 * t + half
                log_ref[0, head : head + 1, here] = peak + jnp.log(mass)
            done = total.T.astype(BF16)
            step = min(block, QUERY_ROWS)
            for part in range(QUERY_ROWS // step):
                first = i * QUERY_ROWS + part * step
                place = block_place(meta_ref, first // block, devices) * block + first % block
                attended_ref[
                    pl.ds(pl.multiple_of(place, step), step), t * LANES : (t + 1) * LANES
                ] = done[part * step : (part + 1) * step, :]


def backward_kernel(docs, devices, meta_ref, qkv_ref, log_ref, back_ref, cos_ref, sin_ref, grad_ref, keys_ref, values_ref, turned_ref, key_total, value_total, query_total, back_here):
    rows = qkv_ref.shape[0]
    block = rows // devices
    key_halves(qkv_ref, keys_ref, values_ref, (0, turned_ref))
    for j in range(devices):
        source = pl.multiple_of(block_place(meta_ref, j, devices) * block, block)
        back_here[j * block : (j + 1) * block, :] = back_ref[pl.ds(source, block), :]
    key_total[...] = jnp.zeros_like(key_total)
    value_total[...] = jnp.zeros_like(value_total)
    for i in range(rows // QUERY_ROWS):
        keys = (i + 1) * QUERY_ROWS
        here = slice(i * QUERY_ROWS, keys)
        bias = allowed_bias(meta_ref, docs, i * QUERY_ROWS, keys, QUERY_ROWS)
        lane = lax.broadcasted_iota(jnp.int32, (QUERY_ROWS, LANES), 1)
        for t in range(2):
            columns = slice(t * LANES, (t + 1) * LANES)
            query = qkv_ref[here, columns] * BF16(HD**-0.5)
            back = back_here[here, columns]
            total = jnp.zeros((LANES, QUERY_ROWS), F32)
            for half in range(2):
                head = 2 * t + half
                mine = (lane < HD) if half == 0 else (lane >= HD)
                scores = last_dims(keys_ref[half, :keys, :], query) + bias
                probs = jnp.exp(scores - log_ref[0, head : head + 1, here])
                moved = last_dims(values_ref[half, :keys, :], back)
                inner = jnp.sum(probs * moved, axis=0, keepdims=True)
                grad = (probs * (moved - inner)).astype(BF16)
                total = total + jnp.dot(
                    turned_ref[half, :, :keys], grad, preferred_element_type=F32
                )
                key_total[:keys, :] += jnp.dot(
                    grad, jnp.where(mine, query, BF16(0)), preferred_element_type=F32
                )
                value_total[:keys, :] += jnp.dot(
                    probs.astype(BF16), jnp.where(mine, back, BF16(0)), preferred_element_type=F32
                )
            query_total[here, columns] = total.T * HD**-0.5
    for j in range(devices):
        place = pl.multiple_of(block_place(meta_ref, j, devices) * block, block)
        here = slice(j * block, (j + 1) * block)
        cosine, sine = cos_ref[here, :], sin_ref[here, :]
        lane = lax.broadcasted_iota(jnp.int32, cosine.shape, 1)
        for t in range(2):
            columns = slice(t * LANES, (t + 1) * LANES)
            tile = query_total[here, columns]
            grad_ref[pl.ds(place, block), columns] = (
                tile * cosine - exchange_halves(tile) * sine
            ).astype(BF16)
        tile = key_total[here, :]
        tile = tile + pltpu.roll(tile, HD, 1)
        other = value_total[here, :]
        other = other + pltpu.roll(other, HD, 1)
        tile = jnp.where(lane < HD, tile * cosine - exchange_halves(tile) * sine, other)
        grad_ref[pl.ds(place, block), 2 * LANES : 3 * LANES] = tile.astype(BF16)


def attend_forward(meta, joined, cosine, sine, docs, devices):
    rows, width = joined.shape
    wide = (GROUP + 2) * HD
    groups = width // wide
    whole = pl.BlockSpec((rows, LANES), lambda g: (0, 0))
    return pl.pallas_call(
        functools.partial(forward_kernel, docs, devices),
        grid=(groups,),
        in_specs=[
            pl.BlockSpec(memory_space=pltpu.SMEM),
            pl.BlockSpec((rows, wide), lambda g: (0, g)),
            whole,
            whole,
        ],
        out_specs=[
            pl.BlockSpec((rows, GROUP * HD), lambda g: (0, g)),
            pl.BlockSpec((rows, wide), lambda g: (0, g)),
            pl.BlockSpec((1, 8, rows), lambda g: (g, 0, 0)),
        ],
        out_shape=[
            jax.ShapeDtypeStruct((rows, groups * GROUP * HD), BF16),
            jax.ShapeDtypeStruct((rows, width), BF16),
            jax.ShapeDtypeStruct((groups, 8, rows), F32),
        ],
        scratch_shapes=[
            pltpu.VMEM((2, rows, LANES), BF16),
            pltpu.VMEM((2, LANES, rows), BF16),
        ],
        compiler_params=pltpu.CompilerParams(vmem_limit_bytes=32 * 2**20),
        cost_estimate=pl.CostEstimate(
            flops=groups * GROUP * rows * rows * LANES * 4,
            bytes_accessed=rows * width * 8,
            transcendentals=groups * GROUP * rows * rows // 2,
        ),
        name="attend_forward",
    )(meta, joined, cosine, sine)


def attend_backward(meta, qkv, logs, back, cosine, sine, docs, devices):
    rows, width = qkv.shape
    wide = (GROUP + 2) * HD
    groups = width // wide
    whole = pl.BlockSpec((rows, LANES), lambda g: (0, 0))
    return pl.pallas_call(
        functools.partial(backward_kernel, docs, devices),
        grid=(groups,),
        in_specs=[
            pl.BlockSpec(memory_space=pltpu.SMEM),
            pl.BlockSpec((rows, wide), lambda g: (0, g)),
            pl.BlockSpec((1, 8, rows), lambda g: (g, 0, 0)),
            pl.BlockSpec((rows, GROUP * HD), lambda g: (0, g)),
            whole,
            whole,
        ],
        out_specs=pl.BlockSpec((rows, wide), lambda g: (0, g)),
        out_shape=jax.ShapeDtypeStruct((rows, width), BF16),
        scratch_shapes=[
            pltpu.VMEM((2, rows, LANES), BF16),
            pltpu.VMEM((2, rows, LANES), BF16),
            pltpu.VMEM((2, LANES, rows), BF16),
            pltpu.VMEM((rows, LANES), F32),
            pltpu.VMEM((rows, LANES), F32),
            pltpu.VMEM((rows, GROUP * HD), F32),
            pltpu.VMEM((rows, GROUP * HD), BF16),
        ],
        compiler_params=pltpu.CompilerParams(vmem_limit_bytes=32 * 2**20),
        cost_estimate=pl.CostEstimate(
            flops=groups * GROUP * rows * rows * LANES * 10,
            bytes_accessed=rows * width * 8,
            transcendentals=groups * GROUP * rows * rows // 2,
        ),
        name="attend_backward",
    )(meta, qkv, logs, back, cosine, sine)


def product(left, right, left_dim, right_dim):
    return lax.dot_general(
        left, right, (((left_dim,), (right_dim,)), ((), ())), preferred_element_type=F32
    )


def norm_rate(vector):
    return lax.rsqrt(jnp.mean(vector * vector, axis=-1, keepdims=True) + EPSILON)


def norm_back(vector, rate, gain, grad):
    scaled = gain * grad
    inner = jnp.mean(vector * scaled, axis=-1, keepdims=True)
    return (
        rate * scaled - vector * (rate * rate * rate * inner),
        jnp.sum(grad * vector * rate, axis=0),
    )


def adam(weight, grad, moment, square, clip, rate, decay):
    clipped = clip * grad
    moment_new = BETA_ONE * moment + (1.0 - BETA_ONE) * clipped
    square_new = BETA_TWO * square + (1.0 - BETA_TWO) * clipped * clipped
    direction = (
        moment_new
        / (1.0 - BETA_ONE**STEP)
        / (jnp.sqrt(square_new / (1.0 - BETA_TWO**STEP)) + ADAM_EPSILON)
    )
    return (weight - rate * (direction + decay * weight), moment_new, square_new)


def in_order(mine, other, first, axis):
    return jnp.where(
        first,
        jnp.concatenate([mine, other], axis=axis),
        jnp.concatenate([other, mine], axis=axis),
    )


def shards(
    sizes,
    tensor,
    tokens,
    cotangent,
    doc_lengths,
    attend_in,
    attend_out,
    feed_in,
    feed_out,
    norm_gains,
    moment_attend_in,
    square_attend_in,
    moment_attend_out,
    square_attend_out,
    moment_feed_in,
    square_feed_in,
    moment_feed_out,
    square_feed_out,
    moment_gains,
    square_gains,
):
    pack_links, core = tensor[:-1], tensor[-1]
    feed_links = ("x",) + tuple(pack_links)
    devices = math.prod(sizes[a] for a in tensor)
    side = lax.axis_index("x")
    is_first = side == 0
    local_rows, width = tokens.shape
    rows = local_rows * devices
    token_total = rows * 2 * sizes["z"]
    inverse_total = 1.0 / token_total
    docs = doc_lengths.shape[1]
    meta = jnp.concatenate(
        [lax.axis_index(tuple(tensor))[None].astype(jnp.int32), jnp.cumsum(doc_lengths[0])]
    )
    cosine, sine = rotation_tables(doc_lengths[0], rows)

    attend_in_z = lax.all_gather(attend_in.astype(BF16), "z", axis=0, tiled=False)
    attend_in_x = flip(attend_in_z, ("x",), sizes)
    full_in = jnp.where(
        is_first,
        jnp.stack([attend_in_z, attend_in_x], axis=1),
        jnp.stack([attend_in_x, attend_in_z], axis=1),
    ).reshape(width, attend_in.shape[1])
    gains = lax.all_gather(norm_gains.astype(BF16), ("z", "x"), axis=1, tiled=True).astype(F32)
    attend_out_z = lax.all_gather(attend_out.T.astype(BF16), "z", axis=0, tiled=False)
    attend_out_x = flip(attend_out_z, ("x",), sizes)
    full_out = jnp.where(
        is_first,
        jnp.stack([attend_out_z, attend_out_x], axis=1),
        jnp.stack([attend_out_x, attend_out_z], axis=1),
    ).reshape(width, attend_out.shape[0])

    hidden = feed_in.shape[2] // 2
    slim = hidden // CHUNKS

    def halves(array, axis):
        size = array.shape[axis] // 2
        mine = lax.dynamic_slice_in_dim(array, side * size, size, axis)
        other = lax.dynamic_slice_in_dim(array, (1 - side) * size, size, axis)
        return mine, other

    in_mine, in_other = halves(feed_in.astype(BF16), 2)
    out_mine, out_other = halves(feed_out.T.astype(BF16), 1)
    weights = []
    for c in range(CHUNKS):
        cut = slice(c * slim, (c + 1) * slim)
        mine = jnp.concatenate([in_mine[0, :, cut], in_mine[1, :, cut], out_mine[:, cut]], axis=1)
        other = jnp.concatenate(
            [in_other[0, :, cut], in_other[1, :, cut], out_other[:, cut]], axis=1
        )
        local = in_order(mine, flip(other, ("x",), sizes), is_first, 0)
        weights.append(
            (
                lax.all_gather(local[:, : 2 * slim], "z", axis=0, tiled=True),
                lax.all_gather(local[:, 2 * slim :], "z", axis=0, tiled=True),
            )
        )

    inputs_all = spread(tokens, pack_links, core, sizes).astype(F32)
    normed_one = (inputs_all * norm_rate(inputs_all) * gains[0]).astype(BF16)
    joined = product(normed_one, full_in, 1, 0)
    attended, qkv, logs = attend_forward(meta, joined, cosine, sine, docs, devices)
    branch_one = collect(product(attended, full_out, 1, 1).astype(BF16), pack_links, core, sizes)
    inputs = tokens.astype(F32)
    hidden_state = inputs + branch_one
    rate_two = norm_rate(hidden_state)
    normed_two = (hidden_state * rate_two * gains[1]).astype(BF16)
    gathered_two = spread(normed_two, feed_links, core, sizes)
    gathered_back = spread(cotangent, feed_links, core, sizes)

    feed_in_parts, feed_out_parts = [], []
    forward_total, backward_total = 0.0, 0.0
    for c in range(CHUNKS):
        weight_in, weight_out = weights[c]
        gate_up = product(gathered_two, weight_in, 1, 0)
        grad_activated = product(gathered_back, weight_out, 1, 0)
        gate, upward = gate_up[:, :slim], gate_up[:, slim:]
        chance = jax.nn.sigmoid(gate)
        silu = gate * chance
        activated = (silu * upward).astype(BF16)
        grad_gate = grad_activated * upward * (chance * (1.0 + gate * (1.0 - chance)))
        grad_upward = grad_activated * silu
        grad_gate_up = jnp.concatenate([grad_gate.astype(BF16), grad_upward.astype(BF16)], axis=1)
        feed_out_parts.append(
            lax.psum_scatter(
                (product(gathered_back, activated, 0, 0) * inverse_total).astype(BF16),
                "z",
                scatter_dimension=0,
                tiled=True,
            )
        )
        feed_in_parts.append(
            lax.psum_scatter(
                (product(gathered_two, grad_gate_up, 0, 0) * inverse_total).astype(BF16),
                "z",
                scatter_dimension=0,
                tiled=True,
            )
        )
        backward_total = backward_total + product(grad_gate_up, weight_in, 1, 1)
        forward_total = forward_total + product(activated, weight_out, 1, 1)
    grad_normed_two = collect(backward_total.astype(BF16), feed_links, core, sizes)
    branch_two = collect(forward_total.astype(BF16), feed_links, core, sizes)
    block_out = (hidden_state + branch_two).astype(BF16)

    grad_from_two, gain_two_grad = norm_back(hidden_state, rate_two, gains[1], grad_normed_two)
    grad_hidden = cotangent.astype(F32) + grad_from_two
    gathered_grad = spread(grad_hidden.astype(BF16), pack_links, core, sizes)
    grad_attended = product(gathered_grad, full_out, 1, 0).astype(BF16)
    grad_joined = attend_backward(meta, qkv, logs, grad_attended, cosine, sine, docs, devices)
    grad_normed_one = collect(
        product(grad_joined, full_in, 1, 1).astype(BF16), pack_links, core, sizes
    )
    grad_from_one, gain_one_grad = norm_back(inputs, norm_rate(inputs), gains[0], grad_normed_one)
    tokens_grad = (grad_hidden + grad_from_one).astype(BF16)

    def sum_documents(grad):
        split = (grad * inverse_total).astype(BF16).reshape(sizes["z"], 2, -1, grad.shape[1])
        mine = lax.dynamic_index_in_dim(split, side, 1, keepdims=False)
        other = lax.dynamic_index_in_dim(split, 1 - side, 1, keepdims=False)
        both = (mine.astype(F32) + flip(other, ("x",), sizes).astype(F32)).astype(BF16)
        return lax.psum_scatter(both, "z", scatter_dimension=0, tiled=False).astype(F32)

    attend_out_shard = sum_documents(product(gathered_grad, attended, 0, 0)).T
    attend_in_shard = sum_documents(product(normed_one, grad_joined, 0, 0))

    def regroup(part):
        mine, other = halves(part, 0)
        return in_order(mine[:, None], flip(other, ("x",), sizes)[:, None], is_first, 1)

    pieces_in = [
        regroup(part).reshape(-1, 2, 2, slim) for part in feed_in_parts
    ]
    feed_in_shard = (
        jnp.stack(pieces_in, axis=3)
        .transpose(2, 0, 1, 3, 4)
        .reshape(feed_in.shape)
        .astype(F32)
    )
    pieces_out = [regroup(part) for part in feed_out_parts]
    feed_out_shard = (
        jnp.stack(pieces_out, axis=2).reshape(feed_out.shape[1], feed_out.shape[0]).T.astype(F32)
    )

    matrix_squares = (
        jnp.sum(attend_in_shard * attend_in_shard)
        + jnp.sum(attend_out_shard * attend_out_shard)
        + jnp.sum(feed_in_shard * feed_in_shard)
        + jnp.sum(feed_out_shard * feed_out_shard)
    )
    gain_partial = jnp.stack([gain_one_grad, gain_two_grad]) * inverse_total
    total_squares, gain_grads = lax.psum(
        (matrix_squares, gain_partial), ("z", "x") + tuple(tensor)
    )
    grad_norm = jnp.sqrt(total_squares + jnp.sum(gain_grads * gain_grads))
    clip = jnp.minimum(1.0, CLIP_LIMIT / (grad_norm + 1e-06))
    gain_width = norm_gains.shape[1]
    gain_shard = lax.dynamic_slice_in_dim(
        gain_grads, lax.axis_index(("z", "x")) * gain_width, gain_width, 1
    )
    first = adam(attend_in, attend_in_shard, moment_attend_in, square_attend_in, clip, MATRIX_RATE, MATRIX_DECAY)
    second = adam(attend_out, attend_out_shard, moment_attend_out, square_attend_out, clip, OUTPUT_RATE, MATRIX_DECAY)
    third = adam(feed_in, feed_in_shard, moment_feed_in, square_feed_in, clip, MATRIX_RATE, MATRIX_DECAY)
    fourth = adam(feed_out, feed_out_shard, moment_feed_out, square_feed_out, clip, MATRIX_RATE, MATRIX_DECAY)
    fifth = adam(norm_gains, gain_shard, moment_gains, square_gains, clip, GAIN_RATE, 0.0)
    return (block_out, tokens_grad, grad_norm, *first, *second, *third, *fourth, *fifth)


def solution(mesh):
    depth, across = mesh.shape["dp"], mesh.shape["tensor"]
    tensor = tuple("t" + str(i) for i in range(across.bit_length() - 1))
    sizes = {"z": depth // 2, "x": 2, **{a: 2 for a in tensor}}
    assert depth % 2 == 0 and 2 ** len(tensor) == across
    fine = Mesh(mesh.devices.reshape(tuple(sizes.values())), tuple(sizes))
    dp = ("z", "x")
    both = P(dp + tensor, None)
    rows_cut, columns_cut = P(dp, tensor), P(tensor, dp)
    feed_cut, gain_cut = P(None, dp, tensor), P(None, dp)
    state = (rows_cut,) * 3 + (columns_cut,) * 3 + (feed_cut,) * 3 + (columns_cut,) * 3 + (gain_cut,) * 3
    return jax.shard_map(
        functools.partial(shards, sizes, tensor),
        mesh=fine,
        in_specs=(both, both, P(dp, None), rows_cut, columns_cut, feed_cut, columns_cut, gain_cut)
        + (rows_cut,) * 2
        + (columns_cut,) * 2
        + (feed_cut,) * 2
        + (columns_cut,) * 2
        + (gain_cut,) * 2,
        out_specs=(both, both, P()) + state,
        check_vma=False,
    )
```

time: 1560 us -> 866 us (0.56)
  waiting for transfers between devices: 1020 us -> 308 us
  matrix products: 244 us -> 184 us
  Pallas kernels: 0 us -> 36.3 us
  starting transfers between devices: 1.18 us -> 33.5 us
  other arithmetic: 99 us -> 115 us
    reduce_scatter x8 -> x6, waiting for transfers between devices: 519 us -> 0.03 us  [the longest x2 0.02 us: sum_documents(): lax.psum_scatter(both, 'z', scatter_dimension=0, tiled=False).astype(F32)]
    all_gather x8 -> x6, waiting for transfers between devices: 500 us -> 0.07 us  [the longest x1 0.02 us: shards(): lax.all_gather(attend_out.T.astype(BF16), 'z', axis=0, tiled=False)]
    ppermute x0 -> x34, waiting for transfers between devices: none -> 307 us  [flip(): return lax.ppermute(value, tuple(axes), pairs)]
    dot_general x26 -> x18, matrix products: 244 us -> 184 us  [product(): lax.dot_general(left, right, (((left_dim,), (right_dim,)), ((), ())), pre...]
    dynamic_update_slice x4 -> x0, local copies, waits for them, and re-layouts: 41.4 us -> none  [shards(): lax.scan(backward_block, (zero_heads, zero_heads), (jnp.arange(blocks, dt...]
    pallas_call x0 -> x2, Pallas kernels: none -> 36.3 us  [the longest x1 22.8 us: attend_backward(): pl.pallas_call(functools.partial(backward_kernel, docs, devices), grid=(g...]
    ppermute x0 -> x34, starting transfers between devices: none -> 33 us  [flip(): return lax.ppermute(value, tuple(axes), pairs)]
    slice x1 -> x15, local copies, waits for them, and re-layouts: 0.6 us -> 24.7 us  [the longest x4 12.8 us: collect(): near = flip(partial[half:], (core,), sizes)]
  transfers between devices with their start and end apart: 16 -> 46, of which waited for: 14 -> 16; matrix products, arithmetic and copies ran while one was open for 21% -> 39% of each run, Pallas kernels for 0% -> 4%
where the time goes in v1:
time: 866 us; the launch traced here: 860 us
  waiting for transfers between devices  308 us (36%)
  matrix products  184 us (21%)
  other arithmetic  115 us (13%)
  local copies, waits for them, and re-layouts  103 us (12%)
  blocking collectives  58.8 us (7%)
  Pallas kernels  36.3 us (4%)
  starting transfers between devices  33.5 us (4%)
  between operations  20.6 us (2%)
    ppermute x34, waiting for transfers between devices, flip(): return lax.ppermute(value, tuple(axes), pairs)  307 us
    dot_general x18, matrix products, product(): lax.dot_general(left, right, (((left_dim,), (right_dim,)), ((), ())), pre...  184 us
    psum x1, blocking collectives, shards(): lax.psum((matrix_squares, gain_partial), ('z', 'x') + tuple(tensor))  38 us
    ppermute x34, starting transfers between devices, flip(): return lax.ppermute(value, tuple(axes), pairs)  33 us
    unnamed x185, local copies, waits for them, and re-layouts  28.7 us
    pallas_call x1, Pallas kernels, attend_backward(): pl.pallas_call(functools.partial(backward_kernel, docs, devices), grid=(g...  22.8 us
    all_gather x1, blocking collectives, shards(): lax.all_gather(norm_gains.astype(BF16), ('z', 'x'), axis=1, tiled=True)  20.8 us
    sub x5, other arithmetic, adam(): weight - rate * (direction + decay * weight)  18.7 us
  transfers between devices with their start and end apart: 46, of which 16 were waited for; matrix products, arithmetic and copies ran while one was open for 39% of the time, Pallas kernels for 4%

profile of v1, /device:TPU:0, one launch (start us, length us, event | category | flops | bytes accessed | tf_op | source)
XLA Modules:
  0.0 859.9 jit_solution(12908407505581024833)
XLA Ops:
  22.6 16.9 %collective-permute-done.11 = bf16[256,1536]{0,1:T(8,128)(2,1)} collective-permute-done((bf16[256,1536]{0,1:T(8,128)(2,1)S(1)}, bf16[256,1536]{0,1:T(8,128)(2,1)}, u32[]{:S(2)}, u32[]{:S(2)}) %collective-permute-start.11) | collective-permute-done | bytes 786464 | tf_op jit(solution)/shard_map/ppermute | solution.py:39
  45.8 22.6 %collective-permute-done = bf16[256,2048]{1,0:T(8,128)(2,1)S(1)} collective-permute-done((bf16[256,2048]{1,0:T(8,128)(2,1)S(1)}, bf16[256,2048]{1,0:T(8,128)(2,1)S(1)}, u32[]{:S(2)}, u32[]{:S(2)}) %collective-permute-start) | collective-permute-done | bytes 1048608 | tf_op jit(solution)/shard_map/ppermute | solution.py:39
  70.2 20.8 %all_gather.27 = bf16[2,2048]{1,0:T(2,128)(2,1)S(1)} all-gather(bf16[2,256]{1,0:T(2,128)(2,1)S(1)} %convert_element_type.223), channel_id=1, replica_groups=mesh['z'=4,'x'=2,'t0'=2,'t1'=2] {'z','x'}, dimensions={1}, use_global_device_ids=true | all-gather | bytes 9216 | tf_op jit(solution)/shard_map/all_gather | solution.py:392
  99.6 19.4 %collective-permute-done.3 = bf16[4,256,512]{2,1,0:T(8,128)(2,1)} collective-permute-done((bf16[4,256,512]{2,1,0:T(8,128)(2,1)S(1)}, bf16[4,256,512]{2,1,0:T(8,128)(2,1)}, u32[]{:S(2)}, u32[]{:S(2)}) %collective-permute-start.3) | collective-permute-done | bytes 1048608 | tf_op jit(solution)/shard_map/ppermute | solution.py:39
  124.0 24.5 %collective-permute-done.2 = bf16[4,256,768]{2,1,0:T(8,128)(2,1)} collective-permute-done((bf16[4,256,768]{2,1,0:T(8,128)(2,1)}, bf16[4,256,768]{2,1,0:T(8,128)(2,1)}, u32[]{:S(2)}, u32[]{:S(2)}) %collective-permute-start.2) | collective-permute-done | bytes 1572896 | tf_op jit(solution)/shard_map/ppermute | solution.py:39
  157.0 13.5 %attend_forward.1 = (bf16[1024,512]{1,0:T(8,128)(2,1)S(1)}, bf16[1024,768]{1,0:T(8,128)(2,1)S(1)}, f32[2,8,1024]{2,1,0:T(8,128)S(1)}) custom-call(s32[3]{0:T(128)S(1)} %pad_add_fusion.meta_ref, f32[1024,768]{1,0:T(8,128)S(1)} %fusion.48.joined_ref, f32[1024,128]{1,0:T(8,128)S(1)} %get-tuple-element.94.cos_ref, f32[1024,128]{1,0:T(8,128)S(1)} %get-tuple-element.95.sin_ref), custom_call_target="tpu_custom_call" | custom-call | flops 4294967296 | bytes 6291456 | tf_op jit(solution)/shard_map/attend_forward/pallas_call | solution.py:239
  175.0 19.7 %collective-permute-done.10 = bf16[256,1536]{0,1:T(8,128)(2,1)S(1)} collective-permute-done((bf16[256,1536]{0,1:T(8,128)(2,1)S(1)}, bf16[256,1536]{0,1:T(8,128)(2,1)S(1)}, u32[]{:S(2)}, u32[]{:S(2)}) %collective-permute-start.10) | collective-permute-done | bytes 786464 | tf_op jit(solution)/shard_map/ppermute | solution.py:39
  213.0 43.5 %collective-permute-done.5 = bf16[256,2048]{1,0:T(8,128)(2,1)S(1)} collective-permute-done((bf16[256,2048]{1,0:T(8,128)(2,1)S(1)}, bf16[256,2048]{1,0:T(8,128)(2,1)S(1)}, u32[]{:S(2)}, u32[]{:S(2)}) %collective-permute-start.5) | collective-permute-done | bytes 1048608 | tf_op jit(solution)/shard_map/ppermute | solution.py:39
  263.8 37.6 %collective-permute-done.16 = bf16[256,2048]{1,0:T(8,128)(2,1)S(1)} collective-permute-done((bf16[256,2048]{1,0:T(8,128)(2,1)S(1)}, bf16[256,2048]{1,0:T(8,128)(2,1)S(1)}, u32[]{:S(2)}, u32[]{:S(2)}) %collective-permute-start.16) | collective-permute-done | bytes 1048608 | tf_op jit(solution)/shard_map/ppermute | solution.py:39
  306.7 16.0 %collective-permute-done.6 = bf16[256,2048]{1,0:T(8,128)(2,1)S(1)} collective-permute-done((bf16[256,2048]{1,0:T(8,128)(2,1)S(1)}, bf16[256,2048]{1,0:T(8,128)(2,1)S(1)}, u32[]{:S(2)}, u32[]{:S(2)}) %collective-permute-start.6) | collective-permute-done | bytes 1048608 | tf_op jit(solution)/shard_map/ppermute | solution.py:39
  346.8 14.8 %fusion.65 = f32[2048,1024]{0,1:T(8,128)} fusion(bf16[2048,2048]{1,0:T(8,128)(2,1)} %constant_dynamic-update-slice_fusion, bf16[2048,1024]{0,1:T(8,128)(2,1)} %all-gather.13.cloned.1.call-done), kind=kOutput, calls=%fused_computation.184 | convolution fusion | flops 8589934592 | bytes 20971520 | tf_op jit(solution)/shard_map/dot_general | solution.py:310
  361.6 13.6 %multiply_convert_fusion.7 = (bf16[2048,512]{0,1:T(8,128)(2,1)S(1)}, bf16[2048,512]{0,1:T(8,128)(2,1)}, bf16[2048,512]{0,1:T(8,128)(2,1)S(1)}) fusion(f32[2048,1024]{0,1:T(8,128)} %fusion.65, bf16[2048,2048]{1,0:T(8,128)(2,1)} %constant_dynamic-update-slice_fusion.5, bf16[2048,512]{0,1:T(8,128)(2,1)} %all-gather.15.cloned.1.call-done), kind=kOutput, calls=%fused_computation.31 | convolution fusion | flops 4310695936 | bytes 25165824 | tf_op jit(solution)/shard_map/dot_general | solution.py:310
  386.0 15.3 %fusion.63 = f32[2048,1024]{0,1:T(8,128)} fusion(bf16[2048,2048]{1,0:T(8,128)(2,1)} %constant_dynamic-update-slice_fusion, bf16[2048,1024]{0,1:T(8,128)(2,1)} %all-gather.9.cloned.1.call-done), kind=kOutput, calls=%fused_computation.182 | convolution fusion | flops 8589934592 | bytes 20971520 | tf_op jit(solution)/shard_map/dot_general | solution.py:310
  401.3 14.4 %multiply_convert_fusion.9 = (bf16[2048,512]{0,1:T(8,128)(2,1)}, bf16[2048,512]{0,1:T(8,128)(2,1)}, bf16[2048,512]{0,1:T(8,128)(2,1)S(1)}) fusion(f32[2048,1024]{0,1:T(8,128)} %fusion.63, bf16[2048,2048]{1,0:T(8,128)(2,1)} %constant_dynamic-update-slice_fusion.5, bf16[2048,512]{0,1:T(8,128)(2,1)} %all-gather.11.cloned.1.call-done), kind=kOutput, calls=%fused_computation.33 | convolution fusion | flops 4310695936 | bytes 25165824 | tf_op jit(solution)/shard_map/dot_general | solution.py:310
  426.7 13.5 %multiply_convert_fusion = bf16[2048,1024]{1,0:T(8,128)(2,1)} fusion(bf16[2048,2048]{1,0:T(8,128)(2,1)} %constant_dynamic-update-slice_fusion, bf16[2048,512]{0,1:T(8,128)(2,1)} %get-tuple-element.51, bf16[2048,512]{0,1:T(8,128)(2,1)S(1)} %get-tuple-element.50), kind=kOutput, calls=%fused_computation.7 | convolution fusion | flops 8602517504 | bytes 16777216 | tf_op jit(solution)/shard_map/dot_general | solution.py:310
  440.3 15.7 %fusion.9 = f32[2048,2048]{1,0:T(8,128)} fusion(bf16[2048,1024]{0,1:T(8,128)(2,1)} %all-gather.9.cloned.1.call-done, bf16[2048,512]{0,1:T(8,128)(2,1)} %get-tuple-element.53, bf16[2048,512]{0,1:T(8,128)(2,1)} %get-tuple-element.52), kind=kOutput, calls=%fused_computation.52 | convolution fusion | flops 8598323200 | bytes 25165824 | tf_op jit(solution)/shard_map/dot_general | solution.py:310
  456.0 14.6 %add_convert_fusion = bf16[2048,2048]{1,0:T(8,128)(2,1)} fusion(f32[2048,2048]{1,0:T(8,128)} %fusion.9, bf16[2048,1024]{0,1:T(8,128)(2,1)S(1)} %copy-done.78, bf16[2048,512]{0,1:T(8,128)(2,1)S(1)} %copy-done.85, bf16[2048,512]{0,1:T(8,128)(2,1)S(1)} %get-tuple-element.50), kind=kOutput, calls=%fused_computation | convolution fusion | flops 8606711808 | bytes 33554432 | tf_op jit(solution)/shard_map/dot_general | solution.py:310
  493.8 13.0 %multiply_convert_fusion.1 = bf16[2048,1024]{1,0:T(8,128)(2,1)} fusion(bf16[2048,2048]{1,0:T(8,128)(2,1)} %constant_dynamic-update-slice_fusion, bf16[2048,512]{0,1:T(8,128)(2,1)S(1)} %copy-done.87, bf16[2048,512]{0,1:T(8,128)(2,1)S(1)} %copy-done.86), kind=kOutput, calls=%fused_computation.8 | convolution fusion | flops 8602517504 | bytes 16777216 | tf_op jit(solution)/shard_map/dot_general | solution.py:310
  506.9 31.6 %collective-permute-done.21 = bf16[256,2048]{1,0:T(8,128)(2,1)} collective-permute-done((bf16[256,2048]{1,0:T(8,128)(2,1)}, bf16[256,2048]{1,0:T(8,128)(2,1)}, u32[]{:S(2)}, u32[]{:S(2)}) %collective-permute-start.21) | collective-permute-done | bytes 1048608 | tf_op jit(solution)/shard_map/ppermute | solution.py:39
  555.1 13.7 %collective-permute-done.24 = bf16[256,2048]{1,0:T(8,128)(2,1)S(1)} collective-permute-done((bf16[256,2048]{1,0:T(8,128)(2,1)S(1)}, bf16[256,2048]{1,0:T(8,128)(2,1)S(1)}, u32[]{:S(2)}, u32[]{:S(2)}) %collective-permute-start.24) | collective-permute-done | bytes 1048608 | tf_op jit(solution)/shard_map/ppermute | solution.py:39
  604.0 22.8 %attend_backward.1 = bf16[1024,768]{1,0:T(8,128)(2,1)S(1)} custom-call(s32[3]{0:T(128)S(1)} %pad_add_fusion.meta_ref, bf16[1024,768]{1,0:T(8,128)(2,1)S(1)} %copy-done.3, f32[2,8,1024]{2,1,0:T(8,128)S(1)} %get-tuple-element.23.log_ref, bf16[1024,512]{1,0:T(8,128)(2,1)S(1)} %fusion.23.back_ref, f32[1024,128]{1,0:T(8,128)S(1)} %get-tuple-element.94.cos_ref, ...), custom_call_target="tpu_custom_call" | custom-call | flops 10737418240 | bytes 6291456 | tf_op jit(solution)/shard_map/attend_backward/pallas_call | solution.py:277
  663.4 20.4 %collective-permute-done.28 = bf16[4,256,768]{2,1,0:T(8,128)(2,1)} collective-permute-done((bf16[4,256,768]{2,1,0:T(8,128)(2,1)}, bf16[4,256,768]{2,1,0:T(8,128)(2,1)}, u32[]{:S(2)}, u32[]{:S(2)}) %collective-permute-start.28) | collective-permute-done | bytes 1572896 | tf_op jit(solution)/shard_map/ppermute | solution.py:39
  728.5 26.9 %collective-permute-done.27 = bf16[256,2048]{1,0:T(8,128)(2,1)} collective-permute-done((bf16[256,2048]{1,0:T(8,128)(2,1)}, bf16[256,2048]{1,0:T(8,128)(2,1)}, u32[]{:S(2)}, u32[]{:S(2)}) %collective-permute-start.27) | collective-permute-done | bytes 1048608 | tf_op jit(solution)/shard_map/ppermute | solution.py:39
  768.1 38.0 %all-reduce = (f32[]{:T(128)}, f32[2,2048]{1,0:T(2,128)S(1)}) all-reduce(f32[]{:T(128)S(6)} %add.301, f32[2,2048]{1,0:T(2,128)S(1)} %maximum_multiply_fusion), channel_id=1, replica_groups=mesh['z'=4,'x'=2,'t0'=2,'t1'=2] {'z','x','t0','t1'}, use_global_device_ids=true, to_apply=%region_17.18 | all-reduce | flops 4097 | bytes 32776 | tf_op jit(solution)/shard_map/psum | solution.py:520
  (377 shorter events, 336.6 us)
Async XLA Ops:
  7.2 84.0 %all-gather.19.cloned.1.call-start = ((), (), s32[]{:S(2)}) async-start(), calls=%async_computation.17 | async-start | bytes 1310720 | tf_op jit(solution)/shard_map/all_gather | solution.py:393
  9.0 83.8 %all-gather.17.cloned.1.call-start = ((), (), s32[]{:S(2)}) async-start(), calls=%async_computation.16 | async-start | bytes 1966080 | tf_op jit(solution)/shard_map/all_gather | solution.py:385
  11.0 335.8 %all-gather.13.cloned.1.call-start = ((), (), s32[]{:S(2)}) async-start(), calls=%async_computation.8 | async-start | bytes 5242880 | tf_op jit(solution)/shard_map/all_gather | solution.py:422
  43.9 317.7 %all-gather.15.cloned.1.call-start = ((), (), s32[]{:S(2)}) async-start(), calls=%async_computation.9 | async-start | bytes 2621440 | tf_op jit(solution)/shard_map/all_gather | solution.py:423
  92.9 55.6 %collective-permute-start.2 = (bf16[4,256,768]{2,1,0:T(8,128)(2,1)}, bf16[4,256,768]{2,1,0:T(8,128)(2,1)}, u32[]{:S(2)}, u32[]{:S(2)}) collective-permute-start(bf16[4,256,768]{2,1,0:T(8,128)(2,1)} %bitcast.131), channel_id=1, source_target_pairs={{0,4},{4,0},{1,5},{5,1},{2,6},{6,2},{3,7},{7,3},{8,12},{12,8},{9,1... | collective-permute-start | bytes 4718600 | tf_op jit(solution)/shard_map/ppermute | solution.py:39
  99.6 286.5 %all-gather.9.cloned.1.call-start = ((), (), s32[]{:S(2)}) async-start(), calls=%async_computation.6 | async-start | bytes 5242880 | tf_op jit(solution)/shard_map/all_gather | solution.py:422
  204.6 196.7 %all-gather.11.cloned.1.call-start = ((), (), s32[]{:S(2)}) async-start(), calls=%async_computation.7 | async-start | bytes 2621440 | tf_op jit(solution)/shard_map/all_gather | solution.py:423
  209.5 53.8 %collective-permute-start.18 = (bf16[256,2048]{1,0:T(8,128)(2,1)S(1)}, bf16[256,2048]{1,0:T(8,128)(2,1)S(1)}, u32[]{:S(2)}, u32[]{:S(2)}) collective-permute-start(bf16[256,2048]{1,0:T(8,128)(2,1)S(1)} %copy-done.14), channel_id=1, source_target_pairs={{0,6},{2,4},{4,2},{6,0},{1,7},{3,5},{5,3},{7,1},{8,14},{10,12},{12... | collective-permute-start | bytes 3145736 | tf_op jit(solution)/shard_map/ppermute | solution.py:39
  209.7 54.1 %collective-permute-start.17 = (bf16[256,2048]{1,0:T(8,128)(2,1)S(1)}, bf16[256,2048]{1,0:T(8,128)(2,1)S(1)}, u32[]{:S(2)}, u32[]{:S(2)}) collective-permute-start(bf16[256,2048]{1,0:T(8,128)(2,1)S(1)} %copy-done.14), channel_id=1, source_target_pairs={{0,4},{4,0},{1,5},{5,1},{2,6},{6,2},{3,7},{7,3},{8,12},{12,8},{9,1... | collective-permute-start | bytes 3145736 | tf_op jit(solution)/shard_map/ppermute | solution.py:39
  211.5 90.0 %collective-permute-start.16 = (bf16[256,2048]{1,0:T(8,128)(2,1)S(1)}, bf16[256,2048]{1,0:T(8,128)(2,1)S(1)}, u32[]{:S(2)}, u32[]{:S(2)}) collective-permute-start(bf16[256,2048]{1,0:T(8,128)(2,1)S(1)} %copy-done.14), channel_id=1, source_target_pairs={{0,2},{2,0},{1,3},{3,1},{4,6},{6,4},{5,7},{7,5},{8,10},{10,8},{9,1... | collective-permute-start | bytes 3145736 | tf_op jit(solution)/shard_map/ppermute | solution.py:39
  263.3 59.4 %collective-permute-start.6 = (bf16[256,2048]{1,0:T(8,128)(2,1)S(1)}, bf16[256,2048]{1,0:T(8,128)(2,1)S(1)}, u32[]{:S(2)}, u32[]{:S(2)}) collective-permute-start(bf16[256,2048]{1,0:T(8,128)(2,1)S(1)} %get-tuple-element.47), channel_id=1, source_target_pairs={{0,2},{2,0},{1,3},{3,1},{4,6},{6,4},{5,7},{7,5},{8,10},{10,8},{9,1... | collective-permute-start | bytes 3145736 | tf_op jit(solution)/shard_map/ppermute | solution.py:39
  328.1 258.2 %reduce-scatter.17.cloned.1.call-start = ((), (), s32[]{:S(2)}) async-start(), calls=%async_computation.15 | async-start | bytes 2621440 | tf_op jit(solution)/shard_map/reduce_scatter | solution.py:453
  386.0 202.4 %reduce-scatter.15.cloned.1.call-start = ((), (), s32[]{:S(2)}) async-start(), calls=%async_computation.14 | async-start | bytes 2621440 | tf_op jit(solution)/shard_map/reduce_scatter | solution.py:453
  426.7 231.9 %reduce-scatter.13.cloned.1.call-start = ((), (), s32[]{:S(2)}) async-start(), calls=%async_computation.13 | async-start | bytes 5242880 | tf_op jit(solution)/shard_map/reduce_scatter | solution.py:461
  440.2 221.0 %reduce-scatter.11.cloned.1.call-start = ((), (), s32[]{:S(2)}) async-start(), calls=%async_computation.12 | async-start | bytes 5242880 | tf_op jit(solution)/shard_map/reduce_scatter | solution.py:461
  506.8 220.1 %reduce-scatter.9.cloned.1.call-start = ((), (), s32[]{:S(2)}) async-start(), calls=%async_computation.11 | async-start | bytes 1310720 | tf_op jit(solution)/shard_map/reduce_scatter | solution.py:490
  585.9 63.5 %collective-permute-start.12 = (bf16[1024,2048]{1,0:T(8,128)(2,1)}, bf16[1024,2048]{1,0:T(8,128)(2,1)}, u32[]{:S(2)}, u32[]{:S(2)}) collective-permute-start(bf16[1024,2048]{1,0:T(8,128)(2,1)} %slice.189), channel_id=1, source_target_pairs={{0,1},{1,0},{2,3},{3,2},{4,5},{5,4},{6,7},{7,6},{8,9},{9,8},{10,11... | collective-permute-start | bytes 12582920 | tf_op jit(solution)/shard_map/ppermute | solution.py:39
  588.1 100.8 %collective-permute-start.33 = (bf16[256,512]{1,0:T(8,128)(2,1)}, bf16[256,512]{1,0:T(8,128)(2,1)}, u32[]{:S(2)}, u32[]{:S(2)}) collective-permute-start(bf16[256,512]{1,0:T(8,128)(2,1)} %get-tuple-element.84), channel_id=1, source_target_pairs={{0,4},{4,0},{1,5},{5,1},{2,6},{6,2},{3,7},{7,3},{8,12},{12,8},{9,1... | collective-permute-start | bytes 786440 | tf_op jit(solution)/shard_map/ppermute | solution.py:39
  590.2 101.4 %collective-permute-start.32 = (bf16[256,512]{1,0:T(8,128)(2,1)}, bf16[256,512]{1,0:T(8,128)(2,1)}, u32[]{:S(2)}, u32[]{:S(2)}) collective-permute-start(bf16[256,512]{1,0:T(8,128)(2,1)} %get-tuple-element.82), channel_id=1, source_target_pairs={{0,4},{4,0},{1,5},{5,1},{2,6},{6,2},{3,7},{7,3},{8,12},{12,8},{9,1... | collective-permute-start | bytes 786440 | tf_op jit(solution)/shard_map/ppermute | solution.py:39
  638.5 119.4 %reduce-scatter.7.cloned.1.call-start = ((), (), s32[]{:S(2)}) async-start(), calls=%async_computation.10 | async-start | bytes 1966080 | tf_op jit(solution)/shard_map/reduce_scatter | solution.py:490
  649.3 63.4 %collective-permute-start.26 = (bf16[512,2048]{1,0:T(8,128)(2,1)}, bf16[512,2048]{1,0:T(8,128)(2,1)S(1)}, u32[]{:S(2)}, u32[]{:S(2)}) collective-permute-start(bf16[512,2048]{1,0:T(8,128)(2,1)} %slice.201), channel_id=1, source_target_pairs={{0,1},{1,0},{2,3},{3,2},{4,5},{5,4},{6,7},{7,6},{8,9},{9,8},{10,11... | collective-permute-start | bytes 6291464 | tf_op jit(solution)/shard_map/ppermute | solution.py:39
  689.0 73.3 %collective-permute-start.13 = (bf16[256,2048]{1,0:T(8,128)(2,1)}, bf16[256,2048]{1,0:T(8,128)(2,1)}, u32[]{:S(2)}, u32[]{:S(2)}) collective-permute-start(bf16[256,2048]{1,0:T(8,128)(2,1)} %get-tuple-element.59), channel_id=1, source_target_pairs={{0,2},{2,0},{1,3},{3,1},{4,6},{6,4},{5,7},{7,5},{8,10},{10,8},{9,1... | collective-permute-start | bytes 3145736 | tf_op jit(solution)/shard_map/ppermute | solution.py:39
  691.6 70.6 %collective-permute-start.15 = (bf16[256,2048]{1,0:T(8,128)(2,1)}, bf16[256,2048]{1,0:T(8,128)(2,1)}, u32[]{:S(2)}, u32[]{:S(2)}) collective-permute-start(bf16[256,2048]{1,0:T(8,128)(2,1)} %get-tuple-element.60), channel_id=1, source_target_pairs={{0,6},{2,4},{4,2},{6,0},{1,7},{3,5},{5,3},{7,1},{8,14},{10,12},{12... | collective-permute-start | bytes 3145736 | tf_op jit(solution)/shard_map/ppermute | solution.py:39
  699.0 63.3 %collective-permute-start.14 = (bf16[256,2048]{1,0:T(8,128)(2,1)}, bf16[256,2048]{1,0:T(8,128)(2,1)}, u32[]{:S(2)}, u32[]{:S(2)}) collective-permute-start(bf16[256,2048]{1,0:T(8,128)(2,1)} %get-tuple-element.61), channel_id=1, source_target_pairs={{0,4},{4,0},{1,5},{5,1},{2,6},{6,2},{3,7},{7,3},{8,12},{12,8},{9,1... | collective-permute-start | bytes 3145736 | tf_op jit(solution)/shard_map/ppermute | solution.py:39
  (110 other events, 2181.8 us)
Sparse Core Ops, SparseCore 0:
  10.2 32.8 all-gather.18
  45.2 35.4 all-gather.16
  82.3 79.5 all-gather.12
  163.9 44.4 all-gather.14
  210.4 79.4 all-gather.8
  328.3 43.3 all-gather.10
  386.1 41.3 reduce-scatter.16
  429.9 43.1 reduce-scatter.14
  476.0 76.0 reduce-scatter.12
  554.3 77.2 reduce-scatter.10
  638.6 25.4 reduce-scatter.8
  689.1 32.5 reduce-scatter.6

commit v2 on v1

--- a/solution.py
+++ b/solution.py
@@ -16,7 +16,7 @@
 STEP = 10
 LANES = 128
 QUERY_ROWS = 256
-CHUNKS = 2
+UNITS = 4
 
 EPSILON = 1e-05
 NEGATIVE = -1e30
@@ -46,23 +46,59 @@
     ]
 
 
-def spread(block, links, core, sizes):
-    parts = [block] + [flip(block, c, sizes) for c in combos(links)[1:]]
-    mine = jnp.concatenate(parts, axis=0) if len(parts) > 1 else block
-    return jnp.concatenate([mine, flip(mine, (core,), sizes)], axis=0)
-
-
-def collect(partial, links, core, sizes):
-    half = partial.shape[0] // 2
-    near = flip(partial[half:], (core,), sizes)
-    mine = (partial[:half].astype(F32) + near.astype(F32)).astype(BF16)
+def add_kernel(mine_ref, near_ref, *out_refs):
+    for k, ref in enumerate(out_refs):
+
+        @pl.when(pl.program_id(0) == k)
+        def _():
+            ref[...] = (mine_ref[...].astype(F32) + near_ref[...].astype(F32)).astype(BF16)
+
+
+def add_blocks(mine, near, count):
+    rows, width = mine.shape[0] // count, mine.shape[1]
+    cut = pl.BlockSpec((rows, width), lambda i: (i, 0))
+    return pl.pallas_call(
+        add_kernel,
+        grid=(count,),
+        in_specs=[cut, cut],
+        out_specs=[pl.BlockSpec((rows, width), lambda i: (0, 0))] * count,
+        out_shape=[jax.ShapeDtypeStruct((rows, width), BF16)] * count,
+        compiler_params=pltpu.CompilerParams(vmem_limit_bytes=32 * 2**20),
+        cost_estimate=pl.CostEstimate(
+            flops=mine.size, bytes_accessed=6 * mine.size, transcendentals=0
+        ),
+        name="add_blocks",
+    )(mine, near)
+
+
+def collect(mine, near, links, core, sizes):
     places = combos(links)
-    rows = half // len(places)
-    total = mine[:rows].astype(F32)
-    for place, c in enumerate(places):
-        if place:
-            total = total + flip(mine[place * rows : (place + 1) * rows], c, sizes).astype(F32)
-    return total
+    blocks = add_blocks(mine, flip(near, (core,), sizes), len(places))
+    return blocks[0], [flip(block, c, sizes) for block, c in zip(blocks[1:], places[1:])]
+
+
+def added(own, moved):
+    return sum((block.astype(F32) for block in moved), own.astype(F32))
+
+
+def gather_depth(block, sizes):
+    copies = jnp.broadcast_to(block, (sizes["z"],) + block.shape)
+    return lax.all_to_all(copies, "z", 0, 0, tiled=True)
+
+
+def sum_depth(blocks):
+    arrived = lax.all_to_all(blocks, "z", 0, 0, tiled=True)
+    return jnp.sum(arrived.astype(F32), axis=0).astype(BF16)
+
+
+def sum_everywhere(value, tensor, sizes):
+    for a in tuple(reversed(tensor)) + ("x",):
+        value = value + flip(value, (a,), sizes)
+    step, count = 1, sizes["z"]
+    while step < count:
+        value = value + lax.ppermute(value, "z", [(i, i ^ step) for i in range(count)])
+        step *= 2
+    return value
 
 
 def frequencies(head_size):
@@ -269,24 +305,23 @@
     )(meta, joined, cosine, sine)
 
 
-def attend_backward(meta, qkv, logs, back, cosine, sine, docs, devices):
-    rows, width = qkv.shape
+def attend_backward(meta, qkv, logs, back, cosine, sine, docs, devices, group):
+    rows = qkv.shape[0]
     wide = (GROUP + 2) * HD
-    groups = width // wide
     whole = pl.BlockSpec((rows, LANES), lambda g: (0, 0))
     return pl.pallas_call(
         functools.partial(backward_kernel, docs, devices),
-        grid=(groups,),
+        grid=(1,),
         in_specs=[
             pl.BlockSpec(memory_space=pltpu.SMEM),
-            pl.BlockSpec((rows, wide), lambda g: (0, g)),
-            pl.BlockSpec((1, 8, rows), lambda g: (g, 0, 0)),
-            pl.BlockSpec((rows, GROUP * HD), lambda g: (0, g)),
+            pl.BlockSpec((rows, wide), lambda g: (0, group)),
+            pl.BlockSpec((1, 8, rows), lambda g: (group, 0, 0)),
+            pl.BlockSpec((rows, GROUP * HD), lambda g: (0, group)),
             whole,
             whole,
         ],
-        out_specs=pl.BlockSpec((rows, wide), lambda g: (0, g)),
-        out_shape=jax.ShapeDtypeStruct((rows, width), BF16),
+        out_specs=pl.BlockSpec((rows, wide), lambda g: (0, 0)),
+        out_shape=jax.ShapeDtypeStruct((rows, wide), BF16),
         scratch_shapes=[
             pltpu.VMEM((2, rows, LANES), BF16),
             pltpu.VMEM((2, rows, LANES), BF16),
@@ -298,9 +333,9 @@
         ],
         compiler_params=pltpu.CompilerParams(vmem_limit_bytes=32 * 2**20),
         cost_estimate=pl.CostEstimate(
-            flops=groups * GROUP * rows * rows * LANES * 10,
-            bytes_accessed=rows * width * 8,
-            transcendentals=groups * GROUP * rows * rows // 2,
+            flops=GROUP * rows * rows * LANES * 10,
+            bytes_accessed=rows * wide * 8,
+            transcendentals=GROUP * rows * rows // 2,
         ),
         name="attend_backward",
     )(meta, qkv, logs, back, cosine, sine)
@@ -335,6 +370,256 @@
         / (jnp.sqrt(square_new / (1.0 - BETA_TWO**STEP)) + ADAM_EPSILON)
     )
     return (weight - rate * (direction + decay * weight), moment_new, square_new)
+
+
+def adam_kernel(rate, decay, clip_ref, weight_ref, grad_ref, moment_ref, square_ref, *out_refs):
+    done = adam(
+        weight_ref[...],
+        grad_ref[...].astype(F32),
+        moment_ref[...],
+        square_ref[...],
+        clip_ref[0],
+        rate,
+        decay,
+    )
+    for ref, value in zip(out_refs, done):
+        ref[...] = value
+
+
+def update(weight, grad, moment, square, clip, rate, decay):
+    shape = weight.shape
+    rows, columns = math.prod(shape[:-1]), shape[-1]
+    tall = rows // 2
+    spec = pl.BlockSpec((tall, columns), lambda i: (i, 0))
+    flat = [a.reshape(rows, columns) for a in (weight, grad, moment, square)]
+    done = pl.pallas_call(
+        functools.partial(adam_kernel, rate, decay),
+        grid=(rows // tall,),
+        in_specs=[pl.BlockSpec(memory_space=pltpu.SMEM)] + [spec] * 4,
+        out_specs=[spec] * 3,
+        out_shape=[jax.ShapeDtypeStruct((rows, columns), F32)] * 3,
+        compiler_params=pltpu.CompilerParams(vmem_limit_bytes=60 * 2**20),
+        cost_estimate=pl.CostEstimate(
+            flops=rows * columns * 16, bytes_accessed=rows * columns * 26, transcendentals=rows * columns
+        ),
+        name="update",
+    )(clip.reshape(1), *flat)
+    return [a.reshape(shape) for a in done]
+
+
+def adam_rows_kernel(rate, decay, side_ref, clip_ref, weight_ref, grad_ref, moment_ref, square_ref, *out_refs):
+    heads, _, columns = weight_ref.shape
+    halves = grad_ref.shape[1]
+    unit = columns // (2 * UNITS)
+    per_half = UNITS // halves
+    for n in range(2 * UNITS):
+        which, half, place = n // UNITS, n % UNITS // per_half, n % per_half
+        cut = slice(n * unit, (n + 1) * unit)
+        for j in range(heads):
+            first = (heads * place + j) * unit
+            done = adam(
+                weight_ref[j, :, cut],
+                grad_ref[which ^ side_ref[0], half, :, first : first + unit].astype(F32),
+                moment_ref[j, :, cut],
+                square_ref[j, :, cut],
+                clip_ref[0],
+                rate,
+                decay,
+            )
+            for ref, value in zip(out_refs, done):
+                ref[j, :, cut] = value
+
+
+def adam_columns_kernel(rate, decay, side_ref, clip_ref, weight_ref, grad_ref, moment_ref, square_ref, *out_refs):
+    done = adam(
+        weight_ref[...],
+        grad_ref[0, 0].astype(F32).T,
+        moment_ref[...],
+        square_ref[...],
+        clip_ref[0],
+        rate,
+        decay,
+    )
+    for ref, value in zip(out_refs, done):
+        ref[...] = value
+
+
+def update_pieces(kernel, weight, pieces, moment, square, clip, side, block, at, piece_block, piece_at, rate, decay):
+    spec = pl.BlockSpec(block, lambda i, s: at(i))
+    grid_spec = pltpu.PrefetchScalarGridSpec(
+        num_scalar_prefetch=1,
+        grid=(weight.size // math.prod(block),),
+        in_specs=[
+            pl.BlockSpec(memory_space=pltpu.SMEM),
+            spec,
+            pl.BlockSpec(piece_block, lambda i, s: piece_at(i, s[0])),
+            spec,
+            spec,
+        ],
+        out_specs=[spec] * 3,
+    )
+    return pl.pallas_call(
+        functools.partial(kernel, rate, decay),
+        grid_spec=grid_spec,
+        out_shape=[jax.ShapeDtypeStruct(weight.shape, F32)] * 3,
+        compiler_params=pltpu.CompilerParams(vmem_limit_bytes=60 * 2**20),
+        cost_estimate=pl.CostEstimate(
+            flops=weight.size * 16, bytes_accessed=weight.size * 26, transcendentals=weight.size
+        ),
+        name="update_pieces",
+    )(side.reshape(1).astype(jnp.int32), clip.reshape(1), weight, pieces, moment, square)
+
+
+def split_kernel(side_ref, in_ref, out_ref, *unit_refs):
+    unit = unit_refs[0].shape[1] // 3
+    for n, ref in enumerate(unit_refs):
+        cut = slice(n * unit, (n + 1) * unit)
+        ref[:, :unit] = in_ref[0, :, cut].astype(BF16)
+        ref[:, unit : 2 * unit] = in_ref[1, :, cut].astype(BF16)
+        ref[:, 2 * unit :] = out_ref[cut, :].T.astype(BF16)
+
+
+def split_feed(feed_in, feed_out, side, unit):
+    depth, hidden = feed_in.shape[1], feed_in.shape[2] // 2
+    part = jax.ShapeDtypeStruct((depth, 3 * unit), BF16)
+    grid_spec = pltpu.PrefetchScalarGridSpec(
+        num_scalar_prefetch=1,
+        grid=(1,),
+        in_specs=[
+            pl.BlockSpec((2, depth, hidden), lambda i, s: (0, 0, s[0])),
+            pl.BlockSpec((hidden, depth), lambda i, s: (s[0], 0)),
+        ],
+        out_specs=[pl.BlockSpec(part.shape, lambda i, s: (0, 0))] * (hidden // unit),
+    )
+    return pl.pallas_call(
+        split_kernel,
+        grid_spec=grid_spec,
+        out_shape=[part] * (hidden // unit),
+        compiler_params=pltpu.CompilerParams(vmem_limit_bytes=60 * 2**20),
+        cost_estimate=pl.CostEstimate(
+            flops=depth * hidden * 3, bytes_accessed=depth * hidden * 18, transcendentals=0
+        ),
+        name="split_feed",
+    )(side.reshape(1).astype(jnp.int32), feed_in, feed_out)
+
+
+def feed_kernel(rows_ref, back_ref, *refs):
+    *weight_refs, activated_ref, grad_ref = refs
+    for n, weight_ref in enumerate(weight_refs):
+        unit = weight_ref.shape[1] // 3
+        both = jnp.dot(rows_ref[...], weight_ref[:, : 2 * unit], preferred_element_type=F32)
+        back = jnp.dot(back_ref[...], weight_ref[:, 2 * unit :], preferred_element_type=F32)
+        gate, upward = both[:, :unit], both[:, unit:]
+        chance = jax.nn.sigmoid(gate)
+        silu = gate * chance
+        activated_ref[:, n * unit : (n + 1) * unit] = (silu * upward).astype(BF16)
+        grad_ref[:, 2 * n * unit : (2 * n + 1) * unit] = (
+            back * upward * (chance + silu * (1.0 - chance))
+        ).astype(BF16)
+        grad_ref[:, (2 * n + 1) * unit : 2 * (n + 1) * unit] = (back * silu).astype(BF16)
+
+
+def feed_both_ways(rows, back, weights):
+    count, width = rows.shape
+    slim = sum(w.shape[1] // 3 for w in weights)
+    tall = min(count, 512)
+    return pl.pallas_call(
+        feed_kernel,
+        grid=(count // tall,),
+        in_specs=[
+            pl.BlockSpec((tall, width), lambda i: (i, 0)),
+            pl.BlockSpec((tall, width), lambda i: (i, 0)),
+        ]
+        + [pl.BlockSpec(w.shape, lambda i: (0, 0)) for w in weights],
+        out_specs=[
+            pl.BlockSpec((tall, slim), lambda i: (i, 0)),
+            pl.BlockSpec((tall, 2 * slim), lambda i: (i, 0)),
+        ],
+        out_shape=[
+            jax.ShapeDtypeStruct((count, slim), BF16),
+            jax.ShapeDtypeStruct((count, 2 * slim), BF16),
+        ],
+        compiler_params=pltpu.CompilerParams(vmem_limit_bytes=48 * 2**20),
+        cost_estimate=pl.CostEstimate(
+            flops=6 * count * width * slim,
+            bytes_accessed=4 * count * width + 6 * width * slim + 6 * count * slim,
+            transcendentals=count * slim,
+        ),
+        name="feed_both_ways",
+    )(rows, back, *weights)
+
+
+def weights_kernel(scale, rows_ref, grad_ref, back_ref, activated_ref, out_ref):
+    wide = grad_ref.shape[1]
+    out_ref[0, :, :wide] = (product(rows_ref[...], grad_ref[...], 0, 0) * scale).astype(BF16)
+    out_ref[0, :, wide:] = (product(back_ref[...], activated_ref[...], 0, 0) * scale).astype(BF16)
+
+
+def weight_gradients(rows, grad, back, activated, parts, scale):
+    count, width = rows.shape
+    cut, slim = width // parts, activated.shape[1]
+    return pl.pallas_call(
+        functools.partial(weights_kernel, scale),
+        grid=(parts,),
+        in_specs=[
+            pl.BlockSpec((count, cut), lambda i: (0, i)),
+            pl.BlockSpec(grad.shape, lambda i: (0, 0)),
+            pl.BlockSpec((count, cut), lambda i: (0, i)),
+            pl.BlockSpec(activated.shape, lambda i: (0, 0)),
+        ],
+        out_specs=pl.BlockSpec((1, cut, 3 * slim), lambda i: (i, 0, 0)),
+        out_shape=jax.ShapeDtypeStruct((parts, cut, 3 * slim), BF16),
+        compiler_params=pltpu.CompilerParams(vmem_limit_bytes=48 * 2**20),
+        cost_estimate=pl.CostEstimate(
+            flops=6 * count * width * slim,
+            bytes_accessed=4 * count * width + 6 * count * slim + 6 * width * slim,
+            transcendentals=0,
+        ),
+        name="weight_gradients",
+    )(rows, grad, back, activated)
+
+
+def back_kernel(first, last, counts, *refs):
+    total, refs = 0.0, list(refs)
+    for count in counts:
+        left = refs.pop(0)
+        for n in range(count):
+            right = refs.pop(0)
+            unit = right.shape[1] // 3
+            wide = (last - first) * unit
+            total = total + product(
+                left[:, n * wide : (n + 1) * wide],
+                right[:, first * unit : last * unit],
+                1,
+                1,
+            )
+    refs[0][...] = total.astype(BF16)
+
+
+def back_products(pairs, first, last, half):
+    count, width = pairs[0][0].shape[0] // 2, pairs[0][1][0].shape[0]
+    tall = min(count, 512)
+    skip = half * (count // tall)
+    specs, operands = [], []
+    for left, right in pairs:
+        specs.append(pl.BlockSpec((tall, left.shape[1]), lambda i: (i + skip, 0)))
+        specs += [pl.BlockSpec(w.shape, lambda i: (0, 0)) for w in right]
+        operands += [left, *right]
+    depth = sum(left.shape[1] for left, _ in pairs)
+    return pl.pallas_call(
+        functools.partial(back_kernel, first, last, [len(right) for _, right in pairs]),
+        grid=(count // tall,),
+        in_specs=specs,
+        out_specs=pl.BlockSpec((tall, width), lambda i: (i, 0)),
+        out_shape=jax.ShapeDtypeStruct((count, width), BF16),
+        compiler_params=pltpu.CompilerParams(vmem_limit_bytes=56 * 2**20),
+        cost_estimate=pl.CostEstimate(
+            flops=2 * count * width * depth,
+            bytes_accessed=2 * count * (width + depth) + 2 * width * depth,
+            transcendentals=0,
+        ),
+        name="back_products",
+    )(*operands)
 
 
 def in_order(mine, other, first, axis):
@@ -382,24 +667,11 @@
     )
     cosine, sine = rotation_tables(doc_lengths[0], rows)
 
-    attend_in_z = lax.all_gather(attend_in.astype(BF16), "z", axis=0, tiled=False)
-    attend_in_x = flip(attend_in_z, ("x",), sizes)
-    full_in = jnp.where(
-        is_first,
-        jnp.stack([attend_in_z, attend_in_x], axis=1),
-        jnp.stack([attend_in_x, attend_in_z], axis=1),
-    ).reshape(width, attend_in.shape[1])
-    gains = lax.all_gather(norm_gains.astype(BF16), ("z", "x"), axis=1, tiled=True).astype(F32)
-    attend_out_z = lax.all_gather(attend_out.T.astype(BF16), "z", axis=0, tiled=False)
-    attend_out_x = flip(attend_out_z, ("x",), sizes)
-    full_out = jnp.where(
-        is_first,
-        jnp.stack([attend_out_z, attend_out_x], axis=1),
-        jnp.stack([attend_out_x, attend_out_z], axis=1),
-    ).reshape(width, attend_out.shape[0])
-
     hidden = feed_in.shape[2] // 2
-    slim = hidden // CHUNKS
+    slim = hidden // 2
+    unit = hidden // UNITS
+    depth = attend_in.shape[0]
+    half = rows // 2
 
     def halves(array, axis):
         size = array.shape[axis] // 2
@@ -407,129 +679,208 @@
         other = lax.dynamic_slice_in_dim(array, (1 - side) * size, size, axis)
         return mine, other
 
-    in_mine, in_other = halves(feed_in.astype(BF16), 2)
-    out_mine, out_other = halves(feed_out.T.astype(BF16), 1)
-    weights = []
-    for c in range(CHUNKS):
-        cut = slice(c * slim, (c + 1) * slim)
-        mine = jnp.concatenate([in_mine[0, :, cut], in_mine[1, :, cut], out_mine[:, cut]], axis=1)
-        other = jnp.concatenate(
-            [in_other[0, :, cut], in_other[1, :, cut], out_other[:, cut]], axis=1
+    def sends(block, links):
+        return [flip(block, c, sizes) for c in combos(links)[1:]]
+
+    def over_core(blocks):
+        mine = jnp.concatenate(blocks, axis=0)
+        return jnp.concatenate([mine, flip(mine, (core,), sizes)], axis=0)
+
+    def both_sides(mine, other):
+        pair = jnp.where(
+            is_first, jnp.stack([mine, other], axis=1), jnp.stack([other, mine], axis=1)
         )
-        local = in_order(mine, flip(other, ("x",), sizes), is_first, 0)
-        weights.append(
-            (
-                lax.all_gather(local[:, : 2 * slim], "z", axis=0, tiled=True),
-                lax.all_gather(local[:, 2 * slim :], "z", axis=0, tiled=True),
-            )
-        )
-
-    inputs_all = spread(tokens, pack_links, core, sizes).astype(F32)
+        return pair
+
+    gain_rows = jnp.pad(
+        norm_gains.astype(BF16), ((0, 14), (0, attend_in.shape[1] - norm_gains.shape[1]))
+    )
+    in_z = lax.all_gather(
+        jnp.concatenate([attend_in.astype(BF16), gain_rows], axis=0), "z", axis=0, tiled=False
+    )
+    out_z = lax.all_gather(attend_out.T.astype(BF16), "z", axis=0, tiled=False)
+    tokens_moved = sends(tokens, pack_links)
+    away = split_feed(feed_in, feed_out, 1 - side, unit)
+    moved = [flip(part, ("x",), sizes) for part in away]
+    kept = split_feed(feed_in, feed_out, side, unit)
+    (in_z, cotangent_then), tokens_moved, moved = lax.optimization_barrier(
+        ((in_z, cotangent), tokens_moved, moved)
+    )
+
+    locals_ = [in_order(part, other, is_first, 0) for part, other in zip(kept, moved)]
+    weights = [lax.all_gather(part, "z", axis=0, tiled=True) for part in locals_[:3]]
+    weights.append(gather_depth(locals_[3], sizes).reshape(width, -1))
+    in_x = flip(in_z, ("x",), sizes)
+    back_moved = sends(cotangent_then, pack_links)
+    tokens_all = over_core([tokens] + tokens_moved)
+    in_x, out_z, back_moved, tokens_all = lax.optimization_barrier(
+        (in_x, out_z, back_moved, tokens_all)
+    )
+
+    out_x = flip(out_z, ("x",), sizes)
+    in_both = both_sides(in_z, in_x)
+    full_in = in_both[:, :, :depth].reshape(width, attend_in.shape[1])
+    gains = (
+        in_both[:, :, depth : depth + 2, : norm_gains.shape[1]]
+        .astype(F32)
+        .transpose(2, 0, 1, 3)
+        .reshape(2, width)
+    )
+    inputs_all = tokens_all.astype(F32)
     normed_one = (inputs_all * norm_rate(inputs_all) * gains[0]).astype(BF16)
     joined = product(normed_one, full_in, 1, 0)
     attended, qkv, logs = attend_forward(meta, joined, cosine, sine, docs, devices)
-    branch_one = collect(product(attended, full_out, 1, 1).astype(BF16), pack_links, core, sizes)
+    back_near = jnp.concatenate([cotangent] + back_moved, axis=0)
+    attended, out_x, left, right = lax.optimization_barrier(
+        (attended, out_x, back_near[:, : width // 2], back_near[:, width // 2 :])
+    )
+
+    full_out = both_sides(out_z, out_x).reshape(width, attend_out.shape[0])
+    near = product(attended[half:], full_out, 1, 1).astype(BF16)
+    mine = product(attended[:half], full_out, 1, 1).astype(BF16)
+    own, moved = collect(mine, near, pack_links, core, sizes)
+    left = flip(left, ("x",), sizes)
+    own, moved, left, right = lax.optimization_barrier((own, moved, left, right))
+
     inputs = tokens.astype(F32)
-    hidden_state = inputs + branch_one
+    hidden_state = inputs + added(own, moved)
     rate_two = norm_rate(hidden_state)
     normed_two = (hidden_state * rate_two * gains[1]).astype(BF16)
-    gathered_two = spread(normed_two, feed_links, core, sizes)
-    gathered_back = spread(cotangent, feed_links, core, sizes)
-
-    feed_in_parts, feed_out_parts = [], []
-    forward_total, backward_total = 0.0, 0.0
-    for c in range(CHUNKS):
-        weight_in, weight_out = weights[c]
-        gate_up = product(gathered_two, weight_in, 1, 0)
-        grad_activated = product(gathered_back, weight_out, 1, 0)
-        gate, upward = gate_up[:, :slim], gate_up[:, slim:]
-        chance = jax.nn.sigmoid(gate)
-        silu = gate * chance
-        activated = (silu * upward).astype(BF16)
-        grad_gate = grad_activated * upward * (chance * (1.0 + gate * (1.0 - chance)))
-        grad_upward = grad_activated * silu
-        grad_gate_up = jnp.concatenate([grad_gate.astype(BF16), grad_upward.astype(BF16)], axis=1)
-        feed_out_parts.append(
-            lax.psum_scatter(
-                (product(gathered_back, activated, 0, 0) * inverse_total).astype(BF16),
-                "z",
-                scatter_dimension=0,
-                tiled=True,
-            )
+    normed_moved = sends(normed_two, feed_links)
+    right = flip(right, ("x",), sizes)
+    normed_moved, left, right = lax.optimization_barrier((normed_moved, left, right))
+    gathered_two = over_core([normed_two] + normed_moved)
+    gathered_back = over_core([back_near, jnp.concatenate([left, right], axis=1)])
+
+    def gradients(grad, activated):
+        return weight_gradients(
+            gathered_two, grad, gathered_back, activated, sizes["z"], inverse_total
         )
-        feed_in_parts.append(
-            lax.psum_scatter(
-                (product(gathered_two, grad_gate_up, 0, 0) * inverse_total).astype(BF16),
-                "z",
-                scatter_dimension=0,
-                tiled=True,
-            )
-        )
-        backward_total = backward_total + product(grad_gate_up, weight_in, 1, 1)
-        forward_total = forward_total + product(activated, weight_out, 1, 1)
-    grad_normed_two = collect(backward_total.astype(BF16), feed_links, core, sizes)
-    branch_two = collect(forward_total.astype(BF16), feed_links, core, sizes)
-    block_out = (hidden_state + branch_two).astype(BF16)
-
-    grad_from_two, gain_two_grad = norm_back(hidden_state, rate_two, gains[1], grad_normed_two)
+
+    def summed(parts):
+        return lax.psum_scatter(parts, "z", scatter_dimension=0, tiled=False)
+
+    activated_a, grad_a = feed_both_ways(gathered_two, gathered_back, weights[:2])
+    activated_a, grad_a, weights[2] = lax.optimization_barrier((activated_a, grad_a, weights[2]))
+    parts_a = gradients(grad_a, activated_a)
+    parts_a, weights[3] = lax.optimization_barrier((parts_a, weights[3]))
+    sums_a = summed(parts_a)
+    activated_b, grad_b = feed_both_ways(gathered_two, gathered_back, weights[2:])
+    pairs = [(grad_a, weights[:2]), (grad_b, weights[2:])]
+    near = flip(back_products(pairs, 0, 2, 1), (core,), sizes)
+    mine = back_products(pairs, 0, 2, 0)
+    blocks = add_blocks(mine, near, 2 ** len(feed_links))
+    blocks, grad_b, activated_a, activated_b = lax.optimization_barrier(
+        (blocks, grad_b, activated_a, activated_b)
+    )
+    moved = [flip(block, c, sizes) for block, c in zip(blocks[1:], combos(feed_links)[1:])]
+    parts_b = gradients(grad_b, activated_b)
+    sums_b = summed(parts_b)
+    pairs = [(activated_a, weights[:2]), (activated_b, weights[2:])]
+    forward_near = back_products(pairs, 2, 3, 1)
+    forward_mine = back_products(pairs, 2, 3, 0)
+    moved, forward_near, forward_mine, parts_b = lax.optimization_barrier(
+        (moved, forward_near, forward_mine, parts_b)
+    )
+
+    grad_from_two, gain_two_grad = norm_back(
+        hidden_state, rate_two, gains[1], added(blocks[0], moved)
+    )
     grad_hidden = cotangent.astype(F32) + grad_from_two
-    gathered_grad = spread(grad_hidden.astype(BF16), pack_links, core, sizes)
+    grad_branch = grad_hidden.astype(BF16)
+    grad_moved = sends(grad_branch, pack_links)
+    forward_blocks = add_blocks(
+        forward_mine, flip(forward_near, (core,), sizes), 2 ** len(feed_links)
+    )
+    grad_moved, forward_blocks = lax.optimization_barrier((grad_moved, forward_blocks))
+    gathered_grad = over_core([grad_branch] + grad_moved)
     grad_attended = product(gathered_grad, full_out, 1, 0).astype(BF16)
-    grad_joined = attend_backward(meta, qkv, logs, grad_attended, cosine, sine, docs, devices)
-    grad_normed_one = collect(
-        product(grad_joined, full_in, 1, 1).astype(BF16), pack_links, core, sizes
-    )
-    grad_from_one, gain_one_grad = norm_back(inputs, norm_rate(inputs), gains[0], grad_normed_one)
-    tokens_grad = (grad_hidden + grad_from_one).astype(BF16)
-
-    def sum_documents(grad):
+    forward_moved = [
+        flip(block, c, sizes) for block, c in zip(forward_blocks[1:], combos(feed_links)[1:])
+    ]
+    groups = attend_in.shape[1] // ((GROUP + 2) * HD)
+    grad_joined = [
+        attend_backward(meta, qkv, logs, grad_attended, cosine, sine, docs, devices, group)
+        for group in range(groups)
+    ]
+
+    def split_sides(grad):
         split = (grad * inverse_total).astype(BF16).reshape(sizes["z"], 2, -1, grad.shape[1])
         mine = lax.dynamic_index_in_dim(split, side, 1, keepdims=False)
         other = lax.dynamic_index_in_dim(split, 1 - side, 1, keepdims=False)
-        both = (mine.astype(F32) + flip(other, ("x",), sizes).astype(F32)).astype(BF16)
-        return lax.psum_scatter(both, "z", scatter_dimension=0, tiled=False).astype(F32)
-
-    attend_out_shard = sum_documents(product(gathered_grad, attended, 0, 0)).T
-    attend_in_shard = sum_documents(product(normed_one, grad_joined, 0, 0))
-
-    def regroup(part):
-        mine, other = halves(part, 0)
-        return in_order(mine[:, None], flip(other, ("x",), sizes)[:, None], is_first, 1)
-
-    pieces_in = [
-        regroup(part).reshape(-1, 2, 2, slim) for part in feed_in_parts
+        return mine, flip(other, ("x",), sizes)
+
+    out_mine, out_other = split_sides(product(gathered_grad, attended, 0, 0))
+    grad_joined[-1], forward_moved, out_other = lax.optimization_barrier(
+        (grad_joined[-1], forward_moved, out_other)
+    )
+    block_out = (hidden_state + added(forward_blocks[0], forward_moved)).astype(BF16)
+    attend_out_shard = sum_depth(added(out_mine, [out_other]).astype(BF16)).T
+    in_parts = [
+        added(mine, [other]).astype(BF16)
+        for mine, other in (split_sides(product(normed_one, grad, 0, 0)) for grad in grad_joined)
     ]
-    feed_in_shard = (
-        jnp.stack(pieces_in, axis=3)
-        .transpose(2, 0, 1, 3, 4)
-        .reshape(feed_in.shape)
-        .astype(F32)
-    )
-    pieces_out = [regroup(part) for part in feed_out_parts]
-    feed_out_shard = (
-        jnp.stack(pieces_out, axis=2).reshape(feed_out.shape[1], feed_out.shape[0]).T.astype(F32)
-    )
+    attend_in_shard = sum_depth(jnp.concatenate(in_parts, axis=2))
+    joined_back = jnp.concatenate(grad_joined, axis=1)
+    own, moved = collect(
+        product(joined_back[:half], full_in, 1, 1).astype(BF16),
+        product(joined_back[half:], full_in, 1, 1).astype(BF16),
+        pack_links,
+        core,
+        sizes,
+    )
+    grad_normed_one = added(own, moved)
+    grad_from_one, gain_one_grad = norm_back(inputs, norm_rate(inputs), gains[0], grad_normed_one)
+    tokens_grad = (grad_hidden + grad_from_one).astype(BF16)
+
+    def regroup(sums):
+        mine, other = halves(sums, 0)
+        return jnp.stack([mine, flip(other, ("x",), sizes)])
+
+    pieces = jnp.stack([regroup(sums_a), regroup(sums_b)], axis=1)
+
+    def squares(shard):
+        shard = shard.astype(F32)
+        return jnp.sum(shard * shard)
 
     matrix_squares = (
-        jnp.sum(attend_in_shard * attend_in_shard)
-        + jnp.sum(attend_out_shard * attend_out_shard)
-        + jnp.sum(feed_in_shard * feed_in_shard)
-        + jnp.sum(feed_out_shard * feed_out_shard)
-    )
-    gain_partial = jnp.stack([gain_one_grad, gain_two_grad]) * inverse_total
-    total_squares, gain_grads = lax.psum(
-        (matrix_squares, gain_partial), ("z", "x") + tuple(tensor)
-    )
-    grad_norm = jnp.sqrt(total_squares + jnp.sum(gain_grads * gain_grads))
+        squares(attend_in_shard)
+        + squares(attend_out_shard)
+        + squares(pieces)
+    )
+    total = sum_everywhere(
+        jnp.concatenate(
+            [
+                gain_one_grad * inverse_total,
+                gain_two_grad * inverse_total,
+                jnp.full((LANES,), matrix_squares),
+            ]
+        ),
+        tensor,
+        sizes,
+    )
+    gain_grads = total[: 2 * width].reshape(2, width)
+    grad_norm = jnp.sqrt(total[2 * width] + jnp.sum(gain_grads * gain_grads))
     clip = jnp.minimum(1.0, CLIP_LIMIT / (grad_norm + 1e-06))
     gain_width = norm_gains.shape[1]
     gain_shard = lax.dynamic_slice_in_dim(
         gain_grads, lax.axis_index(("z", "x")) * gain_width, gain_width, 1
     )
-    first = adam(attend_in, attend_in_shard, moment_attend_in, square_attend_in, clip, MATRIX_RATE, MATRIX_DECAY)
-    second = adam(attend_out, attend_out_shard, moment_attend_out, square_attend_out, clip, OUTPUT_RATE, MATRIX_DECAY)
-    third = adam(feed_in, feed_in_shard, moment_feed_in, square_feed_in, clip, MATRIX_RATE, MATRIX_DECAY)
-    fourth = adam(feed_out, feed_out_shard, moment_feed_out, square_feed_out, clip, MATRIX_RATE, MATRIX_DECAY)
+    first = update(attend_in, attend_in_shard, moment_attend_in, square_attend_in, clip, MATRIX_RATE, MATRIX_DECAY)
+    second = update(attend_out, attend_out_shard, moment_attend_out, square_attend_out, clip, OUTPUT_RATE, MATRIX_DECAY)
+    tall = depth // 2
+    third = update_pieces(
+        adam_rows_kernel, feed_in, pieces, moment_feed_in, square_feed_in, clip, side,
+        (2, tall, feed_in.shape[2]), lambda i: (0, i, 0),
+        (2, 2, tall, 2 * slim), lambda i, s: (0, 0, i, 0),
+        MATRIX_RATE, MATRIX_DECAY,
+    )
+    fourth = update_pieces(
+        adam_columns_kernel, feed_out, pieces, moment_feed_out, square_feed_out, clip, side,
+        (slim, depth), lambda i: (i, 0),
+        (1, 1, depth, slim), lambda i, s: ((i // 2) ^ s, i % 2, 0, 2),
+        MATRIX_RATE, MATRIX_DECAY,
+    )
     fifth = adam(norm_gains, gain_shard, moment_gains, square_gains, clip, GAIN_RATE, 0.0)
     return (block_out, tokens_grad, grad_norm, *first, *second, *third, *fourth, *fifth)
 

time: 866 us -> 749 us (0.86)
  Pallas kernels: 36.3 us -> 202 us
  matrix products: 184 us -> 29.7 us
  local copies, waits for them, and re-layouts: 103 us -> 39.9 us
  blocking collectives: 58.8 us -> 0 us
  other arithmetic: 115 us -> 72.7 us
  starting transfers between devices: 33.5 us -> 55 us
  waiting for transfers between devices: 308 us -> 324 us
    pallas_call x1 -> x20, Pallas kernels: 22.8 us -> 188 us  [the longest x4 54.2 us: back_products(): pl.pallas_call(functools.partial(back_kernel, first, last, [len(right) fo...]
    dot_general x18 -> x9, matrix products: 184 us -> 29.7 us  [product(): lax.dot_general(left, right, (((left_dim,), (right_dim,)), ((), ())), pre...]
    all_gather x6 -> x5, waiting for transfers between devices: 0.07 us -> 99.6 us  [the longest x3 78.5 us: shards(): lax.all_gather(part, 'z', axis=0, tiled=True)]
    ppermute x34 -> x38, waiting for transfers between devices: 307 us -> 215 us  [flip(): return lax.ppermute(value, tuple(axes), pairs)]
    psum x1 -> x0, blocking collectives: 38 us -> none  [shards(): lax.psum((matrix_squares, gain_partial), ('z', 'x') + tuple(tensor))]
    slice x15 -> x4, local copies, waits for them, and re-layouts: 24.7 us -> 2.25 us  [the longest x1 1.52 us: shards(): back_near[:, width // 2:]]
    all_gather x1 -> x0, blocking collectives: 20.8 us -> none  [shards(): lax.all_gather(norm_gains.astype(BF16), ('z', 'x'), axis=1, tiled=True)]
    sub x5 -> x1, other arithmetic: 18.7 us -> 0.62 us  [adam(): weight - rate * (direction + decay * weight)]
  transfers between devices with their start and end apart: 46 -> 50, of which waited for: 16 -> 29; matrix products, arithmetic and copies ran while one was open for 39% -> 16% of each run, Pallas kernels for 4% -> 24%
where the time goes in v2:
time: 749 us; the launch traced here: 744 us
  waiting for transfers between devices  324 us (43%)
  Pallas kernels  202 us (27%)
  other arithmetic  72.7 us (10%)
  starting transfers between devices  55 us (7%)
  local copies, waits for them, and re-layouts  39.9 us (5%)
  matrix products  29.7 us (4%)
  between operations  20 us (3%)
    ppermute x38, waiting for transfers between devices, flip(): return lax.ppermute(value, tuple(axes), pairs)  215 us
    all_gather x3, waiting for transfers between devices, shards(): lax.all_gather(part, 'z', axis=0, tiled=True)  78.5 us
    pallas_call x4, Pallas kernels, back_products(): pl.pallas_call(functools.partial(back_kernel, first, last, [len(right) fo...  54.2 us
    pallas_call x2, Pallas kernels, weight_gradients(): pl.pallas_call(functools.partial(weights_kernel, scale), grid=(parts,), i...  37.2 us
    ppermute x38, starting transfers between devices, flip(): return lax.ppermute(value, tuple(axes), pairs)  37.1 us
    pallas_call x2, Pallas kernels, feed_both_ways(): pl.pallas_call(feed_kernel, grid=(count // tall,), in_specs=[pl.BlockSpec...  36.6 us
    dot_general x9, matrix products, product(): lax.dot_general(left, right, (((left_dim,), (right_dim,)), ((), ())), pre...  29.7 us
    pallas_call x2, Pallas kernels, attend_backward(): pl.pallas_call(functools.partial(backward_kernel, docs, devices), grid=(1...  23.2 us
  transfers between devices with their start and end apart: 50, of which 29 were waited for; matrix products, arithmetic and copies ran while one was open for 16% of the time, Pallas kernels for 24%

profile of v2, /device:TPU:0, one launch (start us, length us, event | category | flops | bytes accessed | tf_op | source)
XLA Modules:
  0.0 743.7 jit_solution(734357722015178687)
XLA Ops:
  36.9 8.4 %collective-permute-done.3 = bf16[256,768]{1,0:T(8,128)(2,1)S(1)} collective-permute-done((bf16[256,768]{1,0:T(8,128)(2,1)}, bf16[256,768]{1,0:T(8,128)(2,1)S(1)}, u32[]{:S(2)}, u32[]{:S(2)}) %collective-permute-start.3) | collective-permute-done | bytes 393248 | tf_op jit(solution)/shard_map/ppermute | solution.py:39
  64.5 21.1 %all-gather.16.cloned.1.call-done = bf16[1024,512]{0,1:T(8,128)(2,1)} async-done(((bf16[256,512]{0,1:T(8,128)(2,1)}), bf16[1024,512]{0,1:T(8,128)(2,1)}) %all-gather.16.cloned.1.call-update) | async-done | bytes 1048592 | tf_op jit(solution)/shard_map/all_gather | solution.py:701
  111.0 13.9 %attend_forward.1 = (bf16[1024,512]{1,0:T(8,128)(2,1)S(1)}, bf16[1024,768]{1,0:T(8,128)(2,1)S(1)}, f32[2,8,1024]{2,1,0:T(8,128)S(1)}) custom-call(s32[3]{0:T(128)S(1)} %pad_add_fusion.meta_ref, f32[1024,768]{1,0:T(8,128)S(1)} %fusion.36.joined_ref, f32[1024,128]{1,0:T(8,128)S(1)} %get-tuple-element.225.cos_ref, f32[1024,128]{1,0:T(8,128)S(1)} %get-tuple-element.226.sin_ref), custom_call_target="tpu_custom_call" | custom-call | flops 4294967296 | bytes 6291456 | tf_op jit(solution)/shard_map/attend_forward/pallas_call | solution.py:275
  138.9 19.4 %collective-permute-done.11 = bf16[512,1024]{1,0:T(8,128)(2,1)} collective-permute-done((bf16[512,1024]{1,0:T(8,128)(2,1)}, bf16[512,1024]{1,0:T(8,128)(2,1)}, u32[]{:S(2)}, u32[]{:S(2)}) %collective-permute-start.11) | collective-permute-done | bytes 1048608 | tf_op jit(solution)/shard_map/ppermute | solution.py:39
  171.6 20.1 %collective-permute-done.12 = bf16[256,2048]{1,0:T(8,128)(2,1)S(1)} collective-permute-done((bf16[256,2048]{1,0:T(8,128)(2,1)S(1)}, bf16[256,2048]{1,0:T(8,128)(2,1)S(1)}, u32[]{:S(2)}, u32[]{:S(2)}) %collective-permute-start.12) | collective-permute-done | bytes 1048608 | tf_op jit(solution)/shard_map/ppermute | solution.py:39
  193.2 23.5 %collective-permute-done.14 = bf16[256,2048]{1,0:T(8,128)(2,1)S(1)} collective-permute-done((bf16[256,2048]{1,0:T(8,128)(2,1)S(1)}, bf16[256,2048]{1,0:T(8,128)(2,1)S(1)}, u32[]{:S(2)}, u32[]{:S(2)}) %collective-permute-start.14) | collective-permute-done | bytes 1048608 | tf_op jit(solution)/shard_map/ppermute | solution.py:39
  216.6 19.6 %collective-permute-done.15 = bf16[512,1024]{1,0:T(8,128)(2,1)S(1)} collective-permute-done((bf16[512,1024]{1,0:T(8,128)(2,1)S(1)}, bf16[512,1024]{1,0:T(8,128)(2,1)S(1)}, u32[]{:S(2)}, u32[]{:S(2)}) %collective-permute-start.15) | collective-permute-done | bytes 1048608 | tf_op jit(solution)/shard_map/ppermute | solution.py:39
  271.3 18.2 %feed_both_ways.2 = (bf16[2048,512]{1,0:T(8,128)(2,1)S(1)}, bf16[2048,1024]{1,0:T(8,128)(2,1)}) custom-call(bf16[2048,2048]{1,0:T(8,128)(2,1)} %constant_dynamic-update-slice_fusion.2.rows_ref, bf16[2048,2048]{1,0:T(8,128)(2,1)} %pad_maximum_fusion.back_ref, bf16[2048,768]{1,0:T(8,128)(2,1)S(1)} %copy-done.1, ...), custom_call_target="tpu_custom_call" | custom-call | flops 12884901888 | bytes 29360128 | tf_op jit(solution)/shard_map/feed_both_ways/pallas_call | solution.py:526
  289.5 78.5 %all-gather.12.cloned.1.call-done.refs_0_.refs_4_ = bf16[2048,768]{1,0:T(8,128)(2,1)} async-done(((bf16[512,768]{1,0:T(8,128)(2,1)}), bf16[2048,768]{1,0:T(8,128)(2,1)}) %all-gather.12.cloned.1.call-update) | async-done | bytes 3145744 | tf_op jit(solution)/shard_map/all_gather | solution.py:711
  368.0 18.5 %weight_gradients.2 = bf16[4,512,1536]{2,1,0:T(8,128)(2,1)} custom-call(bf16[2048,2048]{1,0:T(8,128)(2,1)} %constant_dynamic-update-slice_fusion.2.rows_ref, bf16[2048,1024]{1,0:T(8,128)(2,1)} %get-tuple-element.143.grad_ref.refs_0_, bf16[2048,2048]{1,0:T(8,128)(2,1)} %pad_maximum_fusion.back_ref, bf16[2048,512]{1,0:T(8,128)(2,1)S(1)} %get-tuple-element.159.activated_ref.refs_0_), custom_call_target="tpu_custom_call" | custom-call | flops 12884901888 | bytes 29360128 | tf_op jit(solution)/shard_map/weight_gradients/pallas_call | solution.py:561
  388.4 18.4 %feed_both_ways.3 = (bf16[2048,512]{1,0:T(8,128)(2,1)S(1)}, bf16[2048,1024]{1,0:T(8,128)(2,1)}) custom-call(bf16[2048,2048]{1,0:T(8,128)(2,1)} %constant_dynamic-update-slice_fusion.2.rows_ref, bf16[2048,2048]{1,0:T(8,128)(2,1)} %pad_maximum_fusion.back_ref, bf16[2048,768]{1,0:T(8,128)(2,1)S(1)} %copy-done.2, bf16[2048,768]{1,0:T(8,128)(2,1)} %bitcast.18.refs_1_.refs_5_), custom_call_target="tpu_custom_call" | custom-call | flops 12884901888 | bytes 29360128 | tf_op jit(solution)/shard_map/feed_both_ways/pallas_call | solution.py:526
  408.1 15.8 %back_products.5 = bf16[1024,2048]{1,0:T(8,128)(2,1)} custom-call(bf16[2048,1024]{1,0:T(8,128)(2,1)} %get-tuple-element.143.grad_ref.refs_0_, bf16[2048,768]{1,0:T(8,128)(2,1)} %all-gather.8.cloned.1.call-done.refs_0_.refs_1_, bf16[2048,768]{1,0:T(8,128)(2,1)} %all-gather.10.cloned.1.call-done.refs_1_.refs_2_, ...), custom_call_target="tpu_custom_call" | custom-call | flops 8589934592 | bytes 16777216 | tf_op jit(solution)/shard_map/back_products/pallas_call | solution.py:609
  424.0 15.7 %back_products.4.mine_ref = bf16[1024,2048]{1,0:T(8,128)(2,1)} custom-call(bf16[2048,1024]{1,0:T(8,128)(2,1)} %get-tuple-element.143.grad_ref.refs_0_, bf16[2048,768]{1,0:T(8,128)(2,1)} %all-gather.8.cloned.1.call-done.refs_0_.refs_1_, bf16[2048,768]{1,0:T(8,128)(2,1)} %all-gather.10.cloned.1.call-done.refs_1_.refs_2_, ...), custom_call_target="tpu_custom_call" | custom-call | flops 8589934592 | bytes 16777216 | tf_op jit(solution)/shard_map/back_products/pallas_call | solution.py:609
  447.4 11.3 %back_products.7.mine_ref = bf16[1024,2048]{1,0:T(8,128)(2,1)} custom-call(bf16[2048,512]{1,0:T(8,128)(2,1)} %copy-done.3, bf16[2048,768]{1,0:T(8,128)(2,1)} %all-gather.8.cloned.1.call-done.refs_0_.refs_1_, bf16[2048,768]{1,0:T(8,128)(2,1)} %all-gather.10.cloned.1.call-done.refs_1_.refs_2_, bf16[2048,512]{1,0:T(8,128)(2,1)} %copy-done.4, ...), custom_call_target="tpu_custom_call" | custom-call | flops 4294967296 | bytes 10485760 | tf_op jit(solution)/shard_map/back_products/pallas_call | solution.py:609
  458.8 11.3 %back_products.6 = bf16[1024,2048]{1,0:T(8,128)(2,1)} custom-call(bf16[2048,512]{1,0:T(8,128)(2,1)} %copy-done.3, bf16[2048,768]{1,0:T(8,128)(2,1)} %all-gather.8.cloned.1.call-done.refs_0_.refs_1_, bf16[2048,768]{1,0:T(8,128)(2,1)} %all-gather.10.cloned.1.call-done.refs_1_.refs_2_, bf16[2048,512]{1,0:T(8,128)(2,1)} %copy-done.4, ...), custom_call_target="tpu_custom_call" | custom-call | flops 4294967296 | bytes 10485760 | tf_op jit(solution)/shard_map/back_products/pallas_call | solution.py:609
  470.1 18.7 %weight_gradients.3 = bf16[4,512,1536]{2,1,0:T(8,128)(2,1)} custom-call(bf16[2048,2048]{1,0:T(8,128)(2,1)} %constant_dynamic-update-slice_fusion.2.rows_ref, bf16[2048,1024]{1,0:T(8,128)(2,1)} %get-tuple-element.161.refs_3_.grad_ref, bf16[2048,2048]{1,0:T(8,128)(2,1)} %pad_maximum_fusion.back_ref, bf16[2048,512]{1,0:T(8,128)(2,1)S(1)} %copy-done.5), custom_call_target="tpu_custom_call" | custom-call | flops 12884901888 | bytes 29360128 | tf_op jit(solution)/shard_map/weight_gradients/pallas_call | solution.py:561
  508.6 18.3 %collective-permute-done.22 = bf16[256,2048]{1,0:T(8,128)(2,1)S(1)} collective-permute-done((bf16[256,2048]{1,0:T(8,128)(2,1)S(1)}, bf16[256,2048]{1,0:T(8,128)(2,1)S(1)}, u32[]{:S(2)}, u32[]{:S(2)}) %collective-permute-start.22) | collective-permute-done | bytes 1048608 | tf_op jit(solution)/shard_map/ppermute | solution.py:39
  543.9 11.6 %attend_backward.3 = bf16[1024,384]{1,0:T(8,128)(2,1)S(1)} custom-call(s32[3]{0:T(128)S(1)} %pad_add_fusion.meta_ref, bf16[1024,768]{1,0:T(8,128)(2,1)S(1)} %copy-done.20, f32[2,8,1024]{2,1,0:T(8,128)S(1)} %get-tuple-element.173.log_ref, bf16[1024,512]{1,0:T(8,128)(2,1)S(1)} %fusion.15.back_ref, f32[1024,128]{1,0:T(8,128)S(1)} %copy-done.10, ...), custom_call_target="tpu_custom_call" | custom-call | flops 5368709120 | bytes 3145728 | tf_op jit(solution)/shard_map/attend_backward/pallas_call | solution.py:312
  561.0 11.6 %attend_backward.2 = bf16[1024,384]{1,0:T(8,128)(2,1)S(1)} custom-call(s32[3]{0:T(128)S(1)} %pad_add_fusion.meta_ref, bf16[1024,768]{1,0:T(8,128)(2,1)S(1)} %copy-done.20, f32[2,8,1024]{2,1,0:T(8,128)S(1)} %get-tuple-element.173.log_ref, bf16[1024,512]{1,0:T(8,128)(2,1)S(1)} %fusion.15.back_ref, f32[1024,128]{1,0:T(8,128)S(1)} %copy-done.10, ...), custom_call_target="tpu_custom_call" | custom-call | flops 5368709120 | bytes 3145728 | tf_op jit(solution)/shard_map/attend_backward/pallas_call | solution.py:312
  578.6 22.6 %collective-permute-done.28 = bf16[4,256,512]{2,1,0:T(8,128)(2,1)S(1)} collective-permute-done((bf16[4,256,512]{2,1,0:T(8,128)(2,1)S(1)}, bf16[4,256,512]{2,1,0:T(8,128)(2,1)S(1)}, u32[]{:S(2)}, u32[]{:S(2)}) %collective-permute-start.28) | collective-permute-done | bytes 1048608 | tf_op jit(solution)/shard_map/ppermute | solution.py:39
  619.5 14.6 %collective-permute-done.32 = bf16[4,256,384]{2,1,0:T(8,128)(2,1)S(1)} collective-permute-done((bf16[4,256,384]{2,1,0:T(8,128)(2,1)S(1)}, bf16[4,256,384]{2,1,0:T(8,128)(2,1)S(1)}, u32[]{:S(2)}, u32[]{:S(2)}) %collective-permute-start.32) | collective-permute-done | bytes 786464 | tf_op jit(solution)/shard_map/ppermute | solution.py:39
  649.7 11.0 %collective-permute-done.33 = bf16[256,1536]{1,0:T(8,128)(2,1)S(1)} collective-permute-done((bf16[256,1536]{1,0:T(8,128)(2,1)S(1)}, bf16[256,1536]{1,0:T(8,128)(2,1)S(1)}, u32[]{:S(2)}, u32[]{:S(2)}) %collective-permute-start.33) | collective-permute-done | bytes 786464 | tf_op jit(solution)/shard_map/ppermute | solution.py:39
  668.5 8.5 %all-to-all-done.1 = bf16[4,256,768]{2,1,0:T(8,128)(2,1)} async-done(((bf16[4,256,768]{2,1,0:T(8,128)(2,1)}), bf16[4,256,768]{2,1,0:T(8,128)(2,1)}, u32[]{:S(2)}, u32[]{:S(2)}) %all-to-all-start.1) | async-done | bytes 1572896 | tf_op jit(solution)/shard_map/all_to_all | solution.py:90
  719.3 9.6 %update_pieces.2 = (f32[2,256,2048]{2,1,0:T(8,128)}, f32[2,256,2048]{2,1,0:T(8,128)}, f32[2,256,2048]{2,1,0:T(8,128)}) custom-call(s32[1]{0:T(128)} %bitcast.17.side_ref, f32[1]{0:T(128)} %bitcast.36.clip_ref, f32[2,256,2048]{2,1,0:T(8,128)} %weight_ref.6, bf16[2,2,256,1536]{3,2,1,0:T(8,128)(2,1)} %pad_maximum_fusion.5.grad_ref, f32[2,256,2048]{2,1,0:T(8,128)} %moment_ref.6, ...), custom_call_target="tpu_custom_call" | custom-call | flops 16777216 | bytes 27262976 | tf_op jit(solution)/shard_map/update_pieces/pallas_call | solution.py:461
  (348 shorter events, 283.3 us)
Async XLA Ops:
  7.2 45.3 %all-gather.14.cloned.1.call-start = ((), (), s32[]{:S(2)}) async-start(), calls=%async_computation.10 | async-start | bytes 2088960 | tf_op jit(solution)/shard_map/all_gather | solution.py:698
  10.0 75.7 %all-gather.16.cloned.1.call-start = ((), (), s32[]{:S(2)}) async-start(), calls=%async_computation.11 | async-start | bytes 1310720 | tf_op jit(solution)/shard_map/all_gather | solution.py:701
  10.1 42.4 %collective-permute-start = (bf16[256,2048]{1,0:T(8,128)(2,1)S(1)}, bf16[256,2048]{1,0:T(8,128)(2,1)S(1)}, u32[]{:S(2)}, u32[]{:S(2)}) collective-permute-start(bf16[256,2048]{1,0:T(8,128)(2,1)S(1)} %copy-done.23), channel_id=1, source_target_pairs={{0,2},{2,0},{1,3},{3,1},{4,6},{6,4},{5,7},{7,5},{8,10},{10,8},{9,1... | collective-permute-start | bytes 3145736 | tf_op jit(solution)/shard_map/ppermute | solution.py:39
  54.1 36.5 %collective-permute-start.7 = (bf16[512,2048]{1,0:T(8,128)(2,1)}, bf16[512,2048]{1,0:T(8,128)(2,1)}, u32[]{:S(2)}, u32[]{:S(2)}) collective-permute-start(bf16[512,2048]{1,0:T(8,128)(2,1)} %pad_maximum_fusion.6), channel_id=1, source_target_pairs={{0,1},{1,0},{2,3},{3,2},{4,5},{5,4},{6,7},{7,6},{8,9},{9,8},{10,11... | collective-permute-start | bytes 6291464 | tf_op jit(solution)/shard_map/ppermute | solution.py:39
  54.9 214.5 %all-gather.10.cloned.1.call-start = ((), (), s32[]{:S(2)}) async-start(), calls=%async_computation.6 | async-start | bytes 3932160 | tf_op jit(solution)/shard_map/all_gather | solution.py:711
  58.3 39.2 %collective-permute-start.5 = (bf16[4,272,768]{2,1,0:T(8,128)(2,1)}, bf16[4,272,768]{2,1,0:T(8,128)(2,1)}, u32[]{:S(2)}, u32[]{:S(2)}) collective-permute-start(bf16[4,272,768]{2,1,0:T(8,128)(2,1)} %bitcast.77), channel_id=1, source_target_pairs={{0,4},{4,0},{1,5},{5,1},{2,6},{6,2},{3,7},{7,3},{8,12},{12,8},{9,1... | collective-permute-start | bytes 5013512 | tf_op jit(solution)/shard_map/ppermute | solution.py:39
  60.0 32.9 %collective-permute-start.6 = (bf16[256,2048]{1,0:T(8,128)(2,1)S(1)}, bf16[256,2048]{1,0:T(8,128)(2,1)}, u32[]{:S(2)}, u32[]{:S(2)}) collective-permute-start(bf16[256,2048]{1,0:T(8,128)(2,1)S(1)} %copy-done.27), channel_id=1, source_target_pairs={{0,2},{2,0},{1,3},{3,1},{4,6},{6,4},{5,7},{7,5},{8,10},{10,8},{9,1... | collective-permute-start | bytes 3145736 | tf_op jit(solution)/shard_map/ppermute | solution.py:39
  90.4 179.0 %all-gather.8.cloned.1.call-start = ((), (), s32[]{:S(2)}) async-start(), calls=%async_computation.5 | async-start | bytes 3932160 | tf_op jit(solution)/shard_map/all_gather | solution.py:711
  138.8 229.2 %all-gather.12.cloned.1.call-start = ((), (), s32[]{:S(2)}) async-start(), calls=%async_computation.7 | async-start | bytes 3932160 | tf_op jit(solution)/shard_map/all_gather | solution.py:711
  168.6 48.0 %collective-permute-start.14 = (bf16[256,2048]{1,0:T(8,128)(2,1)S(1)}, bf16[256,2048]{1,0:T(8,128)(2,1)S(1)}, u32[]{:S(2)}, u32[]{:S(2)}) collective-permute-start(bf16[256,2048]{1,0:T(8,128)(2,1)S(1)} %get-tuple-element.208), channel_id=1, source_target_pairs={{0,6},{2,4},{4,2},{6,0},{1,7},{3,5},{5,3},{7,1},{8,14},{10,12},{12... | collective-permute-start | bytes 3145736 | tf_op jit(solution)/shard_map/ppermute | solution.py:39
  170.1 66.1 %collective-permute-start.15 = (bf16[512,1024]{1,0:T(8,128)(2,1)S(1)}, bf16[512,1024]{1,0:T(8,128)(2,1)S(1)}, u32[]{:S(2)}, u32[]{:S(2)}) collective-permute-start(bf16[512,1024]{1,0:T(8,128)(2,1)S(1)} %copy-done.61), channel_id=1, source_target_pairs={{0,4},{4,0},{1,5},{5,1},{2,6},{6,2},{3,7},{7,3},{8,12},{12,8},{9,1... | collective-permute-start | bytes 3145736 | tf_op jit(solution)/shard_map/ppermute | solution.py:39
  248.6 137.9 %all-to-all-start = ((bf16[4,512,768]{2,1,0:T(8,128)(2,1)}), bf16[4,512,768]{2,1,0:T(8,128)(2,1)}, u32[]{:S(2)}, u32[]{:S(2)}) async-start(bf16[4,512,768]{2,1,0:T(8,128)(2,1)} %broadcast_in_dim.7), calls=%async_computation | async-start | bytes 6291456 | tf_op jit(solution)/shard_map/all_to_all | solution.py:86
  253.5 386.7 %reduce-scatter.3.cloned.1.call-start = ((), (), s32[]{:S(2)}) async-start(), calls=%async_computation.8 | async-start | bytes 7864320 | tf_op jit(solution)/shard_map/reduce_scatter | solution.py:761
  386.5 277.0 %reduce-scatter.5.cloned.1.call-start = ((), (), s32[]{:S(2)}) async-start(), calls=%async_computation.9 | async-start | bytes 7864320 | tf_op jit(solution)/shard_map/reduce_scatter | solution.py:761
  443.9 44.9 %collective-permute-start.19 = (bf16[256,2048]{1,0:T(8,128)(2,1)}, bf16[256,2048]{1,0:T(8,128)(2,1)}, u32[]{:S(2)}, u32[]{:S(2)}) collective-permute-start(bf16[256,2048]{1,0:T(8,128)(2,1)} %get-tuple-element.156), channel_id=1, source_target_pairs={{0,2},{2,0},{1,3},{3,1},{4,6},{6,4},{5,7},{7,5},{8,10},{10,8},{9,1... | collective-permute-start | bytes 3145736 | tf_op jit(solution)/shard_map/ppermute | solution.py:39
  445.5 43.3 %collective-permute-start.20 = (bf16[256,2048]{1,0:T(8,128)(2,1)S(1)}, bf16[256,2048]{1,0:T(8,128)(2,1)}, u32[]{:S(2)}, u32[]{:S(2)}) collective-permute-start(bf16[256,2048]{1,0:T(8,128)(2,1)S(1)} %get-tuple-element.157), channel_id=1, source_target_pairs={{0,4},{4,0},{1,5},{5,1},{2,6},{6,2},{3,7},{7,3},{8,12},{12,8},{9,1... | collective-permute-start | bytes 3145736 | tf_op jit(solution)/shard_map/ppermute | solution.py:39
  447.0 46.2 %collective-permute-start.21 = (bf16[256,2048]{1,0:T(8,128)(2,1)S(1)}, bf16[256,2048]{1,0:T(8,128)(2,1)}, u32[]{:S(2)}, u32[]{:S(2)}) collective-permute-start(bf16[256,2048]{1,0:T(8,128)(2,1)S(1)} %get-tuple-element.158), channel_id=1, source_target_pairs={{0,6},{2,4},{4,2},{6,0},{1,7},{3,5},{5,3},{7,1},{8,14},{10,12},{12... | collective-permute-start | bytes 3145736 | tf_op jit(solution)/shard_map/ppermute | solution.py:39
  528.6 44.9 %collective-permute-start.25 = (bf16[256,2048]{1,0:T(8,128)(2,1)S(1)}, bf16[256,2048]{1,0:T(8,128)(2,1)S(1)}, u32[]{:S(2)}, u32[]{:S(2)}) collective-permute-start(bf16[256,2048]{1,0:T(8,128)(2,1)S(1)} %get-tuple-element.175), channel_id=1, source_target_pairs={{0,2},{2,0},{1,3},{3,1},{4,6},{6,4},{5,7},{7,5},{8,10},{10,8},{9,1... | collective-permute-start | bytes 3145736 | tf_op jit(solution)/shard_map/ppermute | solution.py:39
  530.2 43.3 %collective-permute-start.26 = (bf16[256,2048]{1,0:T(8,128)(2,1)S(1)}, bf16[256,2048]{1,0:T(8,128)(2,1)S(1)}, u32[]{:S(2)}, u32[]{:S(2)}) collective-permute-start(bf16[256,2048]{1,0:T(8,128)(2,1)S(1)} %get-tuple-element.176), channel_id=1, source_target_pairs={{0,4},{4,0},{1,5},{5,1},{2,6},{6,2},{3,7},{7,3},{8,12},{12,8},{9,1... | collective-permute-start | bytes 3145736 | tf_op jit(solution)/shard_map/ppermute | solution.py:39
  531.7 46.9 %collective-permute-start.27 = (bf16[256,2048]{1,0:T(8,128)(2,1)S(1)}, bf16[256,2048]{1,0:T(8,128)(2,1)S(1)}, u32[]{:S(2)}, u32[]{:S(2)}) collective-permute-start(bf16[256,2048]{1,0:T(8,128)(2,1)S(1)} %get-tuple-element.177), channel_id=1, source_target_pairs={{0,6},{2,4},{4,2},{6,0},{1,7},{3,5},{5,3},{7,1},{8,14},{10,12},{12... | collective-permute-start | bytes 3145736 | tf_op jit(solution)/shard_map/ppermute | solution.py:39
  538.4 62.8 %collective-permute-start.28 = (bf16[4,256,512]{2,1,0:T(8,128)(2,1)S(1)}, bf16[4,256,512]{2,1,0:T(8,128)(2,1)S(1)}, u32[]{:S(2)}, u32[]{:S(2)}) collective-permute-start(bf16[4,256,512]{2,1,0:T(8,128)(2,1)S(1)} %dynamic-slice_bitcast_fusion), channel_id=1, source_target_pairs={{0,4},{4,0},{1,5},{5,1},{2,6},{6,2},{3,7},{7,3},{8,12},{12,8},{9,1... | collective-permute-start | bytes 3145736 | tf_op jit(solution)/shard_map/ppermute | solution.py:39
  559.7 58.5 %collective-permute-start.31 = (bf16[4,256,384]{2,1,0:T(8,128)(2,1)}, bf16[4,256,384]{2,1,0:T(8,128)(2,1)}, u32[]{:S(2)}, u32[]{:S(2)}) collective-permute-start(bf16[4,256,384]{2,1,0:T(8,128)(2,1)} %dynamic-slice_bitcast_fusion.4), channel_id=1, source_target_pairs={{0,4},{4,0},{1,5},{5,1},{2,6},{6,2},{3,7},{7,3},{8,12},{12,8},{9,1... | collective-permute-start | bytes 2359304 | tf_op jit(solution)/shard_map/ppermute | solution.py:39
  602.4 33.1 %all-to-all-start.2 = ((bf16[4,256,512]{2,1,0:T(8,128)(2,1)}), bf16[4,256,512]{2,1,0:T(8,128)(2,1)}, u32[]{:S(2)}, u32[]{:S(2)}) async-start(bf16[4,256,512]{2,1,0:T(8,128)(2,1)} %fusion.10), calls=%async_computation.2 | async-start | bytes 2097152 | tf_op jit(solution)/shard_map/all_to_all | solution.py:90
  635.6 41.4 %all-to-all-start.1 = ((bf16[4,256,768]{2,1,0:T(8,128)(2,1)}), bf16[4,256,768]{2,1,0:T(8,128)(2,1)}, u32[]{:S(2)}, u32[]{:S(2)}) async-start(bf16[4,256,768]{2,1,0:T(8,128)(2,1)} %pad_maximum_fusion.10), calls=%async_computation.1 | async-start | bytes 3145728 | tf_op jit(solution)/shard_map/all_to_all | solution.py:90
  (103 other events, 1228.6 us)
Sparse Core Ops, SparseCore 0:
  10.2 41.3 all-gather.13
  55.0 30.6 all-gather.15
  90.5 61.8 all-gather.9
  154.3 62.1 all-gather.7
  245.2 122.7 all-gather.11
  386.7 110.1 reduce-scatter.2
  499.2 111.6 reduce-scatter.4

commit v3 on v2

--- a/solution.py
+++ b/solution.py
@@ -470,18 +470,20 @@
     )(side.reshape(1).astype(jnp.int32), clip.reshape(1), weight, pieces, moment, square)
 
 
-def split_kernel(side_ref, in_ref, out_ref, *unit_refs):
-    unit = unit_refs[0].shape[1] // 3
-    for n, ref in enumerate(unit_refs):
-        cut = slice(n * unit, (n + 1) * unit)
-        ref[:, :unit] = in_ref[0, :, cut].astype(BF16)
-        ref[:, unit : 2 * unit] = in_ref[1, :, cut].astype(BF16)
-        ref[:, 2 * unit :] = out_ref[cut, :].T.astype(BF16)
+def split_kernel(unit, side_ref, in_ref, out_ref, *part_refs):
+    slim = part_refs[0].shape[1] // 3
+    for part, ref in enumerate(part_refs):
+        for n in range(slim // unit):
+            cut = slice(part * slim + n * unit, part * slim + (n + 1) * unit)
+            for j in range(2):
+                first = (2 * n + j) * unit
+                ref[:, first : first + unit] = in_ref[j, :, cut].astype(BF16)
+        ref[:, 2 * slim :] = out_ref[part * slim : (part + 1) * slim, :].T.astype(BF16)
 
 
 def split_feed(feed_in, feed_out, side, unit):
     depth, hidden = feed_in.shape[1], feed_in.shape[2] // 2
-    part = jax.ShapeDtypeStruct((depth, 3 * unit), BF16)
+    part = jax.ShapeDtypeStruct((depth, 3 * hidden // 2), BF16)
     grid_spec = pltpu.PrefetchScalarGridSpec(
         num_scalar_prefetch=1,
         grid=(1,),
@@ -489,12 +491,12 @@
             pl.BlockSpec((2, depth, hidden), lambda i, s: (0, 0, s[0])),
             pl.BlockSpec((hidden, depth), lambda i, s: (s[0], 0)),
         ],
-        out_specs=[pl.BlockSpec(part.shape, lambda i, s: (0, 0))] * (hidden // unit),
+        out_specs=[pl.BlockSpec(part.shape, lambda i, s: (0, 0))] * 2,
     )
     return pl.pallas_call(
-        split_kernel,
+        functools.partial(split_kernel, unit),
         grid_spec=grid_spec,
-        out_shape=[part] * (hidden // unit),
+        out_shape=[part] * 2,
         compiler_params=pltpu.CompilerParams(vmem_limit_bytes=60 * 2**20),
         cost_estimate=pl.CostEstimate(
             flops=depth * hidden * 3, bytes_accessed=depth * hidden * 18, transcendentals=0
@@ -503,12 +505,17 @@
     )(side.reshape(1).astype(jnp.int32), feed_in, feed_out)
 
 
-def feed_kernel(rows_ref, back_ref, *refs):
-    *weight_refs, activated_ref, grad_ref = refs
-    for n, weight_ref in enumerate(weight_refs):
-        unit = weight_ref.shape[1] // 3
-        both = jnp.dot(rows_ref[...], weight_ref[:, : 2 * unit], preferred_element_type=F32)
-        back = jnp.dot(back_ref[...], weight_ref[:, 2 * unit :], preferred_element_type=F32)
+def feed_kernel(unit, rows_ref, back_ref, weight_ref, activated_ref, grad_ref):
+    units = activated_ref.shape[1] // unit
+    for n in range(units):
+        first = 2 * n * unit
+        both = jnp.dot(
+            rows_ref[...], weight_ref[:, first : first + 2 * unit], preferred_element_type=F32
+        )
+        first = (2 * units + n) * unit
+        back = jnp.dot(
+            back_ref[...], weight_ref[:, first : first + unit], preferred_element_type=F32
+        )
         gate, upward = both[:, :unit], both[:, unit:]
         chance = jax.nn.sigmoid(gate)
         silu = gate * chance
@@ -519,18 +526,18 @@
         grad_ref[:, (2 * n + 1) * unit : 2 * (n + 1) * unit] = (back * silu).astype(BF16)
 
 
-def feed_both_ways(rows, back, weights):
+def feed_both_ways(rows, back, weight, unit):
     count, width = rows.shape
-    slim = sum(w.shape[1] // 3 for w in weights)
+    slim = weight.shape[1] // 3
     tall = min(count, 512)
     return pl.pallas_call(
-        feed_kernel,
+        functools.partial(feed_kernel, unit),
         grid=(count // tall,),
         in_specs=[
             pl.BlockSpec((tall, width), lambda i: (i, 0)),
             pl.BlockSpec((tall, width), lambda i: (i, 0)),
-        ]
-        + [pl.BlockSpec(w.shape, lambda i: (0, 0)) for w in weights],
+            pl.BlockSpec(weight.shape, lambda i: (0, 0)),
+        ],
         out_specs=[
             pl.BlockSpec((tall, slim), lambda i: (i, 0)),
             pl.BlockSpec((tall, 2 * slim), lambda i: (i, 0)),
@@ -546,7 +553,7 @@
             transcendentals=count * slim,
         ),
         name="feed_both_ways",
-    )(rows, back, *weights)
+    )(rows, back, weight)
 
 
 def weights_kernel(scale, rows_ref, grad_ref, back_ref, activated_ref, out_ref):
@@ -579,35 +586,26 @@
     )(rows, grad, back, activated)
 
 
-def back_kernel(first, last, counts, *refs):
-    total, refs = 0.0, list(refs)
-    for count in counts:
-        left = refs.pop(0)
-        for n in range(count):
-            right = refs.pop(0)
-            unit = right.shape[1] // 3
-            wide = (last - first) * unit
-            total = total + product(
-                left[:, n * wide : (n + 1) * wide],
-                right[:, first * unit : last * unit],
-                1,
-                1,
-            )
-    refs[0][...] = total.astype(BF16)
+def back_kernel(*refs):
+    total = 0.0
+    for left, right in zip(refs[:-1:2], refs[1:-1:2]):
+        total = total + product(left[...], right[...], 1, 1)
+    refs[-1][...] = total.astype(BF16)
 
 
 def back_products(pairs, first, last, half):
-    count, width = pairs[0][0].shape[0] // 2, pairs[0][1][0].shape[0]
+    count, width = pairs[0][0].shape[0] // 2, pairs[0][1].shape[0]
     tall = min(count, 512)
-    skip = half * (count // tall)
+    skip, place = half * (count // tall), first // (last - first)
     specs, operands = [], []
     for left, right in pairs:
-        specs.append(pl.BlockSpec((tall, left.shape[1]), lambda i: (i + skip, 0)))
-        specs += [pl.BlockSpec(w.shape, lambda i: (0, 0)) for w in right]
-        operands += [left, *right]
+        depth = left.shape[1]
+        specs.append(pl.BlockSpec((tall, depth), lambda i: (i + skip, 0)))
+        specs.append(pl.BlockSpec((width, depth), lambda i: (0, place)))
+        operands += [left, right]
     depth = sum(left.shape[1] for left, _ in pairs)
     return pl.pallas_call(
-        functools.partial(back_kernel, first, last, [len(right) for _, right in pairs]),
+        back_kernel,
         grid=(count // tall,),
         in_specs=specs,
         out_specs=pl.BlockSpec((tall, width), lambda i: (i, 0)),
@@ -698,24 +696,21 @@
     in_z = lax.all_gather(
         jnp.concatenate([attend_in.astype(BF16), gain_rows], axis=0), "z", axis=0, tiled=False
     )
-    out_z = lax.all_gather(attend_out.T.astype(BF16), "z", axis=0, tiled=False)
+    out_z = gather_depth(attend_out.T.astype(BF16), sizes)
     tokens_moved = sends(tokens, pack_links)
     away = split_feed(feed_in, feed_out, 1 - side, unit)
     moved = [flip(part, ("x",), sizes) for part in away]
     kept = split_feed(feed_in, feed_out, side, unit)
-    (in_z, cotangent_then), tokens_moved, moved = lax.optimization_barrier(
-        ((in_z, cotangent), tokens_moved, moved)
-    )
-
     locals_ = [in_order(part, other, is_first, 0) for part, other in zip(kept, moved)]
-    weights = [lax.all_gather(part, "z", axis=0, tiled=True) for part in locals_[:3]]
-    weights.append(gather_depth(locals_[3], sizes).reshape(width, -1))
+    in_z, out_z, cotangent_then, tokens_moved, locals_ = lax.optimization_barrier(
+        (in_z, out_z, cotangent, tokens_moved, locals_)
+    )
+
+    weight_a, weight_b = [lax.all_gather(part, "z", axis=0, tiled=True) for part in locals_]
     in_x = flip(in_z, ("x",), sizes)
     back_moved = sends(cotangent_then, pack_links)
     tokens_all = over_core([tokens] + tokens_moved)
-    in_x, out_z, back_moved, tokens_all = lax.optimization_barrier(
-        (in_x, out_z, back_moved, tokens_all)
-    )
+    in_x, back_moved, tokens_all = lax.optimization_barrier((in_x, back_moved, tokens_all))
 
     out_x = flip(out_z, ("x",), sizes)
     in_both = both_sides(in_z, in_x)
@@ -740,6 +735,7 @@
     mine = product(attended[:half], full_out, 1, 1).astype(BF16)
     own, moved = collect(mine, near, pack_links, core, sizes)
     left = flip(left, ("x",), sizes)
+    right = flip(right, ("x",), sizes)
     own, moved, left, right = lax.optimization_barrier((own, moved, left, right))
 
     inputs = tokens.astype(F32)
@@ -747,10 +743,9 @@
     rate_two = norm_rate(hidden_state)
     normed_two = (hidden_state * rate_two * gains[1]).astype(BF16)
     normed_moved = sends(normed_two, feed_links)
-    right = flip(right, ("x",), sizes)
-    normed_moved, left, right = lax.optimization_barrier((normed_moved, left, right))
+    gathered_back = over_core([back_near, jnp.concatenate([left, right], axis=1)])
+    normed_moved, gathered_back = lax.optimization_barrier((normed_moved, gathered_back))
     gathered_two = over_core([normed_two] + normed_moved)
-    gathered_back = over_core([back_near, jnp.concatenate([left, right], axis=1)])
 
     def gradients(grad, activated):
         return weight_gradients(
@@ -760,13 +755,12 @@
     def summed(parts):
         return lax.psum_scatter(parts, "z", scatter_dimension=0, tiled=False)
 
-    activated_a, grad_a = feed_both_ways(gathered_two, gathered_back, weights[:2])
-    activated_a, grad_a, weights[2] = lax.optimization_barrier((activated_a, grad_a, weights[2]))
+    activated_a, grad_a = feed_both_ways(gathered_two, gathered_back, weight_a, unit)
     parts_a = gradients(grad_a, activated_a)
-    parts_a, weights[3] = lax.optimization_barrier((parts_a, weights[3]))
+    parts_a, weight_b = lax.optimization_barrier((parts_a, weight_b))
     sums_a = summed(parts_a)
-    activated_b, grad_b = feed_both_ways(gathered_two, gathered_back, weights[2:])
-    pairs = [(grad_a, weights[:2]), (grad_b, weights[2:])]
+    activated_b, grad_b = feed_both_ways(gathered_two, gathered_back, weight_b, unit)
+    pairs = [(grad_a, weight_a), (grad_b, weight_b)]
     near = flip(back_products(pairs, 0, 2, 1), (core,), sizes)
     mine = back_products(pairs, 0, 2, 0)
     blocks = add_blocks(mine, near, 2 ** len(feed_links))
@@ -774,30 +768,34 @@
         (blocks, grad_b, activated_a, activated_b)
     )
     moved = [flip(block, c, sizes) for block, c in zip(blocks[1:], combos(feed_links)[1:])]
+    pairs = [(activated_a, weight_a), (activated_b, weight_b)]
+    forward_near = flip(back_products(pairs, 2, 3, 1), (core,), sizes)
+    forward_mine = back_products(pairs, 2, 3, 0)
+    forward_blocks = add_blocks(forward_mine, forward_near, 2 ** len(feed_links))
     parts_b = gradients(grad_b, activated_b)
     sums_b = summed(parts_b)
-    pairs = [(activated_a, weights[:2]), (activated_b, weights[2:])]
-    forward_near = back_products(pairs, 2, 3, 1)
-    forward_mine = back_products(pairs, 2, 3, 0)
-    moved, forward_near, forward_mine, parts_b = lax.optimization_barrier(
-        (moved, forward_near, forward_mine, parts_b)
-    )
+    moved, forward_blocks, parts_b = lax.optimization_barrier((moved, forward_blocks, parts_b))
 
     grad_from_two, gain_two_grad = norm_back(
         hidden_state, rate_two, gains[1], added(blocks[0], moved)
     )
     grad_hidden = cotangent.astype(F32) + grad_from_two
     grad_branch = grad_hidden.astype(BF16)
+    forward_links = combos(feed_links)[1:]
+    forward_moved = {("x",): flip(forward_blocks[forward_links.index(("x",)) + 1], ("x",), sizes)}
+
+    def regroup(sums):
+        mine, other = halves(sums, 0)
+        return jnp.stack([mine, flip(other, ("x",), sizes)])
+
+    sums_a, grad_branch = lax.optimization_barrier((sums_a, grad_branch))
     grad_moved = sends(grad_branch, pack_links)
-    forward_blocks = add_blocks(
-        forward_mine, flip(forward_near, (core,), sizes), 2 ** len(feed_links)
-    )
-    grad_moved, forward_blocks = lax.optimization_barrier((grad_moved, forward_blocks))
+    pieces_a = regroup(sums_a)
+    grad_moved, forward_moved, pieces_a = lax.optimization_barrier(
+        (grad_moved, forward_moved, pieces_a)
+    )
     gathered_grad = over_core([grad_branch] + grad_moved)
     grad_attended = product(gathered_grad, full_out, 1, 0).astype(BF16)
-    forward_moved = [
-        flip(block, c, sizes) for block, c in zip(forward_blocks[1:], combos(feed_links)[1:])
-    ]
     groups = attend_in.shape[1] // ((GROUP + 2) * HD)
     grad_joined = [
         attend_backward(meta, qkv, logs, grad_attended, cosine, sine, docs, devices, group)
@@ -811,15 +809,18 @@
         return mine, flip(other, ("x",), sizes)
 
     out_mine, out_other = split_sides(product(gathered_grad, attended, 0, 0))
-    grad_joined[-1], forward_moved, out_other = lax.optimization_barrier(
-        (grad_joined[-1], forward_moved, out_other)
-    )
-    block_out = (hidden_state + added(forward_blocks[0], forward_moved)).astype(BF16)
+    grad_joined[-1], out_other = lax.optimization_barrier((grad_joined[-1], out_other))
     attend_out_shard = sum_depth(added(out_mine, [out_other]).astype(BF16)).T
-    in_parts = [
-        added(mine, [other]).astype(BF16)
-        for mine, other in (split_sides(product(normed_one, grad, 0, 0)) for grad in grad_joined)
-    ]
+    in_pairs = [split_sides(product(normed_one, grad, 0, 0)) for grad in grad_joined]
+    forward_moved |= {
+        c: flip(block, c, sizes)
+        for block, c in zip(forward_blocks[1:], forward_links)
+        if c != ("x",)
+    }
+    in_pairs, forward_moved = lax.optimization_barrier((in_pairs, forward_moved))
+    block_out = added(forward_blocks[0], list(forward_moved.values()))
+    block_out = (hidden_state + block_out).astype(BF16)
+    in_parts = [added(mine, [other]).astype(BF16) for mine, other in in_pairs]
     attend_in_shard = sum_depth(jnp.concatenate(in_parts, axis=2))
     joined_back = jnp.concatenate(grad_joined, axis=1)
     own, moved = collect(
@@ -833,11 +834,7 @@
     grad_from_one, gain_one_grad = norm_back(inputs, norm_rate(inputs), gains[0], grad_normed_one)
     tokens_grad = (grad_hidden + grad_from_one).astype(BF16)
 
-    def regroup(sums):
-        mine, other = halves(sums, 0)
-        return jnp.stack([mine, flip(other, ("x",), sizes)])
-
-    pieces = jnp.stack([regroup(sums_a), regroup(sums_b)], axis=1)
+    pieces = jnp.stack([pieces_a, regroup(sums_b)], axis=1)
 
     def squares(shard):
         shard = shard.astype(F32)

time: 749 us -> 673 us (0.90)
  waiting for transfers between devices: 324 us -> 265 us
  local copies, waits for them, and re-layouts: 39.9 us -> 31.6 us
    all_gather x3 -> x2, waiting for transfers between devices: 78.5 us -> 12.9 us  [shards(): lax.all_gather(part, 'z', axis=0, tiled=True)]
    all_gather x1 -> x0, waiting for transfers between devices: 21.1 us -> none  [shards(): out_z = lax.all_gather(attend_out.T.astype(BF16), 'z', axis=0, tiled=False)]
    ppermute x38 -> x36, waiting for transfers between devices: 215 us -> 226 us  [flip(): return lax.ppermute(value, tuple(axes), pairs)]
    unnamed x159 -> x119, local copies, waits for them, and re-layouts: 21.7 us -> 16.7 us
    ppermute x38 -> x36, starting transfers between devices: 37.1 us -> 36.3 us  [flip(): return lax.ppermute(value, tuple(axes), pairs)]
  transfers between devices with their start and end apart: 50 -> 46, of which waited for: 29 -> 26; matrix products, arithmetic and copies ran while one was open for 16% -> 17% of each run, Pallas kernels for 24% -> 26%
where the time goes in v3:
time: 673 us; the launch traced here: 667 us
  waiting for transfers between devices  265 us (39%)
  Pallas kernels  198 us (29%)
  other arithmetic  76.6 us (11%)
  starting transfers between devices  52 us (8%)
  local copies, waits for them, and re-layouts  31.6 us (5%)
  matrix products  24.2 us (4%)
  between operations  19.6 us (3%)
    ppermute x36, waiting for transfers between devices, flip(): return lax.ppermute(value, tuple(axes), pairs)  226 us
    pallas_call x4, Pallas kernels, back_products(): pl.pallas_call(back_kernel, grid=(count // tall,), in_specs=specs, out_sp...  46.6 us
    pallas_call x2, Pallas kernels, feed_both_ways(): pl.pallas_call(functools.partial(feed_kernel, unit), grid=(count // tall,...  38.3 us
    pallas_call x2, Pallas kernels, weight_gradients(): pl.pallas_call(functools.partial(weights_kernel, scale), grid=(parts,), i...  37.8 us
    ppermute x36, starting transfers between devices, flip(): return lax.ppermute(value, tuple(axes), pairs)  36.3 us
    dot_general x9, matrix products, product(): lax.dot_general(left, right, (((left_dim,), (right_dim,)), ((), ())), pre...  24.2 us
    pallas_call x2, Pallas kernels, attend_backward(): pl.pallas_call(functools.partial(backward_kernel, docs, devices), grid=(1...  23.2 us
    unnamed x119, local copies, waits for them, and re-layouts  16.7 us
  transfers between devices with their start and end apart: 46, of which 26 were waited for; matrix products, arithmetic and copies ran while one was open for 17% of the time, Pallas kernels for 26%

profile of v3, /device:TPU:0, one launch (start us, length us, event | category | flops | bytes accessed | tf_op | source)
XLA Modules:
  0.0 667.4 jit_solution(12513318025549800931)
XLA Ops:
  27.6 14.1 %collective-permute-done.1 = bf16[256,1536]{1,0:T(8,128)(2,1)} collective-permute-done((bf16[256,1536]{1,0:T(8,128)(2,1)}, bf16[256,1536]{1,0:T(8,128)(2,1)}, u32[]{:S(2)}, u32[]{:S(2)}) %collective-permute-start.1) | collective-permute-done | bytes 786464 | tf_op jit(solution)/shard_map/ppermute | solution.py:39
  45.1 11.7 %collective-permute-done.2 = bf16[256,1536]{1,0:T(8,128)(2,1)S(1)} collective-permute-done((bf16[256,1536]{1,0:T(8,128)(2,1)}, bf16[256,1536]{1,0:T(8,128)(2,1)S(1)}, u32[]{:S(2)}, u32[]{:S(2)}) %collective-permute-start.2) | collective-permute-done | bytes 786464 | tf_op jit(solution)/shard_map/ppermute | solution.py:39
  82.5 16.8 %collective-permute-done.4 = bf16[256,2048]{1,0:T(8,128)(2,1)} collective-permute-done((bf16[256,2048]{1,0:T(8,128)(2,1)S(1)}, bf16[256,2048]{1,0:T(8,128)(2,1)}, u32[]{:S(2)}, u32[]{:S(2)}) %collective-permute-start.4) | collective-permute-done | bytes 1048608 | tf_op jit(solution)/shard_map/ppermute | solution.py:39
  99.3 12.4 %collective-permute-done.3 = bf16[4,272,768]{2,1,0:T(8,128)(2,1)} collective-permute-done((bf16[4,272,768]{2,1,0:T(8,128)(2,1)}, bf16[4,272,768]{2,1,0:T(8,128)(2,1)}, u32[]{:S(2)}, u32[]{:S(2)}) %collective-permute-start.3) | collective-permute-done | bytes 1671200 | tf_op jit(solution)/shard_map/ppermute | solution.py:39
  123.9 13.9 %attend_forward.1 = (bf16[1024,512]{1,0:T(8,128)(2,1)S(1)}, bf16[1024,768]{1,0:T(8,128)(2,1)S(1)}, f32[2,8,1024]{2,1,0:T(8,128)S(1)}) custom-call(s32[3]{0:T(128)S(1)} %pad_add_fusion.meta_ref, f32[1024,768]{1,0:T(8,128)S(1)} %fusion.30.joined_ref, f32[1024,128]{1,0:T(8,128)S(1)} %get-tuple-element.221.cos_ref, f32[1024,128]{1,0:T(8,128)S(1)} %get-tuple-element.222.sin_ref), custom_call_target="tpu_custom_call" | custom-call | flops 4294967296 | bytes 6291456 | tf_op jit(solution)/shard_map/attend_forward/pallas_call | solution.py:275
  149.0 19.8 %collective-permute-done.9 = bf16[512,1024]{1,0:T(8,128)(2,1)S(1)} collective-permute-done((bf16[512,1024]{1,0:T(8,128)(2,1)S(1)}, bf16[512,1024]{1,0:T(8,128)(2,1)S(1)}, u32[]{:S(2)}, u32[]{:S(2)}) %collective-permute-start.9) | collective-permute-done | bytes 1048608 | tf_op jit(solution)/shard_map/ppermute | solution.py:39
  168.7 22.0 %collective-permute-done.10 = bf16[512,1024]{1,0:T(8,128)(2,1)S(1)} collective-permute-done((bf16[512,1024]{1,0:T(8,128)(2,1)S(1)}, bf16[512,1024]{1,0:T(8,128)(2,1)S(1)}, u32[]{:S(2)}, u32[]{:S(2)}) %collective-permute-start.10) | collective-permute-done | bytes 1048608 | tf_op jit(solution)/shard_map/ppermute | solution.py:39
  209.8 15.4 %collective-permute-done.11 = bf16[256,2048]{1,0:T(8,128)(2,1)S(1)} collective-permute-done((bf16[256,2048]{1,0:T(8,128)(2,1)S(1)}, bf16[256,2048]{1,0:T(8,128)(2,1)S(1)}, u32[]{:S(2)}, u32[]{:S(2)}) %collective-permute-start.11) | collective-permute-done | bytes 1048608 | tf_op jit(solution)/shard_map/ppermute | solution.py:39
  227.2 21.7 %collective-permute-done.13 = bf16[256,2048]{1,0:T(8,128)(2,1)S(1)} collective-permute-done((bf16[256,2048]{1,0:T(8,128)(2,1)S(1)}, bf16[256,2048]{1,0:T(8,128)(2,1)S(1)}, u32[]{:S(2)}, u32[]{:S(2)}) %collective-permute-start.13) | collective-permute-done | bytes 1048608 | tf_op jit(solution)/shard_map/ppermute | solution.py:39
  259.0 19.1 %feed_both_ways.2 = (bf16[2048,512]{1,0:T(8,128)(2,1)S(1)}, bf16[2048,1024]{1,0:T(8,128)(2,1)}) custom-call(bf16[2048,2048]{1,0:T(8,128)(2,1)} %constant_dynamic-update-slice_fusion.4.rows_ref, bf16[2048,2048]{1,0:T(8,128)(2,1)} %pad_maximum_fusion.back_ref, bf16[2048,1536]{1,0:T(8,128)(2,1)} %all-gather.5.cloned.1.call-done.weight_ref.refs_1_), custom_call_target="tpu_custom_call" | custom-call | flops 12884901888 | bytes 29360128 | tf_op jit(solution)/shard_map/feed_both_ways/pallas_call | solution.py:533
  278.1 19.3 %weight_gradients.2 = bf16[4,512,1536]{2,1,0:T(8,128)(2,1)} custom-call(bf16[2048,2048]{1,0:T(8,128)(2,1)} %constant_dynamic-update-slice_fusion.4.rows_ref, bf16[2048,1024]{1,0:T(8,128)(2,1)} %get-tuple-element.131.grad_ref.refs_0_, bf16[2048,2048]{1,0:T(8,128)(2,1)} %pad_maximum_fusion.back_ref, bf16[2048,512]{1,0:T(8,128)(2,1)S(1)} %get-tuple-element.144.activated_ref.refs_0_), custom_call_target="tpu_custom_call" | custom-call | flops 12884901888 | bytes 29360128 | tf_op jit(solution)/shard_map/weight_gradients/pallas_call | solution.py:568
  297.4 12.9 %all-gather.7.cloned.1.call-done.weight_ref.refs_3_ = bf16[2048,1536]{1,0:T(8,128)(2,1)} async-done(((bf16[512,1536]{1,0:T(8,128)(2,1)}), bf16[2048,1536]{1,0:T(8,128)(2,1)}) %all-gather.7.cloned.1.call-update) | async-done | bytes 6291472 | tf_op jit(solution)/shard_map/all_gather | solution.py:709
  310.4 19.2 %feed_both_ways.3 = (bf16[2048,512]{1,0:T(8,128)(2,1)S(1)}, bf16[2048,1024]{1,0:T(8,128)(2,1)}) custom-call(bf16[2048,2048]{1,0:T(8,128)(2,1)} %constant_dynamic-update-slice_fusion.4.rows_ref, bf16[2048,2048]{1,0:T(8,128)(2,1)} %pad_maximum_fusion.back_ref, bf16[2048,1536]{1,0:T(8,128)(2,1)} %all-gather.7.cloned.1.call-done.weight_ref.refs_3_), custom_call_target="tpu_custom_call" | custom-call | flops 12884901888 | bytes 29360128 | tf_op jit(solution)/shard_map/feed_both_ways/pallas_call | solution.py:533
  330.9 14.4 %back_products.5 = bf16[1024,2048]{1,0:T(8,128)(2,1)} custom-call(bf16[2048,1024]{1,0:T(8,128)(2,1)} %get-tuple-element.131.grad_ref.refs_0_, bf16[2048,1536]{1,0:T(8,128)(2,1)} %all-gather.5.cloned.1.call-done.weight_ref.refs_1_, bf16[2048,1024]{1,0:T(8,128)(2,1)} %get-tuple-element.150.refs_2_.grad_ref, ...), custom_call_target="tpu_custom_call" | custom-call | flops 8589934592 | bytes 16777216 | tf_op jit(solution)/shard_map/back_products/pallas_call | solution.py:607
  345.4 14.5 %back_products.4.mine_ref = bf16[1024,2048]{1,0:T(8,128)(2,1)} custom-call(bf16[2048,1024]{1,0:T(8,128)(2,1)} %get-tuple-element.131.grad_ref.refs_0_, bf16[2048,1536]{1,0:T(8,128)(2,1)} %all-gather.5.cloned.1.call-done.weight_ref.refs_1_, bf16[2048,1024]{1,0:T(8,128)(2,1)} %get-tuple-element.150.refs_2_.grad_ref, ...), custom_call_target="tpu_custom_call" | custom-call | flops 8589934592 | bytes 16777216 | tf_op jit(solution)/shard_map/back_products/pallas_call | solution.py:607
  377.7 18.5 %weight_gradients.3 = bf16[4,512,1536]{2,1,0:T(8,128)(2,1)} custom-call(bf16[2048,2048]{1,0:T(8,128)(2,1)} %constant_dynamic-update-slice_fusion.4.rows_ref, bf16[2048,1024]{1,0:T(8,128)(2,1)} %get-tuple-element.150.refs_2_.grad_ref, bf16[2048,2048]{1,0:T(8,128)(2,1)} %pad_maximum_fusion.back_ref, bf16[2048,512]{1,0:T(8,128)(2,1)S(1)} %copy-done.3), custom_call_target="tpu_custom_call" | custom-call | flops 12884901888 | bytes 29360128 | tf_op jit(solution)/shard_map/weight_gradients/pallas_call | solution.py:568
  412.2 11.1 %collective-permute-done.19 = bf16[256,2048]{1,0:T(8,128)(2,1)} collective-permute-done((bf16[256,2048]{1,0:T(8,128)(2,1)}, bf16[256,2048]{1,0:T(8,128)(2,1)}, u32[]{:S(2)}, u32[]{:S(2)}) %collective-permute-start.19) | collective-permute-done | bytes 1048608 | tf_op jit(solution)/shard_map/ppermute | solution.py:39
  436.9 16.8 %collective-permute-done.23 = bf16[256,1536]{1,0:T(8,128)(2,1)S(1)} collective-permute-done((bf16[256,1536]{1,0:T(8,128)(2,1)S(1)}, bf16[256,1536]{1,0:T(8,128)(2,1)S(1)}, u32[]{:S(2)}, u32[]{:S(2)}) %collective-permute-start.23) | collective-permute-done | bytes 786464 | tf_op jit(solution)/shard_map/ppermute | solution.py:39
  454.9 19.3 %collective-permute-done.22 = bf16[256,2048]{1,0:T(8,128)(2,1)S(1)} collective-permute-done((bf16[256,2048]{1,0:T(8,128)(2,1)S(1)}, bf16[256,2048]{1,0:T(8,128)(2,1)S(1)}, u32[]{:S(2)}, u32[]{:S(2)}) %collective-permute-start.22) | collective-permute-done | bytes 1048608 | tf_op jit(solution)/shard_map/ppermute | solution.py:39
  489.8 11.6 %attend_backward.2 = bf16[1024,384]{1,0:T(8,128)(2,1)S(1)} custom-call(s32[3]{0:T(128)S(1)} %pad_add_fusion.meta_ref, bf16[1024,768]{1,0:T(8,128)(2,1)S(1)} %copy-done.18, f32[2,8,1024]{2,1,0:T(8,128)S(1)} %get-tuple-element.153.log_ref, bf16[1024,512]{1,0:T(8,128)(2,1)S(1)} %convolution_convert_fusion.4.back_ref, f32[1024,128]{1,0:T(8,128)S(1)} %copy-done.8, ...), custom_call_target="tpu_custom_call" | custom-call | flops 5368709120 | bytes 3145728 | tf_op jit(solution)/shard_map/attend_backward/pallas_call | solution.py:312
  506.9 11.6 %attend_backward.3 = bf16[1024,384]{1,0:T(8,128)(2,1)S(1)} custom-call(s32[3]{0:T(128)S(1)} %pad_add_fusion.meta_ref, bf16[1024,768]{1,0:T(8,128)(2,1)S(1)} %copy-done.18, f32[2,8,1024]{2,1,0:T(8,128)S(1)} %get-tuple-element.153.log_ref, bf16[1024,512]{1,0:T(8,128)(2,1)S(1)} %convolution_convert_fusion.4.back_ref, f32[1024,128]{1,0:T(8,128)S(1)} %copy-done.8, ...), custom_call_target="tpu_custom_call" | custom-call | flops 5368709120 | bytes 3145728 | tf_op jit(solution)/shard_map/attend_backward/pallas_call | solution.py:312
  543.9 16.0 %collective-permute-done.27 = bf16[4,256,384]{2,1,0:T(8,128)(2,1)S(1)} collective-permute-done((bf16[4,256,384]{2,1,0:T(8,128)(2,1)S(1)}, bf16[4,256,384]{2,1,0:T(8,128)(2,1)S(1)}, u32[]{:S(2)}, u32[]{:S(2)}) %collective-permute-start.27) | collective-permute-done | bytes 786464 | tf_op jit(solution)/shard_map/ppermute | solution.py:39
  578.0 10.0 %collective-permute-done.32 = bf16[256,1536]{1,0:T(8,128)(2,1)S(1)} collective-permute-done((bf16[256,1536]{1,0:T(8,128)(2,1)S(1)}, bf16[256,1536]{1,0:T(8,128)(2,1)S(1)}, u32[]{:S(2)}, u32[]{:S(2)}) %collective-permute-start.32) | collective-permute-done | bytes 786464 | tf_op jit(solution)/shard_map/ppermute | solution.py:39
  639.6 9.6 %update_pieces.2 = (f32[2,256,2048]{2,1,0:T(8,128)}, f32[2,256,2048]{2,1,0:T(8,128)}, f32[2,256,2048]{2,1,0:T(8,128)}) custom-call(s32[1]{0:T(128)} %bitcast.5.side_ref, f32[1]{0:T(128)} %bitcast.35.clip_ref, f32[2,256,2048]{2,1,0:T(8,128)} %weight_ref.6, bf16[2,2,256,1536]{3,2,1,0:T(8,128)(2,1)} %pad_maximum_fusion.4.grad_ref, f32[2,256,2048]{2,1,0:T(8,128)} %moment_ref.6, ...), custom_call_target="tpu_custom_call" | custom-call | flops 16777216 | bytes 27262976 | tf_op jit(solution)/shard_map/update_pieces/pallas_call | solution.py:461
  (297 shorter events, 275.9 us)
Async XLA Ops:
  7.2 63.3 %all-gather.9.cloned.1.call-start = ((), (), s32[]{:S(2)}) async-start(), calls=%async_computation.9 | async-start | bytes 2088960 | tf_op jit(solution)/shard_map/all_gather | solution.py:696
  11.2 55.7 %all-to-all-start = ((bf16[4,256,512]{2,1,0:T(8,128)(2,1)}), bf16[4,256,512]{2,1,0:T(8,128)(2,1)}, u32[]{:S(2)}, u32[]{:S(2)}) async-start(bf16[4,256,512]{2,1,0:T(8,128)(2,1)} %broadcast_in_dim.7), calls=%async_computation | async-start | bytes 2097152 | tf_op jit(solution)/shard_map/all_to_all | solution.py:86
  17.5 241.4 %all-gather.5.cloned.1.call-start = ((), (), s32[]{:S(2)}) async-start(), calls=%async_computation.5 | async-start | bytes 7864320 | tf_op jit(solution)/shard_map/all_gather | solution.py:709
  22.3 34.6 %collective-permute-start.2 = (bf16[256,1536]{1,0:T(8,128)(2,1)}, bf16[256,1536]{1,0:T(8,128)(2,1)S(1)}, u32[]{:S(2)}, u32[]{:S(2)}) collective-permute-start(bf16[256,1536]{1,0:T(8,128)(2,1)} %get-tuple-element.107), channel_id=1, source_target_pairs={{0,4},{4,0},{1,5},{5,1},{2,6},{6,2},{3,7},{7,3},{8,12},{12,8},{9,1... | collective-permute-start | bytes 2359304 | tf_op jit(solution)/shard_map/ppermute | solution.py:39
  22.9 37.0 %collective-permute-start = (bf16[256,2048]{1,0:T(8,128)(2,1)S(1)}, bf16[256,2048]{1,0:T(8,128)(2,1)S(1)}, u32[]{:S(2)}, u32[]{:S(2)}) collective-permute-start(bf16[256,2048]{1,0:T(8,128)(2,1)S(1)} %copy-done.22), channel_id=1, source_target_pairs={{0,2},{2,0},{1,3},{3,1},{4,6},{6,4},{5,7},{7,5},{8,10},{10,8},{9,1... | collective-permute-start | bytes 3145736 | tf_op jit(solution)/shard_map/ppermute | solution.py:39
  72.1 39.6 %collective-permute-start.3 = (bf16[4,272,768]{2,1,0:T(8,128)(2,1)}, bf16[4,272,768]{2,1,0:T(8,128)(2,1)}, u32[]{:S(2)}, u32[]{:S(2)}) collective-permute-start(bf16[4,272,768]{2,1,0:T(8,128)(2,1)} %bitcast.3), channel_id=1, source_target_pairs={{0,4},{4,0},{1,5},{5,1},{2,6},{6,2},{3,7},{7,3},{8,12},{12,8},{9,1... | collective-permute-start | bytes 5013512 | tf_op jit(solution)/shard_map/ppermute | solution.py:39
  79.5 58.4 %collective-permute-start.6 = (bf16[4,256,512]{2,1,0:T(8,128)(2,1)}, bf16[4,256,512]{2,1,0:T(8,128)(2,1)}, u32[]{:S(2)}, u32[]{:S(2)}) collective-permute-start(bf16[4,256,512]{2,1,0:T(8,128)(2,1)} %all-to-all-done), channel_id=1, source_target_pairs={{0,4},{4,0},{1,5},{5,1},{2,6},{6,2},{3,7},{7,3},{8,12},{12,8},{9,1... | collective-permute-start | bytes 3145736 | tf_op jit(solution)/shard_map/ppermute | solution.py:39
  80.0 230.3 %all-gather.7.cloned.1.call-start = ((), (), s32[]{:S(2)}) async-start(), calls=%async_computation.6 | async-start | bytes 7864320 | tf_op jit(solution)/shard_map/all_gather | solution.py:709
  144.3 46.5 %collective-permute-start.10 = (bf16[512,1024]{1,0:T(8,128)(2,1)S(1)}, bf16[512,1024]{1,0:T(8,128)(2,1)S(1)}, u32[]{:S(2)}, u32[]{:S(2)}) collective-permute-start(bf16[512,1024]{1,0:T(8,128)(2,1)S(1)} %get-tuple-element.121), channel_id=1, source_target_pairs={{0,4},{4,0},{1,5},{5,1},{2,6},{6,2},{3,7},{7,3},{8,12},{12,8},{9,1... | collective-permute-start | bytes 3145736 | tf_op jit(solution)/shard_map/ppermute | solution.py:39
  147.4 43.4 %collective-permute-start.8 = (bf16[256,2048]{1,0:T(8,128)(2,1)S(1)}, bf16[256,2048]{1,0:T(8,128)(2,1)S(1)}, u32[]{:S(2)}, u32[]{:S(2)}) collective-permute-start(bf16[256,2048]{1,0:T(8,128)(2,1)S(1)} %get-tuple-element.119), channel_id=1, source_target_pairs={{0,2},{2,0},{1,3},{3,1},{4,6},{6,4},{5,7},{7,5},{8,10},{10,8},{9,1... | collective-permute-start | bytes 3145736 | tf_op jit(solution)/shard_map/ppermute | solution.py:39
  195.5 236.1 %reduce-scatter.3.cloned.1.call-start = ((), (), s32[]{:S(2)}) async-start(), calls=%async_computation.7 | async-start | bytes 7864320 | tf_op jit(solution)/shard_map/reduce_scatter | solution.py:756
  202.7 46.2 %collective-permute-start.13 = (bf16[256,2048]{1,0:T(8,128)(2,1)S(1)}, bf16[256,2048]{1,0:T(8,128)(2,1)S(1)}, u32[]{:S(2)}, u32[]{:S(2)}) collective-permute-start(bf16[256,2048]{1,0:T(8,128)(2,1)S(1)} %get-tuple-element.200), channel_id=1, source_target_pairs={{0,6},{2,4},{4,2},{6,0},{1,7},{3,5},{5,3},{7,1},{8,14},{10,12},{12... | collective-permute-start | bytes 3145736 | tf_op jit(solution)/shard_map/ppermute | solution.py:39
  310.3 257.1 %reduce-scatter.5.cloned.1.call-start = ((), (), s32[]{:S(2)}) async-start(), calls=%async_computation.8 | async-start | bytes 7864320 | tf_op jit(solution)/shard_map/reduce_scatter | solution.py:756
  374.2 38.0 %collective-permute-start.17 = (bf16[256,2048]{1,0:T(8,128)(2,1)}, bf16[256,2048]{1,0:T(8,128)(2,1)}, u32[]{:S(2)}, u32[]{:S(2)}) collective-permute-start(bf16[256,2048]{1,0:T(8,128)(2,1)} %get-tuple-element.141), channel_id=1, source_target_pairs={{0,2},{2,0},{1,3},{3,1},{4,6},{6,4},{5,7},{7,5},{8,10},{10,8},{9,1... | collective-permute-start | bytes 3145736 | tf_op jit(solution)/shard_map/ppermute | solution.py:39
  375.7 36.5 %collective-permute-start.18 = (bf16[256,2048]{1,0:T(8,128)(2,1)}, bf16[256,2048]{1,0:T(8,128)(2,1)}, u32[]{:S(2)}, u32[]{:S(2)}) collective-permute-start(bf16[256,2048]{1,0:T(8,128)(2,1)} %get-tuple-element.142), channel_id=1, source_target_pairs={{0,4},{4,0},{1,5},{5,1},{2,6},{6,2},{3,7},{7,3},{8,12},{12,8},{9,1... | collective-permute-start | bytes 3145736 | tf_op jit(solution)/shard_map/ppermute | solution.py:39
  377.2 46.2 %collective-permute-start.19 = (bf16[256,2048]{1,0:T(8,128)(2,1)}, bf16[256,2048]{1,0:T(8,128)(2,1)}, u32[]{:S(2)}, u32[]{:S(2)}) collective-permute-start(bf16[256,2048]{1,0:T(8,128)(2,1)} %get-tuple-element.143), channel_id=1, source_target_pairs={{0,6},{2,4},{4,2},{6,0},{1,7},{3,5},{5,3},{7,1},{8,14},{10,12},{12... | collective-permute-start | bytes 3145736 | tf_op jit(solution)/shard_map/ppermute | solution.py:39
  434.9 39.4 %collective-permute-start.22 = (bf16[256,2048]{1,0:T(8,128)(2,1)S(1)}, bf16[256,2048]{1,0:T(8,128)(2,1)S(1)}, u32[]{:S(2)}, u32[]{:S(2)}) collective-permute-start(bf16[256,2048]{1,0:T(8,128)(2,1)S(1)} %get-tuple-element.160), channel_id=1, source_target_pairs={{0,4},{4,0},{1,5},{5,1},{2,6},{6,2},{3,7},{7,3},{8,12},{12,8},{9,1... | collective-permute-start | bytes 3145736 | tf_op jit(solution)/shard_map/ppermute | solution.py:39
  435.2 40.0 %collective-permute-start.21 = (bf16[256,2048]{1,0:T(8,128)(2,1)S(1)}, bf16[256,2048]{1,0:T(8,128)(2,1)S(1)}, u32[]{:S(2)}, u32[]{:S(2)}) collective-permute-start(bf16[256,2048]{1,0:T(8,128)(2,1)S(1)} %copy-done.32), channel_id=1, source_target_pairs={{0,2},{2,0},{1,3},{3,1},{4,6},{6,4},{5,7},{7,5},{8,10},{10,8},{9,1... | collective-permute-start | bytes 3145736 | tf_op jit(solution)/shard_map/ppermute | solution.py:39
  476.9 65.9 %collective-permute-start.28 = (bf16[256,2048]{1,0:T(8,128)(2,1)}, bf16[256,2048]{1,0:T(8,128)(2,1)}, u32[]{:S(2)}, u32[]{:S(2)}) collective-permute-start(bf16[256,2048]{1,0:T(8,128)(2,1)} %get-tuple-element.164), channel_id=1, source_target_pairs={{0,2},{2,0},{1,3},{3,1},{4,6},{6,4},{5,7},{7,5},{8,10},{10,8},{9,1... | collective-permute-start | bytes 3145736 | tf_op jit(solution)/shard_map/ppermute | solution.py:39
  478.5 64.3 %collective-permute-start.29 = (bf16[256,2048]{1,0:T(8,128)(2,1)S(1)}, bf16[256,2048]{1,0:T(8,128)(2,1)}, u32[]{:S(2)}, u32[]{:S(2)}) collective-permute-start(bf16[256,2048]{1,0:T(8,128)(2,1)S(1)} %get-tuple-element.166), channel_id=1, source_target_pairs={{0,6},{2,4},{4,2},{6,0},{1,7},{3,5},{5,3},{7,1},{8,14},{10,12},{12... | collective-permute-start | bytes 3145736 | tf_op jit(solution)/shard_map/ppermute | solution.py:39
  485.8 41.2 %collective-permute-start.26 = (bf16[4,256,512]{2,1,0:T(8,128)(2,1)S(1)}, bf16[4,256,512]{2,1,0:T(8,128)(2,1)S(1)}, u32[]{:S(2)}, u32[]{:S(2)}) collective-permute-start(bf16[4,256,512]{2,1,0:T(8,128)(2,1)S(1)} %dynamic-slice_bitcast_fusion), channel_id=1, source_target_pairs={{0,4},{4,0},{1,5},{5,1},{2,6},{6,2},{3,7},{7,3},{8,12},{12,8},{9,1... | collective-permute-start | bytes 3145736 | tf_op jit(solution)/shard_map/ppermute | solution.py:39
  505.5 38.4 %collective-permute-start.25 = (bf16[4,256,384]{2,1,0:T(8,128)(2,1)}, bf16[4,256,384]{2,1,0:T(8,128)(2,1)}, u32[]{:S(2)}, u32[]{:S(2)}) collective-permute-start(bf16[4,256,384]{2,1,0:T(8,128)(2,1)} %get-tuple-element.209), channel_id=1, source_target_pairs={{0,4},{4,0},{1,5},{5,1},{2,6},{6,2},{3,7},{7,3},{8,12},{12,8},{9,1... | collective-permute-start | bytes 2359304 | tf_op jit(solution)/shard_map/ppermute | solution.py:39
  542.8 31.6 %collective-permute-start.30 = (bf16[512,2048]{1,0:T(8,128)(2,1)}, bf16[512,2048]{1,0:T(8,128)(2,1)S(1)}, u32[]{:S(2)}, u32[]{:S(2)}) collective-permute-start(bf16[512,2048]{1,0:T(8,128)(2,1)} %convolution_convert_fusion), channel_id=1, source_target_pairs={{0,1},{1,0},{2,3},{3,2},{4,5},{5,4},{6,7},{7,6},{8,9},{9,8},{10,11... | collective-permute-start | bytes 6291464 | tf_op jit(solution)/shard_map/ppermute | solution.py:39
  562.8 41.5 %all-to-all-start.1 = ((bf16[4,256,768]{2,1,0:T(8,128)(2,1)}), bf16[4,256,768]{2,1,0:T(8,128)(2,1)}, u32[]{:S(2)}, u32[]{:S(2)}) async-start(bf16[4,256,768]{2,1,0:T(8,128)(2,1)} %pad_maximum_fusion.8), calls=%async_computation.2 | async-start | bytes 3145728 | tf_op jit(solution)/shard_map/all_to_all | solution.py:90
  (78 other events, 840.3 us)
Sparse Core Ops, SparseCore 0:
  10.2 60.3 all-gather.8
  80.1 113.5 all-gather.4
  195.9 114.3 all-gather.6
  312.5 108.9 reduce-scatter.2
  423.6 111.2 reduce-scatter.4

commit v4 on v3

--- a/solution.py
+++ b/solution.py
@@ -64,9 +64,7 @@
         out_specs=[pl.BlockSpec((rows, width), lambda i: (0, 0))] * count,
         out_shape=[jax.ShapeDtypeStruct((rows, width), BF16)] * count,
         compiler_params=pltpu.CompilerParams(vmem_limit_bytes=32 * 2**20),
-        cost_estimate=pl.CostEstimate(
-            flops=mine.size, bytes_accessed=6 * mine.size, transcendentals=0
-        ),
+        cost_estimate=pl.CostEstimate(flops=1, bytes_accessed=1, transcendentals=0),
         name="add_blocks",
     )(mine, near)
 
@@ -86,19 +84,32 @@
     return lax.all_to_all(copies, "z", 0, 0, tiled=True)
 
 
-def sum_depth(blocks):
-    arrived = lax.all_to_all(blocks, "z", 0, 0, tiled=True)
-    return jnp.sum(arrived.astype(F32), axis=0).astype(BF16)
-
-
-def sum_everywhere(value, tensor, sizes):
+def to_owners(blocks):
+    return lax.all_to_all(blocks, "z", 0, 0, tiled=True)
+
+
+def sum_terms(terms):
+    return jnp.sum(terms.astype(F32), axis=0).astype(BF16)
+
+
+def sum_near(value, tensor, sizes):
     for a in tuple(reversed(tensor)) + ("x",):
         value = value + flip(value, (a,), sizes)
+    return value
+
+
+def sum_far(value, sizes):
     step, count = 1, sizes["z"]
     while step < count:
         value = value + lax.ppermute(value, "z", [(i, i ^ step) for i in range(count)])
         step *= 2
     return value
+
+
+def sum_scalar(value, axes, sizes):
+    count = math.prod(sizes[a] for a in axes)
+    terms = lax.all_to_all(jnp.full((count, LANES), value), axes, 0, 0, tiled=True)
+    return jnp.sum(terms[:, 0])
 
 
 def frequencies(head_size):
@@ -296,11 +307,7 @@
             pltpu.VMEM((2, LANES, rows), BF16),
         ],
         compiler_params=pltpu.CompilerParams(vmem_limit_bytes=32 * 2**20),
-        cost_estimate=pl.CostEstimate(
-            flops=groups * GROUP * rows * rows * LANES * 4,
-            bytes_accessed=rows * width * 8,
-            transcendentals=groups * GROUP * rows * rows // 2,
-        ),
+        cost_estimate=pl.CostEstimate(flops=1, bytes_accessed=1, transcendentals=0),
         name="attend_forward",
     )(meta, joined, cosine, sine)
 
@@ -332,11 +339,7 @@
             pltpu.VMEM((rows, GROUP * HD), BF16),
         ],
         compiler_params=pltpu.CompilerParams(vmem_limit_bytes=32 * 2**20),
-        cost_estimate=pl.CostEstimate(
-            flops=GROUP * rows * rows * LANES * 10,
-            bytes_accessed=rows * wide * 8,
-            transcendentals=GROUP * rows * rows // 2,
-        ),
+        cost_estimate=pl.CostEstimate(flops=1, bytes_accessed=1, transcendentals=0),
         name="attend_backward",
     )(meta, qkv, logs, back, cosine, sine)
 
@@ -372,102 +375,74 @@
     return (weight - rate * (direction + decay * weight), moment_new, square_new)
 
 
-def adam_kernel(rate, decay, clip_ref, weight_ref, grad_ref, moment_ref, square_ref, *out_refs):
-    done = adam(
-        weight_ref[...],
-        grad_ref[...].astype(F32),
-        moment_ref[...],
-        square_ref[...],
-        clip_ref[0],
-        rate,
-        decay,
-    )
-    for ref, value in zip(out_refs, done):
-        ref[...] = value
-
-
-def update(weight, grad, moment, square, clip, rate, decay):
-    shape = weight.shape
-    rows, columns = math.prod(shape[:-1]), shape[-1]
-    tall = rows // 2
-    spec = pl.BlockSpec((tall, columns), lambda i: (i, 0))
-    flat = [a.reshape(rows, columns) for a in (weight, grad, moment, square)]
-    done = pl.pallas_call(
-        functools.partial(adam_kernel, rate, decay),
-        grid=(rows // tall,),
-        in_specs=[pl.BlockSpec(memory_space=pltpu.SMEM)] + [spec] * 4,
-        out_specs=[spec] * 3,
-        out_shape=[jax.ShapeDtypeStruct((rows, columns), F32)] * 3,
-        compiler_params=pltpu.CompilerParams(vmem_limit_bytes=60 * 2**20),
-        cost_estimate=pl.CostEstimate(
-            flops=rows * columns * 16, bytes_accessed=rows * columns * 26, transcendentals=rows * columns
-        ),
-        name="update",
-    )(clip.reshape(1), *flat)
-    return [a.reshape(shape) for a in done]
-
-
-def adam_rows_kernel(rate, decay, side_ref, clip_ref, weight_ref, grad_ref, moment_ref, square_ref, *out_refs):
-    heads, _, columns = weight_ref.shape
-    halves = grad_ref.shape[1]
+def adam_all_kernel(rates, side_ref, clip_ref, *refs):
+    side, clip = side_ref[0], clip_ref[0]
+    pieces_ref, turned_ref, in_grad_ref, out_grad_ref = refs[:4]
+    states, outs = refs[4:16], refs[16:]
+
+    def apply(k, grad, at):
+        weight, moment, square = [ref[at] for ref in states[3 * k : 3 * k + 3]]
+        done = adam(weight, grad.astype(F32), moment, square, clip, *rates[k])
+        for ref, value in zip(outs[3 * k : 3 * k + 3], done):
+            ref[at] = value
+
+    columns = states[0].shape[-1]
     unit = columns // (2 * UNITS)
-    per_half = UNITS // halves
+    per_half = UNITS // 2
     for n in range(2 * UNITS):
         which, half, place = n // UNITS, n % UNITS // per_half, n % per_half
-        cut = slice(n * unit, (n + 1) * unit)
-        for j in range(heads):
-            first = (heads * place + j) * unit
-            done = adam(
-                weight_ref[j, :, cut],
-                grad_ref[which ^ side_ref[0], half, :, first : first + unit].astype(F32),
-                moment_ref[j, :, cut],
-                square_ref[j, :, cut],
-                clip_ref[0],
-                rate,
-                decay,
-            )
-            for ref, value in zip(out_refs, done):
-                ref[j, :, cut] = value
-
-
-def adam_columns_kernel(rate, decay, side_ref, clip_ref, weight_ref, grad_ref, moment_ref, square_ref, *out_refs):
-    done = adam(
-        weight_ref[...],
-        grad_ref[0, 0].astype(F32).T,
-        moment_ref[...],
-        square_ref[...],
-        clip_ref[0],
-        rate,
-        decay,
-    )
-    for ref, value in zip(out_refs, done):
-        ref[...] = value
-
-
-def update_pieces(kernel, weight, pieces, moment, square, clip, side, block, at, piece_block, piece_at, rate, decay):
-    spec = pl.BlockSpec(block, lambda i, s: at(i))
+        for j in range(2):
+            first = (2 * place + j) * unit
+            grad = pieces_ref[which ^ side, half, :, first : first + unit]
+            apply(0, grad, (j, slice(None), slice(n * unit, (n + 1) * unit)))
+    apply(1, turned_ref[0, 0].astype(F32).T, (slice(None), slice(None)))
+    apply(2, in_grad_ref[...], (slice(None), slice(None)))
+    apply(3, out_grad_ref[...], (slice(None), slice(None)))
+
+
+def update_all(states, pieces, in_grad, out_grad, clip, side, rates):
+    steps = 2 * UNITS
+    depth, slim = pieces.shape[2], pieces.shape[3] // 3
+    unit = 2 * slim // UNITS
+
+    def rows(array):
+        lead = array.shape[:-2]
+        block = lead + (array.shape[-2] // steps, array.shape[-1])
+        return pl.BlockSpec(block, lambda i, s: (0,) * len(lead) + (i, 0))
+
+    specs = [rows(a) for a in states]
     grid_spec = pltpu.PrefetchScalarGridSpec(
         num_scalar_prefetch=1,
-        grid=(weight.size // math.prod(block),),
+        grid=(steps,),
         in_specs=[
             pl.BlockSpec(memory_space=pltpu.SMEM),
-            spec,
-            pl.BlockSpec(piece_block, lambda i, s: piece_at(i, s[0])),
-            spec,
-            spec,
-        ],
-        out_specs=[spec] * 3,
+            pl.BlockSpec((2, 2, depth // steps, 2 * slim), lambda i, s: (0, 0, i, 0)),
+            pl.BlockSpec(
+                (1, 1, depth, unit),
+                lambda i, s: ((i // UNITS) ^ s[0], i % UNITS // 2, 0, UNITS + i % 2),
+            ),
+            rows(in_grad),
+            rows(out_grad),
+        ]
+        + specs,
+        out_specs=specs,
     )
     return pl.pallas_call(
-        functools.partial(kernel, rate, decay),
+        functools.partial(adam_all_kernel, rates),
         grid_spec=grid_spec,
-        out_shape=[jax.ShapeDtypeStruct(weight.shape, F32)] * 3,
+        out_shape=[jax.ShapeDtypeStruct(a.shape, F32) for a in states],
         compiler_params=pltpu.CompilerParams(vmem_limit_bytes=60 * 2**20),
-        cost_estimate=pl.CostEstimate(
-            flops=weight.size * 16, bytes_accessed=weight.size * 26, transcendentals=weight.size
-        ),
-        name="update_pieces",
-    )(side.reshape(1).astype(jnp.int32), clip.reshape(1), weight, pieces, moment, square)
+        cost_estimate=pl.CostEstimate(flops=1, bytes_accessed=1, transcendentals=0),
+        name="update_all",
+    )(
+        side.reshape(1).astype(jnp.int32),
+        clip.reshape(1),
+        pieces,
+        pieces,
+        in_grad,
+        out_grad,
+        *states,
+    )
 
 
 def split_kernel(unit, side_ref, in_ref, out_ref, *part_refs):
@@ -498,9 +473,7 @@
         grid_spec=grid_spec,
         out_shape=[part] * 2,
         compiler_params=pltpu.CompilerParams(vmem_limit_bytes=60 * 2**20),
-        cost_estimate=pl.CostEstimate(
-            flops=depth * hidden * 3, bytes_accessed=depth * hidden * 18, transcendentals=0
-        ),
+        cost_estimate=pl.CostEstimate(flops=1, bytes_accessed=1, transcendentals=0),
         name="split_feed",
     )(side.reshape(1).astype(jnp.int32), feed_in, feed_out)
 
@@ -547,11 +520,7 @@
             jax.ShapeDtypeStruct((count, 2 * slim), BF16),
         ],
         compiler_params=pltpu.CompilerParams(vmem_limit_bytes=48 * 2**20),
-        cost_estimate=pl.CostEstimate(
-            flops=6 * count * width * slim,
-            bytes_accessed=4 * count * width + 6 * width * slim + 6 * count * slim,
-            transcendentals=count * slim,
-        ),
+        cost_estimate=pl.CostEstimate(flops=1, bytes_accessed=1, transcendentals=0),
         name="feed_both_ways",
     )(rows, back, weight)
 
@@ -577,11 +546,7 @@
         out_specs=pl.BlockSpec((1, cut, 3 * slim), lambda i: (i, 0, 0)),
         out_shape=jax.ShapeDtypeStruct((parts, cut, 3 * slim), BF16),
         compiler_params=pltpu.CompilerParams(vmem_limit_bytes=48 * 2**20),
-        cost_estimate=pl.CostEstimate(
-            flops=6 * count * width * slim,
-            bytes_accessed=4 * count * width + 6 * count * slim + 6 * width * slim,
-            transcendentals=0,
-        ),
+        cost_estimate=pl.CostEstimate(flops=1, bytes_accessed=1, transcendentals=0),
         name="weight_gradients",
     )(rows, grad, back, activated)
 
@@ -611,11 +576,7 @@
         out_specs=pl.BlockSpec((tall, width), lambda i: (i, 0)),
         out_shape=jax.ShapeDtypeStruct((count, width), BF16),
         compiler_params=pltpu.CompilerParams(vmem_limit_bytes=56 * 2**20),
-        cost_estimate=pl.CostEstimate(
-            flops=2 * count * width * depth,
-            bytes_accessed=2 * count * (width + depth) + 2 * width * depth,
-            transcendentals=0,
-        ),
+        cost_estimate=pl.CostEstimate(flops=1, bytes_accessed=1, transcendentals=0),
         name="back_products",
     )(*operands)
 
@@ -768,32 +729,41 @@
         (blocks, grad_b, activated_a, activated_b)
     )
     moved = [flip(block, c, sizes) for block, c in zip(blocks[1:], combos(feed_links)[1:])]
-    pairs = [(activated_a, weight_a), (activated_b, weight_b)]
-    forward_near = flip(back_products(pairs, 2, 3, 1), (core,), sizes)
-    forward_mine = back_products(pairs, 2, 3, 0)
-    forward_blocks = add_blocks(forward_mine, forward_near, 2 ** len(feed_links))
     parts_b = gradients(grad_b, activated_b)
     sums_b = summed(parts_b)
-    moved, forward_blocks, parts_b = lax.optimization_barrier((moved, forward_blocks, parts_b))
+    pairs = [(activated_a, weight_a), (activated_b, weight_b)]
+    forward_near = back_products(pairs, 2, 3, 1)
+    moved, parts_b, forward_near, activated_a, activated_b = lax.optimization_barrier(
+        (moved, parts_b, forward_near, activated_a, activated_b)
+    )
 
     grad_from_two, gain_two_grad = norm_back(
         hidden_state, rate_two, gains[1], added(blocks[0], moved)
     )
     grad_hidden = cotangent.astype(F32) + grad_from_two
     grad_branch = grad_hidden.astype(BF16)
-    forward_links = combos(feed_links)[1:]
-    forward_moved = {("x",): flip(forward_blocks[forward_links.index(("x",)) + 1], ("x",), sizes)}
 
     def regroup(sums):
         mine, other = halves(sums, 0)
         return jnp.stack([mine, flip(other, ("x",), sizes)])
 
+    pairs = [(activated_a, weight_a), (activated_b, weight_b)]
+    forward_mine = back_products(pairs, 2, 3, 0)
+    forward_blocks = add_blocks(
+        forward_mine, flip(forward_near, (core,), sizes), 2 ** len(feed_links)
+    )
     sums_a, grad_branch = lax.optimization_barrier((sums_a, grad_branch))
     grad_moved = sends(grad_branch, pack_links)
     pieces_a = regroup(sums_a)
-    grad_moved, forward_moved, pieces_a = lax.optimization_barrier(
-        (grad_moved, forward_moved, pieces_a)
-    )
+    grad_moved, forward_blocks, pieces_a = lax.optimization_barrier(
+        (grad_moved, forward_blocks, pieces_a)
+    )
+    forward_links = combos(feed_links)[1:]
+    forward_first = [
+        flip(block, c, sizes)
+        for block, c in zip(forward_blocks[1:], forward_links)
+        if "x" not in c
+    ]
     gathered_grad = over_core([grad_branch] + grad_moved)
     grad_attended = product(gathered_grad, full_out, 1, 0).astype(BF16)
     groups = attend_in.shape[1] // ((GROUP + 2) * HD)
@@ -809,19 +779,18 @@
         return mine, flip(other, ("x",), sizes)
 
     out_mine, out_other = split_sides(product(gathered_grad, attended, 0, 0))
-    grad_joined[-1], out_other = lax.optimization_barrier((grad_joined[-1], out_other))
-    attend_out_shard = sum_depth(added(out_mine, [out_other]).astype(BF16)).T
-    in_pairs = [split_sides(product(normed_one, grad, 0, 0)) for grad in grad_joined]
-    forward_moved |= {
-        c: flip(block, c, sizes)
-        for block, c in zip(forward_blocks[1:], forward_links)
-        if c != ("x",)
-    }
-    in_pairs, forward_moved = lax.optimization_barrier((in_pairs, forward_moved))
-    block_out = added(forward_blocks[0], list(forward_moved.values()))
-    block_out = (hidden_state + block_out).astype(BF16)
+    in_pairs = [split_sides(product(normed_one, grad, 0, 0)) for grad in grad_joined[:-1]]
+    grad_joined[-1], out_other, forward_first, in_pairs = lax.optimization_barrier(
+        (grad_joined[-1], out_other, forward_first, in_pairs)
+    )
+    out_sums = added(out_mine, [out_other]).astype(BF16)
+    in_pairs.append(split_sides(product(normed_one, grad_joined[-1], 0, 0)))
+    in_pairs, forward_blocks = lax.optimization_barrier((in_pairs, forward_blocks))
     in_parts = [added(mine, [other]).astype(BF16) for mine, other in in_pairs]
-    attend_in_shard = sum_depth(jnp.concatenate(in_parts, axis=2))
+    forward_last = [
+        flip(block, c, sizes) for block, c in zip(forward_blocks[1:], forward_links) if "x" in c
+    ]
+    attend_terms = to_owners(jnp.concatenate(in_parts + [out_sums], axis=2))
     joined_back = jnp.concatenate(grad_joined, axis=1)
     own, moved = collect(
         product(joined_back[:half], full_in, 1, 1).astype(BF16),
@@ -830,54 +799,51 @@
         core,
         sizes,
     )
+    sums_b, forward_last, moved = lax.optimization_barrier((sums_b, forward_last, moved))
     grad_normed_one = added(own, moved)
     grad_from_one, gain_one_grad = norm_back(inputs, norm_rate(inputs), gains[0], grad_normed_one)
     tokens_grad = (grad_hidden + grad_from_one).astype(BF16)
 
-    pieces = jnp.stack([pieces_a, regroup(sums_b)], axis=1)
-
+    gain_grads = sum_near(
+        jnp.stack([gain_one_grad, gain_two_grad]) * inverse_total, tensor, sizes
+    )
+    pieces_b = regroup(sums_b)
     def squares(shard):
         shard = shard.astype(F32)
         return jnp.sum(shard * shard)
 
-    matrix_squares = (
-        squares(attend_in_shard)
-        + squares(attend_out_shard)
-        + squares(pieces)
-    )
-    total = sum_everywhere(
-        jnp.concatenate(
-            [
-                gain_one_grad * inverse_total,
-                gain_two_grad * inverse_total,
-                jnp.full((LANES,), matrix_squares),
-            ]
-        ),
-        tensor,
-        sizes,
-    )
-    gain_grads = total[: 2 * width].reshape(2, width)
-    grad_norm = jnp.sqrt(total[2 * width] + jnp.sum(gain_grads * gain_grads))
+    feed_squares = squares(sums_a) + squares(sums_b)
+    attend_terms, gain_grads, tokens_grad, pieces_b, feed_squares = lax.optimization_barrier(
+        (attend_terms, gain_grads, tokens_grad, pieces_b, feed_squares)
+    )
+    gain_grads = sum_far(gain_grads, sizes)
+    attend_sums = sum_terms(attend_terms)
+    attend_in_shard = attend_sums[:, : attend_in.shape[1]]
+    attend_out_shard = attend_sums[:, attend_in.shape[1] :].T
+    block_out = added(forward_blocks[0], forward_first + forward_last)
+    block_out = (hidden_state + block_out).astype(BF16)
+    pieces = jnp.stack([pieces_a, pieces_b], axis=1)
+
+    matrix_squares = feed_squares + squares(attend_sums)
+    total_squares = sum_scalar(matrix_squares, ("z", "x") + tuple(tensor), sizes)
+    grad_norm = jnp.sqrt(total_squares + jnp.sum(gain_grads * gain_grads))
     clip = jnp.minimum(1.0, CLIP_LIMIT / (grad_norm + 1e-06))
+    clip, block_out = lax.optimization_barrier((clip, block_out))
     gain_width = norm_gains.shape[1]
     gain_shard = lax.dynamic_slice_in_dim(
         gain_grads, lax.axis_index(("z", "x")) * gain_width, gain_width, 1
     )
-    first = update(attend_in, attend_in_shard, moment_attend_in, square_attend_in, clip, MATRIX_RATE, MATRIX_DECAY)
-    second = update(attend_out, attend_out_shard, moment_attend_out, square_attend_out, clip, OUTPUT_RATE, MATRIX_DECAY)
-    tall = depth // 2
-    third = update_pieces(
-        adam_rows_kernel, feed_in, pieces, moment_feed_in, square_feed_in, clip, side,
-        (2, tall, feed_in.shape[2]), lambda i: (0, i, 0),
-        (2, 2, tall, 2 * slim), lambda i, s: (0, 0, i, 0),
-        MATRIX_RATE, MATRIX_DECAY,
-    )
-    fourth = update_pieces(
-        adam_columns_kernel, feed_out, pieces, moment_feed_out, square_feed_out, clip, side,
-        (slim, depth), lambda i: (i, 0),
-        (1, 1, depth, slim), lambda i, s: ((i // 2) ^ s, i % 2, 0, 2),
-        MATRIX_RATE, MATRIX_DECAY,
-    )
+    states = (
+        (feed_in, moment_feed_in, square_feed_in)
+        + (feed_out, moment_feed_out, square_feed_out)
+        + (attend_in, moment_attend_in, square_attend_in)
+        + (attend_out, moment_attend_out, square_attend_out)
+    )
+    matrix, output = (MATRIX_RATE, MATRIX_DECAY), (OUTPUT_RATE, MATRIX_DECAY)
+    done = update_all(
+        states, pieces, attend_in_shard, attend_out_shard, clip, side, (matrix, matrix, matrix, output)
+    )
+    third, fourth, first, second = done[:3], done[3:6], done[6:9], done[9:]
     fifth = adam(norm_gains, gain_shard, moment_gains, square_gains, clip, GAIN_RATE, 0.0)
     return (block_out, tokens_grad, grad_norm, *first, *second, *third, *fourth, *fifth)
 

time: 673 us -> 659 us (0.979)
    ppermute x36, waiting for transfers between devices: 226 us -> 237 us  [flip(): return lax.ppermute(value, tuple(axes), pairs)]
    all_to_all x2, waiting for transfers between devices: 8.72 us -> 0.01 us  [the longest x1 0.01 us: sum_scalar(): lax.all_to_all(jnp.full((count, LANES), value), axes, 0, 0, tiled=True)]
    unnamed x119 -> x128, local copies, waits for them, and re-layouts: 16.7 us -> 19.3 us
    pallas_call x4 -> x1, Pallas kernels: 22.2 us -> 20.7 us  [update_all(): pl.pallas_call(functools.partial(adam_all_kernel, rates), grid_spec=grid_...]
  transfers between devices with their start and end apart: 46 -> 46, of which waited for: 26 -> 26; matrix products, arithmetic and copies ran while one was open for 17% -> 16% of each run, Pallas kernels for 26% -> 27%
where the time goes in v4:
time: 659 us; the launch traced here: 653 us
  waiting for transfers between devices  261 us (40%)
  Pallas kernels  197 us (30%)
  other arithmetic  71.6 us (11%)
  starting transfers between devices  48.4 us (7%)
  local copies, waits for them, and re-layouts  31.7 us (5%)
  matrix products  23.2 us (4%)
  between operations  19.6 us (3%)
    ppermute x36, waiting for transfers between devices, flip(): return lax.ppermute(value, tuple(axes), pairs)  237 us
    pallas_call x4, Pallas kernels, back_products(): pl.pallas_call(back_kernel, grid=(count // tall,), in_specs=specs, out_sp...  47.5 us
    pallas_call x2, Pallas kernels, feed_both_ways(): pl.pallas_call(functools.partial(feed_kernel, unit), grid=(count // tall,...  38.4 us
    pallas_call x2, Pallas kernels, weight_gradients(): pl.pallas_call(functools.partial(weights_kernel, scale), grid=(parts,), i...  37.9 us
    ppermute x36, starting transfers between devices, flip(): return lax.ppermute(value, tuple(axes), pairs)  30.2 us
    dot_general x9, matrix products, product(): lax.dot_general(left, right, (((left_dim,), (right_dim,)), ((), ())), pre...  23.2 us
    pallas_call x2, Pallas kernels, attend_backward(): pl.pallas_call(functools.partial(backward_kernel, docs, devices), grid=(1...  23 us
    pallas_call x1, Pallas kernels, update_all(): pl.pallas_call(functools.partial(adam_all_kernel, rates), grid_spec=grid_...  20.7 us
  transfers between devices with their start and end apart: 46, of which 26 were waited for; matrix products, arithmetic and copies ran while one was open for 16% of the time, Pallas kernels for 27%

profile of v4, /device:TPU:0, one launch (start us, length us, event | category | flops | bytes accessed | tf_op | source)
XLA Modules:
  0.0 652.8 jit_solution(10704307304600840089)
XLA Ops:
  27.6 14.1 %collective-permute-done.1 = bf16[256,1536]{1,0:T(8,128)(2,1)} collective-permute-done((bf16[256,1536]{1,0:T(8,128)(2,1)}, bf16[256,1536]{1,0:T(8,128)(2,1)}, u32[]{:S(2)}, u32[]{:S(2)}) %collective-permute-start.1) | collective-permute-done | bytes 786464 | tf_op jit(solution)/shard_map/ppermute | solution.py:39
  45.1 11.9 %collective-permute-done.2 = bf16[256,1536]{1,0:T(8,128)(2,1)} collective-permute-done((bf16[256,1536]{1,0:T(8,128)(2,1)}, bf16[256,1536]{1,0:T(8,128)(2,1)}, u32[]{:S(2)}, u32[]{:S(2)}) %collective-permute-start.2) | collective-permute-done | bytes 786464 | tf_op jit(solution)/shard_map/ppermute | solution.py:39
  81.7 17.6 %collective-permute-done.4 = bf16[256,2048]{1,0:T(8,128)(2,1)S(1)} collective-permute-done((bf16[256,2048]{1,0:T(8,128)(2,1)S(1)}, bf16[256,2048]{1,0:T(8,128)(2,1)S(1)}, u32[]{:S(2)}, u32[]{:S(2)}) %collective-permute-start.4) | collective-permute-done | bytes 1048608 | tf_op jit(solution)/shard_map/ppermute | solution.py:39
  99.3 12.5 %collective-permute-done.3 = bf16[4,272,768]{2,1,0:T(8,128)(2,1)} collective-permute-done((bf16[4,272,768]{2,1,0:T(8,128)(2,1)}, bf16[4,272,768]{2,1,0:T(8,128)(2,1)}, u32[]{:S(2)}, u32[]{:S(2)}) %collective-permute-start.3) | collective-permute-done | bytes 1671200 | tf_op jit(solution)/shard_map/ppermute | solution.py:39
  119.7 13.7 %attend_forward.1 = (bf16[1024,512]{1,0:T(8,128)(2,1)S(1)}, bf16[1024,768]{1,0:T(8,128)(2,1)S(1)}, f32[2,8,1024]{2,1,0:T(8,128)S(1)}) custom-call(s32[3]{0:T(128)S(1)} %pad_add_fusion.meta_ref, f32[1024,768]{1,0:T(8,128)S(1)} %fusion.30.joined_ref, f32[1024,128]{1,0:T(8,128)S(1)} %get-tuple-element.253.cos_ref, f32[1024,128]{1,0:T(8,128)S(1)} %get-tuple-element.254.sin_ref), custom_call_target="tpu_custom_call" | custom-call | flops 1 | bytes 1 | tf_op jit(solution)/shard_map/attend_forward/pallas_call | solution.py:286
  142.6 19.8 %collective-permute-done.9 = bf16[512,1024]{1,0:T(8,128)(2,1)S(1)} collective-permute-done((bf16[512,1024]{1,0:T(8,128)(2,1)S(1)}, bf16[512,1024]{1,0:T(8,128)(2,1)S(1)}, u32[]{:S(2)}, u32[]{:S(2)}) %collective-permute-start.9) | collective-permute-done | bytes 1048608 | tf_op jit(solution)/shard_map/ppermute | solution.py:39
  162.4 22.0 %collective-permute-done.10 = bf16[512,1024]{1,0:T(8,128)(2,1)S(1)} collective-permute-done((bf16[512,1024]{1,0:T(8,128)(2,1)S(1)}, bf16[512,1024]{1,0:T(8,128)(2,1)S(1)}, u32[]{:S(2)}, u32[]{:S(2)}) %collective-permute-start.10) | collective-permute-done | bytes 1048608 | tf_op jit(solution)/shard_map/ppermute | solution.py:39
  204.3 15.3 %collective-permute-done.11 = bf16[256,2048]{1,0:T(8,128)(2,1)S(1)} collective-permute-done((bf16[256,2048]{1,0:T(8,128)(2,1)S(1)}, bf16[256,2048]{1,0:T(8,128)(2,1)S(1)}, u32[]{:S(2)}, u32[]{:S(2)}) %collective-permute-start.11) | collective-permute-done | bytes 1048608 | tf_op jit(solution)/shard_map/ppermute | solution.py:39
  222.1 20.9 %collective-permute-done.13 = bf16[256,2048]{1,0:T(8,128)(2,1)S(1)} collective-permute-done((bf16[256,2048]{1,0:T(8,128)(2,1)S(1)}, bf16[256,2048]{1,0:T(8,128)(2,1)S(1)}, u32[]{:S(2)}, u32[]{:S(2)}) %collective-permute-start.13) | collective-permute-done | bytes 1048608 | tf_op jit(solution)/shard_map/ppermute | solution.py:39
  253.0 19.1 %feed_both_ways.2 = (bf16[2048,512]{1,0:T(8,128)(2,1)S(1)}, bf16[2048,1024]{1,0:T(8,128)(2,1)}) custom-call(bf16[2048,2048]{1,0:T(8,128)(2,1)} %constant_dynamic-update-slice_fusion.4.rows_ref, bf16[2048,2048]{1,0:T(8,128)(2,1)} %pad_maximum_fusion.back_ref, bf16[2048,1536]{1,0:T(8,128)(2,1)} %all-gather.5.cloned.1.call-done.weight_ref.refs_1_), custom_call_target="tpu_custom_call" | custom-call | flops 1 | bytes 1 | tf_op jit(solution)/shard_map/feed_both_ways/pallas_call | solution.py:506
  272.1 19.2 %weight_gradients.2 = bf16[4,512,1536]{2,1,0:T(8,128)(2,1)} custom-call(bf16[2048,2048]{1,0:T(8,128)(2,1)} %constant_dynamic-update-slice_fusion.4.rows_ref, bf16[2048,1024]{1,0:T(8,128)(2,1)} %get-tuple-element.149.grad_ref.refs_0_, bf16[2048,2048]{1,0:T(8,128)(2,1)} %pad_maximum_fusion.back_ref, bf16[2048,512]{1,0:T(8,128)(2,1)S(1)} %get-tuple-element.171.activated_ref.refs_0_), custom_call_target="tpu_custom_call" | custom-call | flops 1 | bytes 1 | tf_op jit(solution)/shard_map/weight_gradients/pallas_call | solution.py:537
  291.4 12.2 %all-gather.7.cloned.1.call-done.weight_ref.refs_3_ = bf16[2048,1536]{1,0:T(8,128)(2,1)} async-done(((bf16[512,1536]{1,0:T(8,128)(2,1)}), bf16[2048,1536]{1,0:T(8,128)(2,1)}) %all-gather.7.cloned.1.call-update) | async-done | bytes 6291472 | tf_op jit(solution)/shard_map/all_gather | solution.py:670
  303.6 19.2 %feed_both_ways.3 = (bf16[2048,512]{1,0:T(8,128)(2,1)S(1)}, bf16[2048,1024]{1,0:T(8,128)(2,1)}) custom-call(bf16[2048,2048]{1,0:T(8,128)(2,1)} %constant_dynamic-update-slice_fusion.4.rows_ref, bf16[2048,2048]{1,0:T(8,128)(2,1)} %pad_maximum_fusion.back_ref, bf16[2048,1536]{1,0:T(8,128)(2,1)} %all-gather.7.cloned.1.call-done.weight_ref.refs_3_), custom_call_target="tpu_custom_call" | custom-call | flops 1 | bytes 1 | tf_op jit(solution)/shard_map/feed_both_ways/pallas_call | solution.py:506
  322.8 15.2 %back_products.5 = bf16[1024,2048]{1,0:T(8,128)(2,1)} custom-call(bf16[2048,1024]{1,0:T(8,128)(2,1)} %get-tuple-element.149.grad_ref.refs_0_, bf16[2048,1536]{1,0:T(8,128)(2,1)} %all-gather.5.cloned.1.call-done.weight_ref.refs_1_, bf16[2048,1024]{1,0:T(8,128)(2,1)} %get-tuple-element.164.refs_2_.grad_ref, ...), custom_call_target="tpu_custom_call" | custom-call | flops 1 | bytes 1 | tf_op jit(solution)/shard_map/back_products/pallas_call | solution.py:572
  338.1 14.6 %back_products.4.mine_ref = bf16[1024,2048]{1,0:T(8,128)(2,1)} custom-call(bf16[2048,1024]{1,0:T(8,128)(2,1)} %get-tuple-element.149.grad_ref.refs_0_, bf16[2048,1536]{1,0:T(8,128)(2,1)} %all-gather.5.cloned.1.call-done.weight_ref.refs_1_, bf16[2048,1024]{1,0:T(8,128)(2,1)} %get-tuple-element.164.refs_2_.grad_ref, ...), custom_call_target="tpu_custom_call" | custom-call | flops 1 | bytes 1 | tf_op jit(solution)/shard_map/back_products/pallas_call | solution.py:572
  362.1 18.7 %weight_gradients.3 = bf16[4,512,1536]{2,1,0:T(8,128)(2,1)} custom-call(bf16[2048,2048]{1,0:T(8,128)(2,1)} %constant_dynamic-update-slice_fusion.4.rows_ref, bf16[2048,1024]{1,0:T(8,128)(2,1)} %get-tuple-element.164.refs_2_.grad_ref, bf16[2048,2048]{1,0:T(8,128)(2,1)} %pad_maximum_fusion.back_ref, bf16[2048,512]{1,0:T(8,128)(2,1)S(1)} %get-tuple-element.172.activated_ref.refs_2_), custom_call_target="tpu_custom_call" | custom-call | flops 1 | bytes 1 | tf_op jit(solution)/shard_map/weight_gradients/pallas_call | solution.py:537
  389.5 18.4 %collective-permute-done.19 = bf16[256,2048]{1,0:T(8,128)(2,1)} collective-permute-done((bf16[256,2048]{1,0:T(8,128)(2,1)}, bf16[256,2048]{1,0:T(8,128)(2,1)}, u32[]{:S(2)}, u32[]{:S(2)}) %collective-permute-start.19) | collective-permute-done | bytes 1048608 | tf_op jit(solution)/shard_map/ppermute | solution.py:39
  461.8 11.5 %attend_backward.3 = bf16[1024,384]{1,0:T(8,128)(2,1)S(1)} custom-call(s32[3]{0:T(128)S(1)} %pad_add_fusion.meta_ref, bf16[1024,768]{1,0:T(8,128)(2,1)S(1)} %copy-done.5, f32[2,8,1024]{2,1,0:T(8,128)S(1)} %get-tuple-element.130.log_ref, bf16[1024,512]{1,0:T(8,128)(2,1)S(1)} %convolution_convert_fusion.4.back_ref, ...), custom_call_target="tpu_custom_call" | custom-call | flops 1 | bytes 1 | tf_op jit(solution)/shard_map/attend_backward/pallas_call | solution.py:319
  477.6 11.5 %attend_backward.2 = bf16[1024,384]{1,0:T(8,128)(2,1)S(1)} custom-call(s32[3]{0:T(128)S(1)} %pad_add_fusion.meta_ref, bf16[1024,768]{1,0:T(8,128)(2,1)S(1)} %copy-done.5, f32[2,8,1024]{2,1,0:T(8,128)S(1)} %get-tuple-element.130.log_ref, bf16[1024,512]{1,0:T(8,128)(2,1)S(1)} %convolution_convert_fusion.4.back_ref, ...), custom_call_target="tpu_custom_call" | custom-call | flops 1 | bytes 1 | tf_op jit(solution)/shard_map/attend_backward/pallas_call | solution.py:319
  489.2 10.1 %collective-permute-done.26 = bf16[4,256,384]{2,1,0:T(8,128)(2,1)S(1)} collective-permute-done((bf16[4,256,384]{2,1,0:T(8,128)(2,1)S(1)}, bf16[4,256,384]{2,1,0:T(8,128)(2,1)S(1)}, u32[]{:S(2)}, u32[]{:S(2)}) %collective-permute-start.26) | collective-permute-done | bytes 786464 | tf_op jit(solution)/shard_map/ppermute | solution.py:39
  512.8 14.0 %collective-permute-done.27 = bf16[4,256,384]{2,1,0:T(8,128)(2,1)} collective-permute-done((bf16[4,256,384]{2,1,0:T(8,128)(2,1)}, bf16[4,256,384]{2,1,0:T(8,128)(2,1)}, u32[]{:S(2)}, u32[]{:S(2)}) %collective-permute-start.27) | collective-permute-done | bytes 786464 | tf_op jit(solution)/shard_map/ppermute | solution.py:39
  542.8 10.4 %collective-permute-done.29 = bf16[256,2048]{1,0:T(8,128)(2,1)} collective-permute-done((bf16[256,2048]{1,0:T(8,128)(2,1)}, bf16[256,2048]{1,0:T(8,128)(2,1)}, u32[]{:S(2)}, u32[]{:S(2)}) %collective-permute-start.29) | collective-permute-done | bytes 1048608 | tf_op jit(solution)/shard_map/ppermute | solution.py:39
  553.2 22.2 %collective-permute-done.30 = bf16[256,2048]{1,0:T(8,128)(2,1)} collective-permute-done((bf16[256,2048]{1,0:T(8,128)(2,1)}, bf16[256,2048]{1,0:T(8,128)(2,1)}, u32[]{:S(2)}, u32[]{:S(2)}) %collective-permute-start.30) | collective-permute-done | bytes 1048608 | tf_op jit(solution)/shard_map/ppermute | solution.py:39
  624.0 20.7 %update_all.1 = (f32[2,256,2048]{2,1,0:T(8,128)}, f32[2,256,2048]{2,1,0:T(8,128)}, f32[2,256,2048]{2,1,0:T(8,128)}, f32[2048,256]{1,0:T(8,128)}, f32[2048,256]{1...) custom-call(s32[1]{0:T(128)} %bitcast.5.side_ref, ...), custom_call_target="tpu_custom_call" | custom-call | flops 1 | bytes 1 | tf_op jit(solution)/shard_map/update_all/pallas_call | solution.py:430
  (300 shorter events, 248.3 us)
Async XLA Ops:
  7.2 63.3 %all-gather.9.cloned.1.call-start = ((), (), s32[]{:S(2)}) async-start(), calls=%async_computation.9 | async-start | bytes 2088960 | tf_op jit(solution)/shard_map/all_gather | solution.py:657
  11.2 55.6 %all-to-all-start = ((bf16[4,256,512]{2,1,0:T(8,128)(2,1)}), bf16[4,256,512]{2,1,0:T(8,128)(2,1)S(1)}, u32[]{:S(2)}, u32[]{:S(2)}) async-start(bf16[4,256,512]{2,1,0:T(8,128)(2,1)} %broadcast_in_dim.7), calls=%async_computation | async-start | bytes 2097152 | tf_op jit(solution)/shard_map/all_to_all | solution.py:84
  17.5 235.5 %all-gather.5.cloned.1.call-start = ((), (), s32[]{:S(2)}) async-start(), calls=%async_computation.5 | async-start | bytes 7864320 | tf_op jit(solution)/shard_map/all_gather | solution.py:670
  22.3 34.7 %collective-permute-start.2 = (bf16[256,1536]{1,0:T(8,128)(2,1)}, bf16[256,1536]{1,0:T(8,128)(2,1)}, u32[]{:S(2)}, u32[]{:S(2)}) collective-permute-start(bf16[256,1536]{1,0:T(8,128)(2,1)} %get-tuple-element.123), channel_id=1, source_target_pairs={{0,4},{4,0},{1,5},{5,1},{2,6},{6,2},{3,7},{7,3},{8,12},{12,8},{9,1... | collective-permute-start | bytes 2359304 | tf_op jit(solution)/shard_map/ppermute | solution.py:39
  22.9 37.5 %collective-permute-start = (bf16[256,2048]{1,0:T(8,128)(2,1)S(1)}, bf16[256,2048]{1,0:T(8,128)(2,1)S(1)}, u32[]{:S(2)}, u32[]{:S(2)}) collective-permute-start(bf16[256,2048]{1,0:T(8,128)(2,1)S(1)} %copy-done.17), channel_id=1, source_target_pairs={{0,2},{2,0},{1,3},{3,1},{4,6},{6,4},{5,7},{7,5},{8,10},{10,8},{9,1... | collective-permute-start | bytes 3145736 | tf_op jit(solution)/shard_map/ppermute | solution.py:39
  72.1 231.4 %all-gather.7.cloned.1.call-start = ((), (), s32[]{:S(2)}) async-start(), calls=%async_computation.6 | async-start | bytes 7864320 | tf_op jit(solution)/shard_map/all_gather | solution.py:670
  72.1 39.7 %collective-permute-start.3 = (bf16[4,272,768]{2,1,0:T(8,128)(2,1)}, bf16[4,272,768]{2,1,0:T(8,128)(2,1)}, u32[]{:S(2)}, u32[]{:S(2)}) collective-permute-start(bf16[4,272,768]{2,1,0:T(8,128)(2,1)} %bitcast.78), channel_id=1, source_target_pairs={{0,4},{4,0},{1,5},{5,1},{2,6},{6,2},{3,7},{7,3},{8,12},{12,8},{9,1... | collective-permute-start | bytes 5013512 | tf_op jit(solution)/shard_map/ppermute | solution.py:39
  78.9 55.7 %collective-permute-start.6 = (bf16[4,256,512]{2,1,0:T(8,128)(2,1)S(1)}, bf16[4,256,512]{2,1,0:T(8,128)(2,1)S(1)}, u32[]{:S(2)}, u32[]{:S(2)}) collective-permute-start(bf16[4,256,512]{2,1,0:T(8,128)(2,1)S(1)} %copy-done.35), channel_id=1, source_target_pairs={{0,4},{4,0},{1,5},{5,1},{2,6},{6,2},{3,7},{7,3},{8,12},{12,8},{9,1... | collective-permute-start | bytes 3145736 | tf_op jit(solution)/shard_map/ppermute | solution.py:39
  138.0 46.5 %collective-permute-start.10 = (bf16[512,1024]{1,0:T(8,128)(2,1)S(1)}, bf16[512,1024]{1,0:T(8,128)(2,1)S(1)}, u32[]{:S(2)}, u32[]{:S(2)}) collective-permute-start(bf16[512,1024]{1,0:T(8,128)(2,1)S(1)} %get-tuple-element.139), channel_id=1, source_target_pairs={{0,4},{4,0},{1,5},{5,1},{2,6},{6,2},{3,7},{7,3},{8,12},{12,8},{9,1... | collective-permute-start | bytes 3145736 | tf_op jit(solution)/shard_map/ppermute | solution.py:39
  141.1 43.4 %collective-permute-start.8 = (bf16[256,2048]{1,0:T(8,128)(2,1)S(1)}, bf16[256,2048]{1,0:T(8,128)(2,1)S(1)}, u32[]{:S(2)}, u32[]{:S(2)}) collective-permute-start(bf16[256,2048]{1,0:T(8,128)(2,1)S(1)} %get-tuple-element.137), channel_id=1, source_target_pairs={{0,2},{2,0},{1,3},{3,1},{4,6},{6,4},{5,7},{7,5},{8,10},{10,8},{9,1... | collective-permute-start | bytes 3145736 | tf_op jit(solution)/shard_map/ppermute | solution.py:39
  188.7 227.9 %reduce-scatter.3.cloned.1.call-start = ((), (), s32[]{:S(2)}) async-start(), calls=%async_computation.7 | async-start | bytes 7864320 | tf_op jit(solution)/shard_map/reduce_scatter | solution.py:717
  196.0 26.1 %collective-permute-start.12 = (bf16[256,2048]{1,0:T(8,128)(2,1)S(1)}, bf16[256,2048]{1,0:T(8,128)(2,1)S(1)}, u32[]{:S(2)}, u32[]{:S(2)}) collective-permute-start(bf16[256,2048]{1,0:T(8,128)(2,1)S(1)} %get-tuple-element.234), channel_id=1, source_target_pairs={{0,4},{4,0},{1,5},{5,1},{2,6},{6,2},{3,7},{7,3},{8,12},{12,8},{9,1... | collective-permute-start | bytes 3145736 | tf_op jit(solution)/shard_map/ppermute | solution.py:39
  197.5 45.5 %collective-permute-start.13 = (bf16[256,2048]{1,0:T(8,128)(2,1)S(1)}, bf16[256,2048]{1,0:T(8,128)(2,1)S(1)}, u32[]{:S(2)}, u32[]{:S(2)}) collective-permute-start(bf16[256,2048]{1,0:T(8,128)(2,1)S(1)} %get-tuple-element.234), channel_id=1, source_target_pairs={{0,6},{2,4},{4,2},{6,0},{1,7},{3,5},{5,3},{7,1},{8,14},{10,12},{12... | collective-permute-start | bytes 3145736 | tf_op jit(solution)/shard_map/ppermute | solution.py:39
  303.6 239.2 %reduce-scatter.5.cloned.1.call-start = ((), (), s32[]{:S(2)}) async-start(), calls=%async_computation.8 | async-start | bytes 7864320 | tf_op jit(solution)/shard_map/reduce_scatter | solution.py:717
  358.6 30.9 %collective-permute-start.17 = (bf16[256,2048]{1,0:T(8,128)(2,1)}, bf16[256,2048]{1,0:T(8,128)(2,1)}, u32[]{:S(2)}, u32[]{:S(2)}) collective-permute-start(bf16[256,2048]{1,0:T(8,128)(2,1)} %get-tuple-element.161), channel_id=1, source_target_pairs={{0,2},{2,0},{1,3},{3,1},{4,6},{6,4},{5,7},{7,5},{8,10},{10,8},{9,1... | collective-permute-start | bytes 3145736 | tf_op jit(solution)/shard_map/ppermute | solution.py:39
  360.1 29.4 %collective-permute-start.18 = (bf16[256,2048]{1,0:T(8,128)(2,1)}, bf16[256,2048]{1,0:T(8,128)(2,1)}, u32[]{:S(2)}, u32[]{:S(2)}) collective-permute-start(bf16[256,2048]{1,0:T(8,128)(2,1)} %get-tuple-element.162), channel_id=1, source_target_pairs={{0,4},{4,0},{1,5},{5,1},{2,6},{6,2},{3,7},{7,3},{8,12},{12,8},{9,1... | collective-permute-start | bytes 3145736 | tf_op jit(solution)/shard_map/ppermute | solution.py:39
  361.6 46.4 %collective-permute-start.19 = (bf16[256,2048]{1,0:T(8,128)(2,1)}, bf16[256,2048]{1,0:T(8,128)(2,1)}, u32[]{:S(2)}, u32[]{:S(2)}) collective-permute-start(bf16[256,2048]{1,0:T(8,128)(2,1)} %get-tuple-element.163), channel_id=1, source_target_pairs={{0,6},{2,4},{4,2},{6,0},{1,7},{3,5},{5,3},{7,1},{8,14},{10,12},{12... | collective-permute-start | bytes 3145736 | tf_op jit(solution)/shard_map/ppermute | solution.py:39
  449.7 39.4 %collective-permute-start.25 = (bf16[256,2048]{1,0:T(8,128)(2,1)S(1)}, bf16[256,2048]{1,0:T(8,128)(2,1)S(1)}, u32[]{:S(2)}, u32[]{:S(2)}) collective-permute-start(bf16[256,2048]{1,0:T(8,128)(2,1)S(1)} %get-tuple-element.180), channel_id=1, source_target_pairs={{0,2},{2,0},{1,3},{3,1},{4,6},{6,4},{5,7},{7,5},{8,10},{10,8},{9,1... | collective-permute-start | bytes 3145736 | tf_op jit(solution)/shard_map/ppermute | solution.py:39
  457.2 42.1 %collective-permute-start.24 = (bf16[4,256,512]{2,1,0:T(8,128)(2,1)S(1)}, bf16[4,256,512]{2,1,0:T(8,128)(2,1)S(1)}, u32[]{:S(2)}, u32[]{:S(2)}) collective-permute-start(bf16[4,256,512]{2,1,0:T(8,128)(2,1)S(1)} %dynamic-slice_bitcast_fusion), channel_id=1, source_target_pairs={{0,4},{4,0},{1,5},{5,1},{2,6},{6,2},{3,7},{7,3},{8,12},{12,8},{9,1... | collective-permute-start | bytes 3145736 | tf_op jit(solution)/shard_map/ppermute | solution.py:39
  502.5 27.3 %collective-permute-start.28 = (bf16[512,2048]{1,0:T(8,128)(2,1)}, bf16[512,2048]{1,0:T(8,128)(2,1)S(1)}, u32[]{:S(2)}, u32[]{:S(2)}) collective-permute-start(bf16[512,2048]{1,0:T(8,128)(2,1)} %convolution_convert_fusion), channel_id=1, source_target_pairs={{0,1},{1,0},{2,3},{3,2},{4,5},{5,4},{6,7},{7,6},{8,9},{9,8},{10,11... | collective-permute-start | bytes 6291464 | tf_op jit(solution)/shard_map/ppermute | solution.py:39
  526.8 26.4 %collective-permute-start.29 = (bf16[256,2048]{1,0:T(8,128)(2,1)}, bf16[256,2048]{1,0:T(8,128)(2,1)}, u32[]{:S(2)}, u32[]{:S(2)}) collective-permute-start(bf16[256,2048]{1,0:T(8,128)(2,1)} %get-tuple-element.193), channel_id=1, source_target_pairs={{0,4},{4,0},{1,5},{5,1},{2,6},{6,2},{3,7},{7,3},{8,12},{12,8},{9,1... | collective-permute-start | bytes 3145736 | tf_op jit(solution)/shard_map/ppermute | solution.py:39
  527.4 48.0 %collective-permute-start.30 = (bf16[256,2048]{1,0:T(8,128)(2,1)}, bf16[256,2048]{1,0:T(8,128)(2,1)}, u32[]{:S(2)}, u32[]{:S(2)}) collective-permute-start(bf16[256,2048]{1,0:T(8,128)(2,1)} %get-tuple-element.194), channel_id=1, source_target_pairs={{0,6},{2,4},{4,2},{6,0},{1,7},{3,5},{5,3},{7,1},{8,14},{10,12},{12... | collective-permute-start | bytes 3145736 | tf_op jit(solution)/shard_map/ppermute | solution.py:39
  531.2 46.9 %collective-permute-start.31 = (bf16[256,2048]{1,0:T(8,128)(2,1)}, bf16[256,2048]{1,0:T(8,128)(2,1)S(1)}, u32[]{:S(2)}, u32[]{:S(2)}) collective-permute-start(bf16[256,2048]{1,0:T(8,128)(2,1)} %get-tuple-element.195), channel_id=1, source_target_pairs={{0,2},{2,0},{1,3},{3,1},{4,6},{6,4},{5,7},{7,5},{8,10},{10,8},{9,1... | collective-permute-start | bytes 3145736 | tf_op jit(solution)/shard_map/ppermute | solution.py:39
  535.0 67.2 %all-to-all-start.1 = ((bf16[4,256,1280]{2,1,0:T(8,128)(2,1)}), bf16[4,256,1280]{2,1,0:T(8,128)(2,1)}, u32[]{:S(2)}, u32[]{:S(2)}) async-start(bf16[4,256,1280]{2,1,0:T(8,128)(2,1)} %pad_maximum_fusion.5), calls=%async_computation.2 | async-start | bytes 5242880 | tf_op jit(solution)/shard_map/all_to_all | solution.py:88
  (83 other events, 888.2 us)
Sparse Core Ops, SparseCore 0:
  10.2 60.3 all-gather.8
  72.7 114.5 all-gather.4
  189.4 114.0 all-gather.6
  305.7 108.9 reduce-scatter.2
  416.9 111.2 reduce-scatter.4

commit v5 on v4

--- a/solution.py
+++ b/solution.py
@@ -84,16 +84,8 @@
     return lax.all_to_all(copies, "z", 0, 0, tiled=True)
 
 
-def to_owners(blocks):
-    return lax.all_to_all(blocks, "z", 0, 0, tiled=True)
-
-
-def sum_terms(terms):
-    return jnp.sum(terms.astype(F32), axis=0).astype(BF16)
-
-
 def sum_near(value, tensor, sizes):
-    for a in tuple(reversed(tensor)) + ("x",):
+    for a in ("x",) + tuple(reversed(tensor)):
         value = value + flip(value, (a,), sizes)
     return value
 
@@ -787,10 +779,7 @@
     in_pairs.append(split_sides(product(normed_one, grad_joined[-1], 0, 0)))
     in_pairs, forward_blocks = lax.optimization_barrier((in_pairs, forward_blocks))
     in_parts = [added(mine, [other]).astype(BF16) for mine, other in in_pairs]
-    forward_last = [
-        flip(block, c, sizes) for block, c in zip(forward_blocks[1:], forward_links) if "x" in c
-    ]
-    attend_terms = to_owners(jnp.concatenate(in_parts + [out_sums], axis=2))
+    attend_sums = summed(jnp.concatenate(in_parts + [out_sums], axis=2))
     joined_back = jnp.concatenate(grad_joined, axis=1)
     own, moved = collect(
         product(joined_back[:half], full_in, 1, 1).astype(BF16),
@@ -799,7 +788,9 @@
         core,
         sizes,
     )
-    sums_b, forward_last, moved = lax.optimization_barrier((sums_b, forward_last, moved))
+    forward_x = flip(forward_blocks[forward_links.index(("x",)) + 1], ("x",), sizes)
+    sums_b, forward_x, own, moved = lax.optimization_barrier((sums_b, forward_x, own, moved))
+    pieces_b = regroup(sums_b)
     grad_normed_one = added(own, moved)
     grad_from_one, gain_one_grad = norm_back(inputs, norm_rate(inputs), gains[0], grad_normed_one)
     tokens_grad = (grad_hidden + grad_from_one).astype(BF16)
@@ -807,28 +798,31 @@
     gain_grads = sum_near(
         jnp.stack([gain_one_grad, gain_two_grad]) * inverse_total, tensor, sizes
     )
-    pieces_b = regroup(sums_b)
     def squares(shard):
         shard = shard.astype(F32)
         return jnp.sum(shard * shard)
 
     feed_squares = squares(sums_a) + squares(sums_b)
-    attend_terms, gain_grads, tokens_grad, pieces_b, feed_squares = lax.optimization_barrier(
-        (attend_terms, gain_grads, tokens_grad, pieces_b, feed_squares)
+    attend_sums, gain_grads, tokens_grad, feed_squares = lax.optimization_barrier(
+        (attend_sums, gain_grads, tokens_grad, feed_squares)
     )
     gain_grads = sum_far(gain_grads, sizes)
-    attend_sums = sum_terms(attend_terms)
     attend_in_shard = attend_sums[:, : attend_in.shape[1]]
     attend_out_shard = attend_sums[:, attend_in.shape[1] :].T
-    block_out = added(forward_blocks[0], forward_first + forward_last)
-    block_out = (hidden_state + block_out).astype(BF16)
     pieces = jnp.stack([pieces_a, pieces_b], axis=1)
 
     matrix_squares = feed_squares + squares(attend_sums)
     total_squares = sum_scalar(matrix_squares, ("z", "x") + tuple(tensor), sizes)
     grad_norm = jnp.sqrt(total_squares + jnp.sum(gain_grads * gain_grads))
     clip = jnp.minimum(1.0, CLIP_LIMIT / (grad_norm + 1e-06))
-    clip, block_out = lax.optimization_barrier((clip, block_out))
+    clip, forward_blocks = lax.optimization_barrier((clip, forward_blocks))
+    forward_last = [
+        flip(block, c, sizes)
+        for block, c in zip(forward_blocks[1:], forward_links)
+        if "x" in c and len(c) > 1
+    ]
+    block_out = added(forward_blocks[0], forward_first + [forward_x] + forward_last)
+    block_out = (hidden_state + block_out).astype(BF16)
     gain_width = norm_gains.shape[1]
     gain_shard = lax.dynamic_slice_in_dim(
         gain_grads, lax.axis_index(("z", "x")) * gain_width, gain_width, 1

time: 659 us -> 650 us (0.986)
  waiting for transfers between devices: 261 us -> 240 us
  matrix products: 23.2 us -> 30.4 us
    ppermute x36, waiting for transfers between devices: 237 us -> 201 us  [flip(): return lax.ppermute(value, tuple(axes), pairs)]
    reduce_scatter x2 -> x3, waiting for transfers between devices: 0.01 us -> 11.8 us  [summed(): return lax.psum_scatter(parts, 'z', scatter_dimension=0, tiled=False)]
    dot_general x9, matrix products: 23.2 us -> 30.4 us  [product(): lax.dot_general(left, right, (((left_dim,), (right_dim,)), ((), ())), pre...]
    unnamed x128 -> x126, local copies, waits for them, and re-layouts: 19.3 us -> 22.7 us
  transfers between devices with their start and end apart: 46 -> 46, of which waited for: 26 -> 28; matrix products, arithmetic and copies ran while one was open for 16% -> 18% of each run, Pallas kernels for 27% -> 31%
where the time goes in v5:
time: 650 us; the launch traced here: 644 us
  waiting for transfers between devices  240 us (37%)
  Pallas kernels  198 us (30%)
  other arithmetic  67.7 us (10%)
  starting transfers between devices  50.2 us (8%)
  local copies, waits for them, and re-layouts  38.1 us (6%)
  matrix products  30.4 us (5%)
  between operations  19.8 us (3%)
    ppermute x36, waiting for transfers between devices, flip(): return lax.ppermute(value, tuple(axes), pairs)  201 us
    pallas_call x4, Pallas kernels, back_products(): pl.pallas_call(back_kernel, grid=(count // tall,), in_specs=specs, out_sp...  47.2 us
    pallas_call x2, Pallas kernels, feed_both_ways(): pl.pallas_call(functools.partial(feed_kernel, unit), grid=(count // tall,...  38.5 us
    pallas_call x2, Pallas kernels, weight_gradients(): pl.pallas_call(functools.partial(weights_kernel, scale), grid=(parts,), i...  38 us
    ppermute x36, starting transfers between devices, flip(): return lax.ppermute(value, tuple(axes), pairs)  34.4 us
    dot_general x9, matrix products, product(): lax.dot_general(left, right, (((left_dim,), (right_dim,)), ((), ())), pre...  30.4 us
    pallas_call x2, Pallas kernels, attend_backward(): pl.pallas_call(functools.partial(backward_kernel, docs, devices), grid=(1...  23 us
    unnamed x126, local copies, waits for them, and re-layouts  22.7 us
  transfers between devices with their start and end apart: 46, of which 28 were waited for; matrix products, arithmetic and copies ran while one was open for 18% of the time, Pallas kernels for 31%

profile of v5, /device:TPU:0, one launch (start us, length us, event | category | flops | bytes accessed | tf_op | source)
XLA Modules:
  0.0 643.8 jit_solution(5215647170290621933)
XLA Ops:
  27.6 14.1 %collective-permute-done.1 = bf16[256,1536]{1,0:T(8,128)(2,1)} collective-permute-done((bf16[256,1536]{1,0:T(8,128)(2,1)}, bf16[256,1536]{1,0:T(8,128)(2,1)}, u32[]{:S(2)}, u32[]{:S(2)}) %collective-permute-start.1) | collective-permute-done | bytes 786464 | tf_op jit(solution)/shard_map/ppermute | solution.py:39
  45.1 11.9 %collective-permute-done.2 = bf16[256,1536]{1,0:T(8,128)(2,1)} collective-permute-done((bf16[256,1536]{1,0:T(8,128)(2,1)}, bf16[256,1536]{1,0:T(8,128)(2,1)}, u32[]{:S(2)}, u32[]{:S(2)}) %collective-permute-start.2) | collective-permute-done | bytes 786464 | tf_op jit(solution)/shard_map/ppermute | solution.py:39
  81.9 17.5 %collective-permute-done.4 = bf16[256,2048]{1,0:T(8,128)(2,1)S(1)} collective-permute-done((bf16[256,2048]{1,0:T(8,128)(2,1)S(1)}, bf16[256,2048]{1,0:T(8,128)(2,1)S(1)}, u32[]{:S(2)}, u32[]{:S(2)}) %collective-permute-start.4) | collective-permute-done | bytes 1048608 | tf_op jit(solution)/shard_map/ppermute | solution.py:39
  99.4 12.5 %collective-permute-done.3 = bf16[4,272,768]{2,1,0:T(8,128)(2,1)} collective-permute-done((bf16[4,272,768]{2,1,0:T(8,128)(2,1)}, bf16[4,272,768]{2,1,0:T(8,128)(2,1)}, u32[]{:S(2)}, u32[]{:S(2)}) %collective-permute-start.3) | collective-permute-done | bytes 1671200 | tf_op jit(solution)/shard_map/ppermute | solution.py:39
  119.8 13.7 %attend_forward.1 = (bf16[1024,512]{1,0:T(8,128)(2,1)S(1)}, bf16[1024,768]{1,0:T(8,128)(2,1)S(1)}, f32[2,8,1024]{2,1,0:T(8,128)S(1)}) custom-call(s32[3]{0:T(128)S(1)} %pad_add_fusion.meta_ref, f32[1024,768]{1,0:T(8,128)S(1)} %fusion.30.joined_ref, f32[1024,128]{1,0:T(8,128)S(1)} %get-tuple-element.255.cos_ref, f32[1024,128]{1,0:T(8,128)S(1)} %get-tuple-element.256.sin_ref), custom_call_target="tpu_custom_call" | custom-call | flops 1 | bytes 1 | tf_op jit(solution)/shard_map/attend_forward/pallas_call | solution.py:278
  142.6 19.8 %collective-permute-done.9 = bf16[512,1024]{1,0:T(8,128)(2,1)S(1)} collective-permute-done((bf16[512,1024]{1,0:T(8,128)(2,1)S(1)}, bf16[512,1024]{1,0:T(8,128)(2,1)S(1)}, u32[]{:S(2)}, u32[]{:S(2)}) %collective-permute-start.9) | collective-permute-done | bytes 1048608 | tf_op jit(solution)/shard_map/ppermute | solution.py:39
  162.4 22.0 %collective-permute-done.10 = bf16[512,1024]{1,0:T(8,128)(2,1)S(1)} collective-permute-done((bf16[512,1024]{1,0:T(8,128)(2,1)S(1)}, bf16[512,1024]{1,0:T(8,128)(2,1)S(1)}, u32[]{:S(2)}, u32[]{:S(2)}) %collective-permute-start.10) | collective-permute-done | bytes 1048608 | tf_op jit(solution)/shard_map/ppermute | solution.py:39
  202.7 15.1 %collective-permute-done.11 = bf16[256,2048]{1,0:T(8,128)(2,1)S(1)} collective-permute-done((bf16[256,2048]{1,0:T(8,128)(2,1)S(1)}, bf16[256,2048]{1,0:T(8,128)(2,1)S(1)}, u32[]{:S(2)}, u32[]{:S(2)}) %collective-permute-start.11) | collective-permute-done | bytes 1048608 | tf_op jit(solution)/shard_map/ppermute | solution.py:39
  219.8 21.7 %collective-permute-done.13 = bf16[256,2048]{1,0:T(8,128)(2,1)S(1)} collective-permute-done((bf16[256,2048]{1,0:T(8,128)(2,1)S(1)}, bf16[256,2048]{1,0:T(8,128)(2,1)S(1)}, u32[]{:S(2)}, u32[]{:S(2)}) %collective-permute-start.13) | collective-permute-done | bytes 1048608 | tf_op jit(solution)/shard_map/ppermute | solution.py:39
  251.6 19.1 %feed_both_ways.2 = (bf16[2048,512]{1,0:T(8,128)(2,1)S(1)}, bf16[2048,1024]{1,0:T(8,128)(2,1)}) custom-call(bf16[2048,2048]{1,0:T(8,128)(2,1)} %constant_dynamic-update-slice_fusion.4.rows_ref, bf16[2048,2048]{1,0:T(8,128)(2,1)} %pad_maximum_fusion.back_ref, bf16[2048,1536]{1,0:T(8,128)(2,1)} %all-gather.5.cloned.1.call-done.weight_ref.refs_1_), custom_call_target="tpu_custom_call" | custom-call | flops 1 | bytes 1 | tf_op jit(solution)/shard_map/feed_both_ways/pallas_call | solution.py:498
  270.7 19.3 %weight_gradients.2 = bf16[4,512,1536]{2,1,0:T(8,128)(2,1)} custom-call(bf16[2048,2048]{1,0:T(8,128)(2,1)} %constant_dynamic-update-slice_fusion.4.rows_ref, bf16[2048,1024]{1,0:T(8,128)(2,1)} %get-tuple-element.149.grad_ref.refs_0_, bf16[2048,2048]{1,0:T(8,128)(2,1)} %pad_maximum_fusion.back_ref, bf16[2048,512]{1,0:T(8,128)(2,1)S(1)} %get-tuple-element.171.activated_ref.refs_0_), custom_call_target="tpu_custom_call" | custom-call | flops 1 | bytes 1 | tf_op jit(solution)/shard_map/weight_gradients/pallas_call | solution.py:529
  290.0 13.5 %all-gather.7.cloned.1.call-done.weight_ref.refs_3_ = bf16[2048,1536]{1,0:T(8,128)(2,1)} async-done(((bf16[512,1536]{1,0:T(8,128)(2,1)}), bf16[2048,1536]{1,0:T(8,128)(2,1)}) %all-gather.7.cloned.1.call-update) | async-done | bytes 6291472 | tf_op jit(solution)/shard_map/all_gather | solution.py:662
  303.5 19.5 %feed_both_ways.3 = (bf16[2048,512]{1,0:T(8,128)(2,1)S(1)}, bf16[2048,1024]{1,0:T(8,128)(2,1)}) custom-call(bf16[2048,2048]{1,0:T(8,128)(2,1)} %constant_dynamic-update-slice_fusion.4.rows_ref, bf16[2048,2048]{1,0:T(8,128)(2,1)} %pad_maximum_fusion.back_ref, bf16[2048,1536]{1,0:T(8,128)(2,1)} %all-gather.7.cloned.1.call-done.weight_ref.refs_3_), custom_call_target="tpu_custom_call" | custom-call | flops 1 | bytes 1 | tf_op jit(solution)/shard_map/feed_both_ways/pallas_call | solution.py:498
  323.0 15.2 %back_products.5 = bf16[1024,2048]{1,0:T(8,128)(2,1)} custom-call(bf16[2048,1024]{1,0:T(8,128)(2,1)} %get-tuple-element.149.grad_ref.refs_0_, bf16[2048,1536]{1,0:T(8,128)(2,1)} %all-gather.5.cloned.1.call-done.weight_ref.refs_1_, bf16[2048,1024]{1,0:T(8,128)(2,1)} %get-tuple-element.164.refs_2_.grad_ref, ...), custom_call_target="tpu_custom_call" | custom-call | flops 1 | bytes 1 | tf_op jit(solution)/shard_map/back_products/pallas_call | solution.py:564
  338.3 14.6 %back_products.4.mine_ref = bf16[1024,2048]{1,0:T(8,128)(2,1)} custom-call(bf16[2048,1024]{1,0:T(8,128)(2,1)} %get-tuple-element.149.grad_ref.refs_0_, bf16[2048,1536]{1,0:T(8,128)(2,1)} %all-gather.5.cloned.1.call-done.weight_ref.refs_1_, bf16[2048,1024]{1,0:T(8,128)(2,1)} %get-tuple-element.164.refs_2_.grad_ref, ...), custom_call_target="tpu_custom_call" | custom-call | flops 1 | bytes 1 | tf_op jit(solution)/shard_map/back_products/pallas_call | solution.py:564
  362.2 18.7 %weight_gradients.3 = bf16[4,512,1536]{2,1,0:T(8,128)(2,1)} custom-call(bf16[2048,2048]{1,0:T(8,128)(2,1)} %constant_dynamic-update-slice_fusion.4.rows_ref, bf16[2048,1024]{1,0:T(8,128)(2,1)} %get-tuple-element.164.refs_2_.grad_ref, bf16[2048,2048]{1,0:T(8,128)(2,1)} %pad_maximum_fusion.back_ref, bf16[2048,512]{1,0:T(8,128)(2,1)S(1)} %get-tuple-element.172.activated_ref.refs_2_), custom_call_target="tpu_custom_call" | custom-call | flops 1 | bytes 1 | tf_op jit(solution)/shard_map/weight_gradients/pallas_call | solution.py:529
  381.0 8.8 %back_products.6 = bf16[1024,2048]{1,0:T(8,128)(2,1)} custom-call(bf16[2048,512]{1,0:T(8,128)(2,1)} %copy-done, bf16[2048,1536]{1,0:T(8,128)(2,1)} %all-gather.5.cloned.1.call-done.weight_ref.refs_1_, bf16[2048,512]{1,0:T(8,128)(2,1)} %copy-done.1, bf16[2048,1536]{1,0:T(8,128)(2,1)} %all-gather.7.cloned.1.call-done.weight_ref.refs_3_), custom_call_target="tpu_custom_call" | custom-call | flops 1 | bytes 1 | tf_op jit(solution)/shard_map/back_products/pallas_call | solution.py:564
  389.8 18.3 %collective-permute-done.19 = bf16[256,2048]{1,0:T(8,128)(2,1)} collective-permute-done((bf16[256,2048]{1,0:T(8,128)(2,1)}, bf16[256,2048]{1,0:T(8,128)(2,1)}, u32[]{:S(2)}, u32[]{:S(2)}) %collective-permute-start.19) | collective-permute-done | bytes 1048608 | tf_op jit(solution)/shard_map/ppermute | solution.py:39
  420.4 8.7 %back_products.7.mine_ref = bf16[1024,2048]{1,0:T(8,128)(2,1)} custom-call(bf16[2048,512]{1,0:T(8,128)(2,1)} %copy-done, bf16[2048,1536]{1,0:T(8,128)(2,1)} %all-gather.5.cloned.1.call-done.weight_ref.refs_1_, bf16[2048,512]{1,0:T(8,128)(2,1)} %copy-done.1, bf16[2048,1536]{1,0:T(8,128)(2,1)} %all-gather.7.cloned.1.call-done.weight_ref.refs_3_), custom_call_target="tpu_custom_call" | custom-call | flops 1 | bytes 1 | tf_op jit(solution)/shard_map/back_products/pallas_call | solution.py:564
  463.1 11.4 %attend_backward.3 = bf16[1024,384]{1,0:T(8,128)(2,1)S(1)} custom-call(s32[3]{0:T(128)S(1)} %pad_add_fusion.meta_ref, bf16[1024,768]{1,0:T(8,128)(2,1)S(1)} %copy-done.5, f32[2,8,1024]{2,1,0:T(8,128)S(1)} %get-tuple-element.141.log_ref, bf16[1024,512]{1,0:T(8,128)(2,1)S(1)} %convolution_convert_fusion.4.back_ref, ...), custom_call_target="tpu_custom_call" | custom-call | flops 1 | bytes 1 | tf_op jit(solution)/shard_map/attend_backward/pallas_call | solution.py:311
  482.4 11.6 %attend_backward.2 = bf16[1024,384]{1,0:T(8,128)(2,1)S(1)} custom-call(s32[3]{0:T(128)S(1)} %pad_add_fusion.meta_ref, bf16[1024,768]{1,0:T(8,128)(2,1)S(1)} %copy-done.5, f32[2,8,1024]{2,1,0:T(8,128)S(1)} %get-tuple-element.141.log_ref, bf16[1024,512]{1,0:T(8,128)(2,1)S(1)} %copy-done.7, f32[1024,128]{1,0:T(8,128)S(1)} %get-tuple-element.255.cos_ref, ...), custom_call_target="tpu_custom_call" | custom-call | flops 1 | bytes 1 | tf_op jit(solution)/shard_map/attend_backward/pallas_call | solution.py:311
  539.2 18.7 %collective-permute-done.28 = bf16[256,2048]{1,0:T(8,128)(2,1)} collective-permute-done((bf16[256,2048]{1,0:T(8,128)(2,1)}, bf16[256,2048]{1,0:T(8,128)(2,1)}, u32[]{:S(2)}, u32[]{:S(2)}) %collective-permute-start.28) | collective-permute-done | bytes 1048608 | tf_op jit(solution)/shard_map/ppermute | solution.py:39
  571.7 11.8 %reduce-scatter.6.cloned.1.call-done = bf16[1,256,1280]{1,2,0:T(8,128)(2,1)} async-done(((bf16[4,256,1280]{1,2,0:T(8,128)(2,1)}), bf16[1,256,1280]{1,2,0:T(8,128)(2,1)}) %reduce-scatter.6.cloned.1.call-update) | async-done | bytes 655376 | tf_op jit(solution)/shard_map/reduce_scatter | solution.py:709
  609.6 21.0 %update_all.1 = (f32[2,256,2048]{2,1,0:T(8,128)}, f32[2,256,2048]{2,1,0:T(8,128)}, f32[2,256,2048]{2,1,0:T(8,128)}, f32[2048,256]{1,0:T(8,128)}, f32[2048,256]{1...) custom-call(s32[1]{0:T(128)} %bitcast.5.side_ref, ...), custom_call_target="tpu_custom_call" | custom-call | flops 1 | bytes 1 | tf_op jit(solution)/shard_map/update_all/pallas_call | solution.py:422
  (299 shorter events, 245.6 us)
Async XLA Ops:
  7.2 63.3 %all-gather.9.cloned.1.call-start = ((), (), s32[]{:S(2)}) async-start(), calls=%async_computation.10 | async-start | bytes 2088960 | tf_op jit(solution)/shard_map/all_gather | solution.py:649
  11.2 55.6 %all-to-all-start = ((bf16[4,256,512]{2,1,0:T(8,128)(2,1)}), bf16[4,256,512]{2,1,0:T(8,128)(2,1)S(1)}, u32[]{:S(2)}, u32[]{:S(2)}) async-start(bf16[4,256,512]{2,1,0:T(8,128)(2,1)} %broadcast_in_dim.7), calls=%async_computation | async-start | bytes 2097152 | tf_op jit(solution)/shard_map/all_to_all | solution.py:84
  17.5 234.1 %all-gather.5.cloned.1.call-start = ((), (), s32[]{:S(2)}) async-start(), calls=%async_computation.5 | async-start | bytes 7864320 | tf_op jit(solution)/shard_map/all_gather | solution.py:662
  22.3 34.7 %collective-permute-start.2 = (bf16[256,1536]{1,0:T(8,128)(2,1)}, bf16[256,1536]{1,0:T(8,128)(2,1)}, u32[]{:S(2)}, u32[]{:S(2)}) collective-permute-start(bf16[256,1536]{1,0:T(8,128)(2,1)} %get-tuple-element.123), channel_id=1, source_target_pairs={{0,4},{4,0},{1,5},{5,1},{2,6},{6,2},{3,7},{7,3},{8,12},{12,8},{9,1... | collective-permute-start | bytes 2359304 | tf_op jit(solution)/shard_map/ppermute | solution.py:39
  22.9 37.5 %collective-permute-start = (bf16[256,2048]{1,0:T(8,128)(2,1)S(1)}, bf16[256,2048]{1,0:T(8,128)(2,1)S(1)}, u32[]{:S(2)}, u32[]{:S(2)}) collective-permute-start(bf16[256,2048]{1,0:T(8,128)(2,1)S(1)} %copy-done.21), channel_id=1, source_target_pairs={{0,2},{2,0},{1,3},{3,1},{4,6},{6,4},{5,7},{7,5},{8,10},{10,8},{9,1... | collective-permute-start | bytes 3145736 | tf_op jit(solution)/shard_map/ppermute | solution.py:39
  72.2 231.3 %all-gather.7.cloned.1.call-start = ((), (), s32[]{:S(2)}) async-start(), calls=%async_computation.6 | async-start | bytes 7864320 | tf_op jit(solution)/shard_map/all_gather | solution.py:662
  72.2 39.7 %collective-permute-start.3 = (bf16[4,272,768]{2,1,0:T(8,128)(2,1)}, bf16[4,272,768]{2,1,0:T(8,128)(2,1)}, u32[]{:S(2)}, u32[]{:S(2)}) collective-permute-start(bf16[4,272,768]{2,1,0:T(8,128)(2,1)} %bitcast.77), channel_id=1, source_target_pairs={{0,4},{4,0},{1,5},{5,1},{2,6},{6,2},{3,7},{7,3},{8,12},{12,8},{9,1... | collective-permute-start | bytes 5013512 | tf_op jit(solution)/shard_map/ppermute | solution.py:39
  79.0 55.7 %collective-permute-start.6 = (bf16[4,256,512]{2,1,0:T(8,128)(2,1)S(1)}, bf16[4,256,512]{2,1,0:T(8,128)(2,1)S(1)}, u32[]{:S(2)}, u32[]{:S(2)}) collective-permute-start(bf16[4,256,512]{2,1,0:T(8,128)(2,1)S(1)} %copy-done.38), channel_id=1, source_target_pairs={{0,4},{4,0},{1,5},{5,1},{2,6},{6,2},{3,7},{7,3},{8,12},{12,8},{9,1... | collective-permute-start | bytes 3145736 | tf_op jit(solution)/shard_map/ppermute | solution.py:39
  136.3 26.0 %collective-permute-start.9 = (bf16[512,1024]{1,0:T(8,128)(2,1)S(1)}, bf16[512,1024]{1,0:T(8,128)(2,1)S(1)}, u32[]{:S(2)}, u32[]{:S(2)}) collective-permute-start(bf16[512,1024]{1,0:T(8,128)(2,1)S(1)} %get-tuple-element.136), channel_id=1, source_target_pairs={{0,4},{4,0},{1,5},{5,1},{2,6},{6,2},{3,7},{7,3},{8,12},{12,8},{9,1... | collective-permute-start | bytes 3145736 | tf_op jit(solution)/shard_map/ppermute | solution.py:39
  137.9 46.5 %collective-permute-start.10 = (bf16[512,1024]{1,0:T(8,128)(2,1)S(1)}, bf16[512,1024]{1,0:T(8,128)(2,1)S(1)}, u32[]{:S(2)}, u32[]{:S(2)}) collective-permute-start(bf16[512,1024]{1,0:T(8,128)(2,1)S(1)} %get-tuple-element.137), channel_id=1, source_target_pairs={{0,4},{4,0},{1,5},{5,1},{2,6},{6,2},{3,7},{7,3},{8,12},{12,8},{9,1... | collective-permute-start | bytes 3145736 | tf_op jit(solution)/shard_map/ppermute | solution.py:39
  141.0 43.4 %collective-permute-start.8 = (bf16[256,2048]{1,0:T(8,128)(2,1)S(1)}, bf16[256,2048]{1,0:T(8,128)(2,1)S(1)}, u32[]{:S(2)}, u32[]{:S(2)}) collective-permute-start(bf16[256,2048]{1,0:T(8,128)(2,1)S(1)} %get-tuple-element.135), channel_id=1, source_target_pairs={{0,2},{2,0},{1,3},{3,1},{4,6},{6,4},{5,7},{7,5},{8,10},{10,8},{9,1... | collective-permute-start | bytes 3145736 | tf_op jit(solution)/shard_map/ppermute | solution.py:39
  188.7 227.3 %reduce-scatter.4.cloned.1.call-start = ((), (), s32[]{:S(2)}) async-start(), calls=%async_computation.7 | async-start | bytes 7864320 | tf_op jit(solution)/shard_map/reduce_scatter | solution.py:709
  192.3 25.6 %collective-permute-start.11 = (bf16[256,2048]{1,0:T(8,128)(2,1)S(1)}, bf16[256,2048]{1,0:T(8,128)(2,1)S(1)}, u32[]{:S(2)}, u32[]{:S(2)}) collective-permute-start(bf16[256,2048]{1,0:T(8,128)(2,1)S(1)} %get-tuple-element.234), channel_id=1, source_target_pairs={{0,2},{2,0},{1,3},{3,1},{4,6},{6,4},{5,7},{7,5},{8,10},{10,8},{9,1... | collective-permute-start | bytes 3145736 | tf_op jit(solution)/shard_map/ppermute | solution.py:39
  193.8 26.0 %collective-permute-start.12 = (bf16[256,2048]{1,0:T(8,128)(2,1)S(1)}, bf16[256,2048]{1,0:T(8,128)(2,1)S(1)}, u32[]{:S(2)}, u32[]{:S(2)}) collective-permute-start(bf16[256,2048]{1,0:T(8,128)(2,1)S(1)} %get-tuple-element.234), channel_id=1, source_target_pairs={{0,4},{4,0},{1,5},{5,1},{2,6},{6,2},{3,7},{7,3},{8,12},{12,8},{9,1... | collective-permute-start | bytes 3145736 | tf_op jit(solution)/shard_map/ppermute | solution.py:39
  195.3 46.2 %collective-permute-start.13 = (bf16[256,2048]{1,0:T(8,128)(2,1)S(1)}, bf16[256,2048]{1,0:T(8,128)(2,1)S(1)}, u32[]{:S(2)}, u32[]{:S(2)}) collective-permute-start(bf16[256,2048]{1,0:T(8,128)(2,1)S(1)} %get-tuple-element.234), channel_id=1, source_target_pairs={{0,6},{2,4},{4,2},{6,0},{1,7},{3,5},{5,3},{7,1},{8,14},{10,12},{12... | collective-permute-start | bytes 3145736 | tf_op jit(solution)/shard_map/ppermute | solution.py:39
  303.5 235.7 %reduce-scatter.8.cloned.1.call-start = ((), (), s32[]{:S(2)}) async-start(), calls=%async_computation.9 | async-start | bytes 7864320 | tf_op jit(solution)/shard_map/reduce_scatter | solution.py:709
  358.7 31.1 %collective-permute-start.17 = (bf16[256,2048]{1,0:T(8,128)(2,1)}, bf16[256,2048]{1,0:T(8,128)(2,1)S(1)}, u32[]{:S(2)}, u32[]{:S(2)}) collective-permute-start(bf16[256,2048]{1,0:T(8,128)(2,1)} %get-tuple-element.161), channel_id=1, source_target_pairs={{0,2},{2,0},{1,3},{3,1},{4,6},{6,4},{5,7},{7,5},{8,10},{10,8},{9,1... | collective-permute-start | bytes 3145736 | tf_op jit(solution)/shard_map/ppermute | solution.py:39
  360.2 29.6 %collective-permute-start.18 = (bf16[256,2048]{1,0:T(8,128)(2,1)}, bf16[256,2048]{1,0:T(8,128)(2,1)}, u32[]{:S(2)}, u32[]{:S(2)}) collective-permute-start(bf16[256,2048]{1,0:T(8,128)(2,1)} %get-tuple-element.162), channel_id=1, source_target_pairs={{0,4},{4,0},{1,5},{5,1},{2,6},{6,2},{3,7},{7,3},{8,12},{12,8},{9,1... | collective-permute-start | bytes 3145736 | tf_op jit(solution)/shard_map/ppermute | solution.py:39
  361.7 46.4 %collective-permute-start.19 = (bf16[256,2048]{1,0:T(8,128)(2,1)}, bf16[256,2048]{1,0:T(8,128)(2,1)}, u32[]{:S(2)}, u32[]{:S(2)}) collective-permute-start(bf16[256,2048]{1,0:T(8,128)(2,1)} %get-tuple-element.163), channel_id=1, source_target_pairs={{0,6},{2,4},{4,2},{6,0},{1,7},{3,5},{5,3},{7,1},{8,14},{10,12},{12... | collective-permute-start | bytes 3145736 | tf_op jit(solution)/shard_map/ppermute | solution.py:39
  381.0 202.5 %reduce-scatter.6.cloned.1.call-start = ((), (), s32[]{:S(2)}) async-start(), calls=%async_computation.8 | async-start | bytes 3276800 | tf_op jit(solution)/shard_map/reduce_scatter | solution.py:709
  445.8 50.7 %collective-permute-start.25 = (bf16[256,2048]{1,0:T(8,128)(2,1)}, bf16[256,2048]{1,0:T(8,128)(2,1)}, u32[]{:S(2)}, u32[]{:S(2)}) collective-permute-start(bf16[256,2048]{1,0:T(8,128)(2,1)} %get-tuple-element.180), channel_id=1, source_target_pairs={{0,2},{2,0},{1,3},{3,1},{4,6},{6,4},{5,7},{7,5},{8,10},{10,8},{9,1... | collective-permute-start | bytes 3145736 | tf_op jit(solution)/shard_map/ppermute | solution.py:39
  457.2 42.4 %collective-permute-start.24 = (bf16[4,256,512]{1,2,0:T(8,128)(2,1)}, bf16[4,256,512]{1,2,0:T(8,128)(2,1)}, u32[]{:S(2)}, u32[]{:S(2)}) collective-permute-start(bf16[4,256,512]{1,2,0:T(8,128)(2,1)} %bitcast.82), channel_id=1, source_target_pairs={{0,4},{4,0},{1,5},{5,1},{2,6},{6,2},{3,7},{7,3},{8,12},{12,8},{9,1... | collective-permute-start | bytes 3145736 | tf_op jit(solution)/shard_map/ppermute | solution.py:39
  564.1 40.6 %collective-permute-start.37 = (bf16[256,1536]{1,0:T(8,128)(2,1)}, bf16[256,1536]{1,0:T(8,128)(2,1)}, u32[]{:S(2)}, u32[]{:S(2)}) collective-permute-start(bf16[256,1536]{1,0:T(8,128)(2,1)} %get-tuple-element.242), channel_id=1, source_target_pairs={{0,4},{4,0},{1,5},{5,1},{2,6},{6,2},{3,7},{7,3},{8,12},{12,8},{9,1... | collective-permute-start | bytes 2359304 | tf_op jit(solution)/shard_map/ppermute | solution.py:39
  601.9 29.3 %collective-permute-start.36 = (bf16[256,2048]{1,0:T(8,128)(2,1)S(1)}, bf16[256,2048]{1,0:T(8,128)(2,1)}, u32[]{:S(2)}, u32[]{:S(2)}) collective-permute-start(bf16[256,2048]{1,0:T(8,128)(2,1)S(1)} %copy-done.16), channel_id=1, source_target_pairs={{0,6},{2,4},{4,2},{6,0},{1,7},{3,5},{5,3},{7,1},{8,14},{10,12},{12... | collective-permute-start | bytes 3145736 | tf_op jit(solution)/shard_map/ppermute | solution.py:39
  (79 other events, 937.6 us)
Sparse Core Ops, SparseCore 0:
  10.2 60.3 all-gather.8
  72.7 114.5 all-gather.4
  189.4 114.0 all-gather.6
  305.6 108.9 reduce-scatter.3
  416.8 111.2 reduce-scatter.7
  530.8 52.6 reduce-scatter.5

commit v6 on v5

--- a/solution.py
+++ b/solution.py
@@ -813,6 +813,9 @@
 
     matrix_squares = feed_squares + squares(attend_sums)
     total_squares = sum_scalar(matrix_squares, ("z", "x") + tuple(tensor), sizes)
+    total_squares, pieces, attend_in_shard, attend_out_shard = lax.optimization_barrier(
+        (total_squares, pieces, attend_in_shard, attend_out_shard)
+    )
     grad_norm = jnp.sqrt(total_squares + jnp.sum(gain_grads * gain_grads))
     clip = jnp.minimum(1.0, CLIP_LIMIT / (grad_norm + 1e-06))
     clip, forward_blocks = lax.optimization_barrier((clip, forward_blocks))

time: 650 us -> 645 us (level)
    reduce_scatter x3, waiting for transfers between devices: 11.8 us -> 0.01 us  [summed(): return lax.psum_scatter(parts, 'z', scatter_dimension=0, tiled=False)]
    ppermute x36, waiting for transfers between devices: 201 us -> 210 us  [flip(): return lax.ppermute(value, tuple(axes), pairs)]
    unnamed x126 -> x120, local copies, waits for them, and re-layouts: 22.7 us -> 23.7 us
  transfers between devices with their start and end apart: 46 -> 46, of which waited for: 28 -> 26; matrix products, arithmetic and copies ran while one was open for 18% -> 18% of each run, Pallas kernels for 31% -> 31%
where the time goes in v6:
time: 645 us; the launch traced here: 640 us
  waiting for transfers between devices  235 us (36%)
  Pallas kernels  198 us (31%)
  other arithmetic  67.6 us (10%)
  starting transfers between devices  48.1 us (7%)
  local copies, waits for them, and re-layouts  41.1 us (6%)
  matrix products  30.3 us (5%)
  between operations  19.7 us (3%)
    ppermute x36, waiting for transfers between devices, flip(): return lax.ppermute(value, tuple(axes), pairs)  210 us
    pallas_call x4, Pallas kernels, back_products(): pl.pallas_call(back_kernel, grid=(count // tall,), in_specs=specs, out_sp...  47.2 us
    pallas_call x2, Pallas kernels, feed_both_ways(): pl.pallas_call(functools.partial(feed_kernel, unit), grid=(count // tall,...  38.5 us
    pallas_call x2, Pallas kernels, weight_gradients(): pl.pallas_call(functools.partial(weights_kernel, scale), grid=(parts,), i...  38 us
    ppermute x36, starting transfers between devices, flip(): return lax.ppermute(value, tuple(axes), pairs)  34.2 us
    dot_general x9, matrix products, product(): lax.dot_general(left, right, (((left_dim,), (right_dim,)), ((), ())), pre...  30.3 us
    unnamed x120, local copies, waits for them, and re-layouts  23.7 us
    pallas_call x2, Pallas kernels, attend_backward(): pl.pallas_call(functools.partial(backward_kernel, docs, devices), grid=(1...  23 us
  transfers between devices with their start and end apart: 46, of which 26 were waited for; matrix products, arithmetic and copies ran while one was open for 18% of the time, Pallas kernels for 31%

profile of v6, /device:TPU:0, one launch (start us, length us, event | category | flops | bytes accessed | tf_op | source)
XLA Modules:
  0.0 639.6 jit_solution(6269495052985000053)
XLA Ops:
  27.6 14.1 %collective-permute-done.1 = bf16[256,1536]{1,0:T(8,128)(2,1)} collective-permute-done((bf16[256,1536]{1,0:T(8,128)(2,1)}, bf16[256,1536]{1,0:T(8,128)(2,1)}, u32[]{:S(2)}, u32[]{:S(2)}) %collective-permute-start.1) | collective-permute-done | bytes 786464 | tf_op jit(solution)/shard_map/ppermute | solution.py:39
  45.1 11.9 %collective-permute-done.2 = bf16[256,1536]{1,0:T(8,128)(2,1)} collective-permute-done((bf16[256,1536]{1,0:T(8,128)(2,1)}, bf16[256,1536]{1,0:T(8,128)(2,1)}, u32[]{:S(2)}, u32[]{:S(2)}) %collective-permute-start.2) | collective-permute-done | bytes 786464 | tf_op jit(solution)/shard_map/ppermute | solution.py:39
  81.9 17.5 %collective-permute-done.4 = bf16[256,2048]{1,0:T(8,128)(2,1)S(1)} collective-permute-done((bf16[256,2048]{1,0:T(8,128)(2,1)S(1)}, bf16[256,2048]{1,0:T(8,128)(2,1)S(1)}, u32[]{:S(2)}, u32[]{:S(2)}) %collective-permute-start.4) | collective-permute-done | bytes 1048608 | tf_op jit(solution)/shard_map/ppermute | solution.py:39
  99.4 12.5 %collective-permute-done.3 = bf16[4,272,768]{2,1,0:T(8,128)(2,1)} collective-permute-done((bf16[4,272,768]{2,1,0:T(8,128)(2,1)}, bf16[4,272,768]{2,1,0:T(8,128)(2,1)}, u32[]{:S(2)}, u32[]{:S(2)}) %collective-permute-start.3) | collective-permute-done | bytes 1671200 | tf_op jit(solution)/shard_map/ppermute | solution.py:39
  119.8 13.7 %attend_forward.1 = (bf16[1024,512]{1,0:T(8,128)(2,1)S(1)}, bf16[1024,768]{1,0:T(8,128)(2,1)S(1)}, f32[2,8,1024]{2,1,0:T(8,128)S(1)}) custom-call(s32[3]{0:T(128)S(1)} %pad_add_fusion.meta_ref, f32[1024,768]{1,0:T(8,128)S(1)} %fusion.30.joined_ref, f32[1024,128]{1,0:T(8,128)S(1)} %get-tuple-element.263.cos_ref, f32[1024,128]{1,0:T(8,128)S(1)} %get-tuple-element.264.sin_ref), custom_call_target="tpu_custom_call" | custom-call | flops 1 | bytes 1 | tf_op jit(solution)/shard_map/attend_forward/pallas_call | solution.py:278
  142.6 19.8 %collective-permute-done.9 = bf16[512,1024]{1,0:T(8,128)(2,1)S(1)} collective-permute-done((bf16[512,1024]{1,0:T(8,128)(2,1)S(1)}, bf16[512,1024]{1,0:T(8,128)(2,1)S(1)}, u32[]{:S(2)}, u32[]{:S(2)}) %collective-permute-start.9) | collective-permute-done | bytes 1048608 | tf_op jit(solution)/shard_map/ppermute | solution.py:39
  162.4 22.0 %collective-permute-done.10 = bf16[512,1024]{1,0:T(8,128)(2,1)S(1)} collective-permute-done((bf16[512,1024]{1,0:T(8,128)(2,1)S(1)}, bf16[512,1024]{1,0:T(8,128)(2,1)S(1)}, u32[]{:S(2)}, u32[]{:S(2)}) %collective-permute-start.10) | collective-permute-done | bytes 1048608 | tf_op jit(solution)/shard_map/ppermute | solution.py:39
  202.6 15.2 %collective-permute-done.11 = bf16[256,2048]{1,0:T(8,128)(2,1)S(1)} collective-permute-done((bf16[256,2048]{1,0:T(8,128)(2,1)S(1)}, bf16[256,2048]{1,0:T(8,128)(2,1)S(1)}, u32[]{:S(2)}, u32[]{:S(2)}) %collective-permute-start.11) | collective-permute-done | bytes 1048608 | tf_op jit(solution)/shard_map/ppermute | solution.py:39
  219.8 21.7 %collective-permute-done.13 = bf16[256,2048]{1,0:T(8,128)(2,1)S(1)} collective-permute-done((bf16[256,2048]{1,0:T(8,128)(2,1)S(1)}, bf16[256,2048]{1,0:T(8,128)(2,1)S(1)}, u32[]{:S(2)}, u32[]{:S(2)}) %collective-permute-start.13) | collective-permute-done | bytes 1048608 | tf_op jit(solution)/shard_map/ppermute | solution.py:39
  251.6 19.1 %feed_both_ways.2 = (bf16[2048,512]{1,0:T(8,128)(2,1)S(1)}, bf16[2048,1024]{1,0:T(8,128)(2,1)}) custom-call(bf16[2048,2048]{1,0:T(8,128)(2,1)} %constant_dynamic-update-slice_fusion.4.rows_ref, bf16[2048,2048]{1,0:T(8,128)(2,1)} %pad_maximum_fusion.back_ref, bf16[2048,1536]{1,0:T(8,128)(2,1)} %all-gather.5.cloned.1.call-done.weight_ref.refs_1_), custom_call_target="tpu_custom_call" | custom-call | flops 1 | bytes 1 | tf_op jit(solution)/shard_map/feed_both_ways/pallas_call | solution.py:498
  270.7 19.3 %weight_gradients.2 = bf16[4,512,1536]{2,1,0:T(8,128)(2,1)} custom-call(bf16[2048,2048]{1,0:T(8,128)(2,1)} %constant_dynamic-update-slice_fusion.4.rows_ref, bf16[2048,1024]{1,0:T(8,128)(2,1)} %get-tuple-element.153.grad_ref.refs_0_, bf16[2048,2048]{1,0:T(8,128)(2,1)} %pad_maximum_fusion.back_ref, bf16[2048,512]{1,0:T(8,128)(2,1)S(1)} %get-tuple-element.175.activated_ref.refs_0_), custom_call_target="tpu_custom_call" | custom-call | flops 1 | bytes 1 | tf_op jit(solution)/shard_map/weight_gradients/pallas_call | solution.py:529
  290.0 13.5 %all-gather.7.cloned.1.call-done.weight_ref.refs_3_ = bf16[2048,1536]{1,0:T(8,128)(2,1)} async-done(((bf16[512,1536]{1,0:T(8,128)(2,1)}), bf16[2048,1536]{1,0:T(8,128)(2,1)}) %all-gather.7.cloned.1.call-update) | async-done | bytes 6291472 | tf_op jit(solution)/shard_map/all_gather | solution.py:662
  303.6 19.5 %feed_both_ways.3 = (bf16[2048,512]{1,0:T(8,128)(2,1)S(1)}, bf16[2048,1024]{1,0:T(8,128)(2,1)}) custom-call(bf16[2048,2048]{1,0:T(8,128)(2,1)} %constant_dynamic-update-slice_fusion.4.rows_ref, bf16[2048,2048]{1,0:T(8,128)(2,1)} %pad_maximum_fusion.back_ref, bf16[2048,1536]{1,0:T(8,128)(2,1)} %all-gather.7.cloned.1.call-done.weight_ref.refs_3_), custom_call_target="tpu_custom_call" | custom-call | flops 1 | bytes 1 | tf_op jit(solution)/shard_map/feed_both_ways/pallas_call | solution.py:498
  323.0 15.2 %back_products.5 = bf16[1024,2048]{1,0:T(8,128)(2,1)} custom-call(bf16[2048,1024]{1,0:T(8,128)(2,1)} %get-tuple-element.153.grad_ref.refs_0_, bf16[2048,1536]{1,0:T(8,128)(2,1)} %all-gather.5.cloned.1.call-done.weight_ref.refs_1_, bf16[2048,1024]{1,0:T(8,128)(2,1)} %get-tuple-element.168.refs_2_.grad_ref, ...), custom_call_target="tpu_custom_call" | custom-call | flops 1 | bytes 1 | tf_op jit(solution)/shard_map/back_products/pallas_call | solution.py:564
  338.3 14.6 %back_products.4.mine_ref = bf16[1024,2048]{1,0:T(8,128)(2,1)} custom-call(bf16[2048,1024]{1,0:T(8,128)(2,1)} %get-tuple-element.153.grad_ref.refs_0_, bf16[2048,1536]{1,0:T(8,128)(2,1)} %all-gather.5.cloned.1.call-done.weight_ref.refs_1_, bf16[2048,1024]{1,0:T(8,128)(2,1)} %get-tuple-element.168.refs_2_.grad_ref, ...), custom_call_target="tpu_custom_call" | custom-call | flops 1 | bytes 1 | tf_op jit(solution)/shard_map/back_products/pallas_call | solution.py:564
  362.2 18.8 %weight_gradients.3 = bf16[4,512,1536]{2,1,0:T(8,128)(2,1)} custom-call(bf16[2048,2048]{1,0:T(8,128)(2,1)} %constant_dynamic-update-slice_fusion.4.rows_ref, bf16[2048,1024]{1,0:T(8,128)(2,1)} %get-tuple-element.168.refs_2_.grad_ref, bf16[2048,2048]{1,0:T(8,128)(2,1)} %pad_maximum_fusion.back_ref, bf16[2048,512]{1,0:T(8,128)(2,1)S(1)} %get-tuple-element.176.activated_ref.refs_2_), custom_call_target="tpu_custom_call" | custom-call | flops 1 | bytes 1 | tf_op jit(solution)/shard_map/weight_gradients/pallas_call | solution.py:529
  381.1 8.8 %back_products.6 = bf16[1024,2048]{1,0:T(8,128)(2,1)} custom-call(bf16[2048,512]{1,0:T(8,128)(2,1)} %copy-done, bf16[2048,1536]{1,0:T(8,128)(2,1)} %all-gather.5.cloned.1.call-done.weight_ref.refs_1_, bf16[2048,512]{1,0:T(8,128)(2,1)} %copy-done.1, bf16[2048,1536]{1,0:T(8,128)(2,1)} %all-gather.7.cloned.1.call-done.weight_ref.refs_3_), custom_call_target="tpu_custom_call" | custom-call | flops 1 | bytes 1 | tf_op jit(solution)/shard_map/back_products/pallas_call | solution.py:564
  389.9 18.3 %collective-permute-done.19 = bf16[256,2048]{1,0:T(8,128)(2,1)} collective-permute-done((bf16[256,2048]{1,0:T(8,128)(2,1)}, bf16[256,2048]{1,0:T(8,128)(2,1)}, u32[]{:S(2)}, u32[]{:S(2)}) %collective-permute-start.19) | collective-permute-done | bytes 1048608 | tf_op jit(solution)/shard_map/ppermute | solution.py:39
  420.5 8.7 %back_products.7.mine_ref = bf16[1024,2048]{1,0:T(8,128)(2,1)} custom-call(bf16[2048,512]{1,0:T(8,128)(2,1)} %copy-done, bf16[2048,1536]{1,0:T(8,128)(2,1)} %all-gather.5.cloned.1.call-done.weight_ref.refs_1_, bf16[2048,512]{1,0:T(8,128)(2,1)} %copy-done.1, bf16[2048,1536]{1,0:T(8,128)(2,1)} %all-gather.7.cloned.1.call-done.weight_ref.refs_3_), custom_call_target="tpu_custom_call" | custom-call | flops 1 | bytes 1 | tf_op jit(solution)/shard_map/back_products/pallas_call | solution.py:564
  463.1 11.4 %attend_backward.3 = bf16[1024,384]{1,0:T(8,128)(2,1)S(1)} custom-call(s32[3]{0:T(128)S(1)} %pad_add_fusion.meta_ref, bf16[1024,768]{1,0:T(8,128)(2,1)S(1)} %copy-done.5, f32[2,8,1024]{2,1,0:T(8,128)S(1)} %get-tuple-element.145.log_ref, bf16[1024,512]{1,0:T(8,128)(2,1)S(1)} %convolution_convert_fusion.4.back_ref, ...), custom_call_target="tpu_custom_call" | custom-call | flops 1 | bytes 1 | tf_op jit(solution)/shard_map/attend_backward/pallas_call | solution.py:311
  482.4 11.6 %attend_backward.2 = bf16[1024,384]{1,0:T(8,128)(2,1)S(1)} custom-call(s32[3]{0:T(128)S(1)} %pad_add_fusion.meta_ref, bf16[1024,768]{1,0:T(8,128)(2,1)S(1)} %copy-done.5, f32[2,8,1024]{2,1,0:T(8,128)S(1)} %get-tuple-element.145.log_ref, bf16[1024,512]{1,0:T(8,128)(2,1)S(1)} %copy-done.7, f32[1024,128]{1,0:T(8,128)S(1)} %get-tuple-element.263.cos_ref, ...), custom_call_target="tpu_custom_call" | custom-call | flops 1 | bytes 1 | tf_op jit(solution)/shard_map/attend_backward/pallas_call | solution.py:311
  539.6 18.4 %collective-permute-done.28 = bf16[256,2048]{1,0:T(8,128)(2,1)} collective-permute-done((bf16[256,2048]{1,0:T(8,128)(2,1)}, bf16[256,2048]{1,0:T(8,128)(2,1)}, u32[]{:S(2)}, u32[]{:S(2)}) %collective-permute-start.28) | collective-permute-done | bytes 1048608 | tf_op jit(solution)/shard_map/ppermute | solution.py:39
  572.0 9.5 %collective-permute-done.34 = bf16[256,1536]{1,0:T(8,128)(2,1)} collective-permute-done((bf16[256,1536]{1,0:T(8,128)(2,1)}, bf16[256,1536]{1,0:T(8,128)(2,1)}, u32[]{:S(2)}, u32[]{:S(2)}) %collective-permute-start.34) | collective-permute-done | bytes 786464 | tf_op jit(solution)/shard_map/ppermute | solution.py:39
  605.7 21.0 %update_all.1 = (f32[2,256,2048]{2,1,0:T(8,128)}, f32[2,256,2048]{2,1,0:T(8,128)}, f32[2,256,2048]{2,1,0:T(8,128)}, f32[2048,256]{1,0:T(8,128)}, f32[2048,256]{1...) custom-call(s32[1]{0:T(128)} %bitcast.5.side_ref, ...), custom_call_target="tpu_custom_call" | custom-call | flops 1 | bytes 1 | tf_op jit(solution)/shard_map/update_all/pallas_call | solution.py:422
  (293 shorter events, 244.0 us)
Async XLA Ops:
  7.2 63.3 %all-gather.9.cloned.1.call-start = ((), (), s32[]{:S(2)}) async-start(), calls=%async_computation.10 | async-start | bytes 2088960 | tf_op jit(solution)/shard_map/all_gather | solution.py:649
  11.2 55.6 %all-to-all-start = ((bf16[4,256,512]{2,1,0:T(8,128)(2,1)}), bf16[4,256,512]{2,1,0:T(8,128)(2,1)S(1)}, u32[]{:S(2)}, u32[]{:S(2)}) async-start(bf16[4,256,512]{2,1,0:T(8,128)(2,1)} %broadcast_in_dim.7), calls=%async_computation | async-start | bytes 2097152 | tf_op jit(solution)/shard_map/all_to_all | solution.py:84
  17.5 234.1 %all-gather.5.cloned.1.call-start = ((), (), s32[]{:S(2)}) async-start(), calls=%async_computation.5 | async-start | bytes 7864320 | tf_op jit(solution)/shard_map/all_gather | solution.py:662
  22.3 34.7 %collective-permute-start.2 = (bf16[256,1536]{1,0:T(8,128)(2,1)}, bf16[256,1536]{1,0:T(8,128)(2,1)}, u32[]{:S(2)}, u32[]{:S(2)}) collective-permute-start(bf16[256,1536]{1,0:T(8,128)(2,1)} %get-tuple-element.127), channel_id=1, source_target_pairs={{0,4},{4,0},{1,5},{5,1},{2,6},{6,2},{3,7},{7,3},{8,12},{12,8},{9,1... | collective-permute-start | bytes 2359304 | tf_op jit(solution)/shard_map/ppermute | solution.py:39
  22.9 37.5 %collective-permute-start = (bf16[256,2048]{1,0:T(8,128)(2,1)S(1)}, bf16[256,2048]{1,0:T(8,128)(2,1)S(1)}, u32[]{:S(2)}, u32[]{:S(2)}) collective-permute-start(bf16[256,2048]{1,0:T(8,128)(2,1)S(1)} %copy-done.21), channel_id=1, source_target_pairs={{0,2},{2,0},{1,3},{3,1},{4,6},{6,4},{5,7},{7,5},{8,10},{10,8},{9,1... | collective-permute-start | bytes 3145736 | tf_op jit(solution)/shard_map/ppermute | solution.py:39
  72.2 231.3 %all-gather.7.cloned.1.call-start = ((), (), s32[]{:S(2)}) async-start(), calls=%async_computation.6 | async-start | bytes 7864320 | tf_op jit(solution)/shard_map/all_gather | solution.py:662
  72.2 39.7 %collective-permute-start.3 = (bf16[4,272,768]{2,1,0:T(8,128)(2,1)}, bf16[4,272,768]{2,1,0:T(8,128)(2,1)}, u32[]{:S(2)}, u32[]{:S(2)}) collective-permute-start(bf16[4,272,768]{2,1,0:T(8,128)(2,1)} %bitcast.77), channel_id=1, source_target_pairs={{0,4},{4,0},{1,5},{5,1},{2,6},{6,2},{3,7},{7,3},{8,12},{12,8},{9,1... | collective-permute-start | bytes 5013512 | tf_op jit(solution)/shard_map/ppermute | solution.py:39
  74.1 25.3 %collective-permute-start.4 = (bf16[256,2048]{1,0:T(8,128)(2,1)S(1)}, bf16[256,2048]{1,0:T(8,128)(2,1)S(1)}, u32[]{:S(2)}, u32[]{:S(2)}) collective-permute-start(bf16[256,2048]{1,0:T(8,128)(2,1)S(1)} %copy-done.25), channel_id=1, source_target_pairs={{0,2},{2,0},{1,3},{3,1},{4,6},{6,4},{5,7},{7,5},{8,10},{10,8},{9,1... | collective-permute-start | bytes 3145736 | tf_op jit(solution)/shard_map/ppermute | solution.py:39
  79.0 55.7 %collective-permute-start.6 = (bf16[4,256,512]{2,1,0:T(8,128)(2,1)S(1)}, bf16[4,256,512]{2,1,0:T(8,128)(2,1)S(1)}, u32[]{:S(2)}, u32[]{:S(2)}) collective-permute-start(bf16[4,256,512]{2,1,0:T(8,128)(2,1)S(1)} %copy-done.38), channel_id=1, source_target_pairs={{0,4},{4,0},{1,5},{5,1},{2,6},{6,2},{3,7},{7,3},{8,12},{12,8},{9,1... | collective-permute-start | bytes 3145736 | tf_op jit(solution)/shard_map/ppermute | solution.py:39
  136.4 26.0 %collective-permute-start.9 = (bf16[512,1024]{1,0:T(8,128)(2,1)S(1)}, bf16[512,1024]{1,0:T(8,128)(2,1)S(1)}, u32[]{:S(2)}, u32[]{:S(2)}) collective-permute-start(bf16[512,1024]{1,0:T(8,128)(2,1)S(1)} %get-tuple-element.140), channel_id=1, source_target_pairs={{0,4},{4,0},{1,5},{5,1},{2,6},{6,2},{3,7},{7,3},{8,12},{12,8},{9,1... | collective-permute-start | bytes 3145736 | tf_op jit(solution)/shard_map/ppermute | solution.py:39
  137.9 46.5 %collective-permute-start.10 = (bf16[512,1024]{1,0:T(8,128)(2,1)S(1)}, bf16[512,1024]{1,0:T(8,128)(2,1)S(1)}, u32[]{:S(2)}, u32[]{:S(2)}) collective-permute-start(bf16[512,1024]{1,0:T(8,128)(2,1)S(1)} %get-tuple-element.141), channel_id=1, source_target_pairs={{0,4},{4,0},{1,5},{5,1},{2,6},{6,2},{3,7},{7,3},{8,12},{12,8},{9,1... | collective-permute-start | bytes 3145736 | tf_op jit(solution)/shard_map/ppermute | solution.py:39
  141.0 43.4 %collective-permute-start.8 = (bf16[256,2048]{1,0:T(8,128)(2,1)S(1)}, bf16[256,2048]{1,0:T(8,128)(2,1)S(1)}, u32[]{:S(2)}, u32[]{:S(2)}) collective-permute-start(bf16[256,2048]{1,0:T(8,128)(2,1)S(1)} %get-tuple-element.139), channel_id=1, source_target_pairs={{0,2},{2,0},{1,3},{3,1},{4,6},{6,4},{5,7},{7,5},{8,10},{10,8},{9,1... | collective-permute-start | bytes 3145736 | tf_op jit(solution)/shard_map/ppermute | solution.py:39
  188.7 227.3 %reduce-scatter.4.cloned.1.call-start = ((), (), s32[]{:S(2)}) async-start(), calls=%async_computation.7 | async-start | bytes 7864320 | tf_op jit(solution)/shard_map/reduce_scatter | solution.py:709
  192.3 25.6 %collective-permute-start.11 = (bf16[256,2048]{1,0:T(8,128)(2,1)S(1)}, bf16[256,2048]{1,0:T(8,128)(2,1)S(1)}, u32[]{:S(2)}, u32[]{:S(2)}) collective-permute-start(bf16[256,2048]{1,0:T(8,128)(2,1)S(1)} %get-tuple-element.242), channel_id=1, source_target_pairs={{0,2},{2,0},{1,3},{3,1},{4,6},{6,4},{5,7},{7,5},{8,10},{10,8},{9,1... | collective-permute-start | bytes 3145736 | tf_op jit(solution)/shard_map/ppermute | solution.py:39
  193.8 26.0 %collective-permute-start.12 = (bf16[256,2048]{1,0:T(8,128)(2,1)S(1)}, bf16[256,2048]{1,0:T(8,128)(2,1)S(1)}, u32[]{:S(2)}, u32[]{:S(2)}) collective-permute-start(bf16[256,2048]{1,0:T(8,128)(2,1)S(1)} %get-tuple-element.242), channel_id=1, source_target_pairs={{0,4},{4,0},{1,5},{5,1},{2,6},{6,2},{3,7},{7,3},{8,12},{12,8},{9,1... | collective-permute-start | bytes 3145736 | tf_op jit(solution)/shard_map/ppermute | solution.py:39
  195.3 46.2 %collective-permute-start.13 = (bf16[256,2048]{1,0:T(8,128)(2,1)S(1)}, bf16[256,2048]{1,0:T(8,128)(2,1)S(1)}, u32[]{:S(2)}, u32[]{:S(2)}) collective-permute-start(bf16[256,2048]{1,0:T(8,128)(2,1)S(1)} %get-tuple-element.242), channel_id=1, source_target_pairs={{0,6},{2,4},{4,2},{6,0},{1,7},{3,5},{5,3},{7,1},{8,14},{10,12},{12... | collective-permute-start | bytes 3145736 | tf_op jit(solution)/shard_map/ppermute | solution.py:39
  303.5 236.0 %reduce-scatter.8.cloned.1.call-start = ((), (), s32[]{:S(2)}) async-start(), calls=%async_computation.9 | async-start | bytes 7864320 | tf_op jit(solution)/shard_map/reduce_scatter | solution.py:709
  358.8 31.1 %collective-permute-start.17 = (bf16[256,2048]{1,0:T(8,128)(2,1)}, bf16[256,2048]{1,0:T(8,128)(2,1)S(1)}, u32[]{:S(2)}, u32[]{:S(2)}) collective-permute-start(bf16[256,2048]{1,0:T(8,128)(2,1)} %get-tuple-element.165), channel_id=1, source_target_pairs={{0,2},{2,0},{1,3},{3,1},{4,6},{6,4},{5,7},{7,5},{8,10},{10,8},{9,1... | collective-permute-start | bytes 3145736 | tf_op jit(solution)/shard_map/ppermute | solution.py:39
  360.3 29.6 %collective-permute-start.18 = (bf16[256,2048]{1,0:T(8,128)(2,1)}, bf16[256,2048]{1,0:T(8,128)(2,1)}, u32[]{:S(2)}, u32[]{:S(2)}) collective-permute-start(bf16[256,2048]{1,0:T(8,128)(2,1)} %get-tuple-element.166), channel_id=1, source_target_pairs={{0,4},{4,0},{1,5},{5,1},{2,6},{6,2},{3,7},{7,3},{8,12},{12,8},{9,1... | collective-permute-start | bytes 3145736 | tf_op jit(solution)/shard_map/ppermute | solution.py:39
  361.7 46.4 %collective-permute-start.19 = (bf16[256,2048]{1,0:T(8,128)(2,1)}, bf16[256,2048]{1,0:T(8,128)(2,1)}, u32[]{:S(2)}, u32[]{:S(2)}) collective-permute-start(bf16[256,2048]{1,0:T(8,128)(2,1)} %get-tuple-element.167), channel_id=1, source_target_pairs={{0,6},{2,4},{4,2},{6,0},{1,7},{3,5},{5,3},{7,1},{8,14},{10,12},{12... | collective-permute-start | bytes 3145736 | tf_op jit(solution)/shard_map/ppermute | solution.py:39
  381.0 203.7 %reduce-scatter.6.cloned.1.call-start = ((), (), s32[]{:S(2)}) async-start(), calls=%async_computation.8 | async-start | bytes 3276800 | tf_op jit(solution)/shard_map/reduce_scatter | solution.py:709
  419.0 25.3 %collective-permute-start.20 = (bf16[256,2048]{1,0:T(8,128)(2,1)S(1)}, bf16[256,2048]{1,0:T(8,128)(2,1)S(1)}, u32[]{:S(2)}, u32[]{:S(2)}) collective-permute-start(bf16[256,2048]{1,0:T(8,128)(2,1)S(1)} %get-tuple-element.174), channel_id=1, source_target_pairs={{0,2},{2,0},{1,3},{3,1},{4,6},{6,4},{5,7},{7,5},{8,10},{10,8},{9,1... | collective-permute-start | bytes 3145736 | tf_op jit(solution)/shard_map/ppermute | solution.py:39
  445.8 50.8 %collective-permute-start.25 = (bf16[256,2048]{1,0:T(8,128)(2,1)}, bf16[256,2048]{1,0:T(8,128)(2,1)}, u32[]{:S(2)}, u32[]{:S(2)}) collective-permute-start(bf16[256,2048]{1,0:T(8,128)(2,1)} %get-tuple-element.184), channel_id=1, source_target_pairs={{0,2},{2,0},{1,3},{3,1},{4,6},{6,4},{5,7},{7,5},{8,10},{10,8},{9,1... | collective-permute-start | bytes 3145736 | tf_op jit(solution)/shard_map/ppermute | solution.py:39
  457.3 42.4 %collective-permute-start.24 = (bf16[4,256,512]{1,2,0:T(8,128)(2,1)}, bf16[4,256,512]{1,2,0:T(8,128)(2,1)}, u32[]{:S(2)}, u32[]{:S(2)}) collective-permute-start(bf16[4,256,512]{1,2,0:T(8,128)(2,1)} %bitcast.82), channel_id=1, source_target_pairs={{0,4},{4,0},{1,5},{5,1},{2,6},{6,2},{3,7},{7,3},{8,12},{12,8},{9,1... | collective-permute-start | bytes 3145736 | tf_op jit(solution)/shard_map/ppermute | solution.py:39
  (76 other events, 877.7 us)
Sparse Core Ops, SparseCore 0:
  10.2 60.3 all-gather.8
  72.7 114.5 all-gather.4
  189.4 114.0 all-gather.6
  305.7 108.9 reduce-scatter.3
  416.8 111.2 reduce-scatter.7
  530.9 52.6 reduce-scatter.5
